TPU v7x, 32 devices: a whole 2x2x4 slice. The times are simulated.
32 devices in a mesh: parts: 2 (over y), dp: 4 (over x, core), tensor: 4 (over z).
Axes of the slice: x: 2, y: 2, z: 4, core: 2. Of those that a mesh axis runs over, the one named last changes fastest.
Arguments:
- gate_preact: bfloat16 [3072, 28672], P(('parts', 'dp'), 'tensor'), parts along dimension 0, may hold values from -6 to 6
- up_output: bfloat16 [3072, 28672], P(('parts', 'dp'), 'tensor'), parts along dimension 0, may hold values from -6 to 6
- normed_input: bfloat16 [3072, 8192], P(('parts', 'dp'), 'tensor'), parts along dimension 0, may hold values from -6 to 6
- output_grad: bfloat16 [3072, 8192], P(('parts', 'dp'), 'tensor'), parts along dimension 0, may hold values from -6 to 6
- down_weight: bfloat16 [28672, 8192], P('tensor', 'dp'), may hold values from -0.0625 to 0.0625
- normed_basis: bfloat16 [8192, 64], P('tensor'), may hold values from -0.0625 to 0.0625
- output_basis: bfloat16 [8192, 64], P('tensor'), may hold values from -0.0625 to 0.0625
- hidden_basis: bfloat16 [28672, 64], P('tensor'), may hold values from -0.03125 to 0.03125
- up_basis: bfloat16 [28672, 64], P('tensor'), may hold values from -0.03125 to 0.03125
- val_bank: bfloat16 [16, 8192], P('tensor', 'dp'), may hold values from -6 to 6
- lengths: int32 [8, 6], P(('parts', 'dp')), parts along dimension 0, may hold values from 1 to 192, 384 in all within a row
Outputs:
- scores: float32 [48, 16], P(('parts', 'dp'), 'tensor'), parts along dimension 0
There are 2 independent parts, one for each index of `parts`. A program takes and returns all parts, laid end to end along the dimension named above; an argument that names none is the same for every part. Nothing has to cross between parts.
Inputs may be any that keep to these rules, and one draw needn't show every extreme that they name: Each row holds the lengths of the 6 examples packed in order into the 384 tokens of one data group; a row sums to 384 and its longest example has exactly 192 tokens.
All inputs are finite; a program needn't handle non-finite values.
Results may differ from a plain program's by a relative error of at most 0.0041.
Values may be sent and summed in bfloat16 or wider, within the bound.
No kernel may reach another device: no remote copies, remote signals or barrier semaphores. Data moves between devices by JAX's collectives and lax.ppermute only.
A program may use at most 320 MiB of HBM per device.

v0:
```python
import jax
import jax.numpy as jnp
from jax import lax
from jax.sharding import PartitionSpec as P

R = 64


def segment_matrix(token_count, lengths_row):
    seg_ends = jnp.cumsum(lengths_row)
    seg_starts = seg_ends - lengths_row
    positions = jnp.arange(token_count, dtype=jnp.int32)
    inside = (positions[:, None] >= seg_starts[None, :]) & (positions[:, None] < seg_ends[None, :])
    return inside.astype(jnp.float32)


def outer_sum(member_rows, left_side, right_side):
    row_total = member_rows.shape[0]
    example_count = member_rows.shape[1]
    weighted = (member_rows[:, :, None] * left_side[:, None, :]).reshape(
        row_total, example_count * R
    )
    product = lax.dot_general(
        weighted,
        right_side,
        (((0,), (0,)), ((), ())),
        precision=lax.Precision.HIGHEST,
        preferred_element_type=jnp.float32,
    )
    return product.reshape(example_count, R * R)


def body(
    gate_preact,
    up_output,
    normed_input,
    output_grad,
    down_weight,
    normed_basis,
    output_basis,
    hidden_basis,
    up_basis,
    val_bank,
    lengths,
):
    group_tokens = gate_preact.shape[0]
    silu_gate = jax.nn.silu(gate_preact.astype(jnp.float32))
    hidden = (silu_gate * up_output.astype(jnp.float32)).astype(jnp.bfloat16)
    w_whole = lax.all_gather(down_weight, "dp", axis=1, tiled=True)
    hidden_grad = lax.dot_general(
        lax.all_gather(output_grad, "tensor", axis=1, tiled=True),
        w_whole,
        (((1,), (1,)), ((), ())),
        preferred_element_type=jnp.float32,
    )
    up_grad = (hidden_grad * silu_gate).astype(jnp.bfloat16)
    member = segment_matrix(group_tokens, lengths[0])
    factor = float(2 * R * R) ** (-0.5)
    totals = lax.psum(
        jnp.concatenate(
            [
                jnp.dot(output_grad, output_basis, preferred_element_type=jnp.float32),
                jnp.dot(normed_input, normed_basis, preferred_element_type=jnp.float32),
                jnp.dot(hidden, hidden_basis, preferred_element_type=jnp.float32),
                jnp.dot(up_grad, up_basis, preferred_element_type=jnp.float32),
            ],
            axis=1,
        ),
        "tensor",
    )
    stacked = jnp.concatenate(
        [
            outer_sum(member, totals[:, :R], totals[:, 2 * R : 3 * R]),
            outer_sum(member, totals[:, 3 * R :], totals[:, R : 2 * R]),
        ],
        axis=1,
    )
    unit_rows = (
        stacked * lax.rsqrt(jnp.mean(stacked * stacked, axis=1, keepdims=True) + 1e-06)
    ).astype(jnp.bfloat16)
    raw_scores = lax.dot_general(
        unit_rows,
        lax.all_gather(val_bank, "dp", axis=1, tiled=True),
        (((1,), (1,)), ((), ())),
        preferred_element_type=jnp.float32,
    )
    return raw_scores * factor


def solution(mesh):
    placed = (
        P(("parts", "dp"), "tensor"),
        P(("parts", "dp"), "tensor"),
        P(("parts", "dp"), "tensor"),
        P(("parts", "dp"), "tensor"),
        P("tensor", "dp"),
        P("tensor", None),
        P("tensor", None),
        P("tensor", None),
        P("tensor", None),
        P("tensor", "dp"),
        P(("parts", "dp"), None),
    )
    return jax.shard_map(
        body, mesh=mesh, in_specs=placed, out_specs=P(("parts", "dp"), "tensor"), check_vma=False
    )
```

profile of v0, /device:TPU:0, one launch (start us, length us, event | category | flops | bytes accessed | tf_op | source)
XLA Modules:
  0.0 919.4 jit_solution(8532745308529860866)
XLA Ops:
  6.5 0.0 copy-start
  6.5 0.0 all-gather.3.cloned.1.call-start
  6.5 0.7 all-gather.3.cloned.1.call-update
  7.3 0.0 copy-start.4
  7.3 0.0 copy-start.3
  7.3 0.0 copy-start.1
  7.3 0.0 all-gather.5.cloned.1.call-start
  7.3 0.7 all-gather.5.cloned.1.call-update
  8.0 0.0 all-reduce.2.cloned.1.call-start
  8.1 0.0 copy-done.4
  8.1 0.2 reduce-window.4
  8.3 6.1 all_gather.11
  14.4 1.5 fusion.16
  16.0 1.5 fusion.17
  17.5 7.8 fusion.3
  25.3 0.0 copy-start.2
  25.3 101.7 %all-gather.3.cloned.1.call-done = bf16[384,8192]{1,0:T(8,128)(2,1)} async-done(((bf16[384,2048]{1,0:T(8,128)(2,1)}), bf16[384,8192]{1,0:T(8,128)(2,1)}) %all-gather.3.cloned.1.call-update) | async-done | bytes 6291472 | tf_op jit(solution)/shard_map/all_gather | solution.py:51
  127.0 679.3 %all-gather.5.cloned.1.call-done = bf16[7168,8192]{1,0:T(8,128)(2,1)} async-done(((bf16[7168,2048]{1,0:T(8,128)(2,1)}), bf16[7168,8192]{1,0:T(8,128)(2,1)}) %all-gather.5.cloned.1.call-update) | async-done | bytes 117440528 | tf_op jit(solution)/shard_map/all_gather | solution.py:49
  806.3 58.8 %multiply_convert_fusion.clone.4 = bf16[384,7168]{1,0:T(8,128)(2,1)} fusion(bf16[384,8192]{1,0:T(8,128)(2,1)} %all-gather.3.cloned.1.call-done, bf16[7168,8192]{1,0:T(8,128)(2,1)} %all-gather.5.cloned.1.call-done, bf16[384,7168]{1,0:T(8,128)(2,1)} %param.11), kind=kOutput, calls=%fused_computation.5.clone.clone.clone.1 | convolution fusion | flops 45116424192 | bytes 134742016 | tf_op jit(solution)/shard_map/dot_general | solution.py:50
  865.1 4.4 fusion.9
  869.5 0.8 pad_maximum_fusion
  870.3 0.0 all-reduce.2.cloned.1.call-update
  870.3 0.1 fusion.11
  870.4 37.1 %all-reduce.2.cloned.1.call-done = f32[384,256]{0,1:T(8,128)} async-done(((f32[384,256]{0,1:T(8,128)}), f32[384,256]{0,1:T(8,128)}) %all-reduce.2.cloned.1.call-update) | async-done | bytes 393232 | tf_op jit(solution)/shard_map/psum | solution.py:59
  907.5 1.0 fusion.15
  908.5 0.1 broadcast_multiply_fusion
  908.6 1.5 fusion.5
  910.1 0.1 reshape.78
  910.2 1.5 fusion.7
  911.7 0.1 reshape.77
  911.9 0.2 multiply_reduce_fusion
  912.1 0.8 convolution_multiply_fusion
  (8 shorter events, 0.0 us)
Async XLA Ops:
  6.5 9.4 %copy-start = (bf16[384,2048]{1,0:T(8,128)(2,1)S(1)}, bf16[384,2048]{1,0:T(8,128)(2,1)}, u32[]{:S(2)}) copy-start(bf16[384,2048]{1,0:T(8,128)(2,1)} %param.13) | copy-start | bytes 4718596
  6.5 120.5 %all-gather.3.cloned.1.call-start = ((), (), s32[]{:S(2)}) async-start(), calls=%async_computation | async-start | bytes 7864320 | tf_op jit(solution)/shard_map/all_gather | solution.py:51
  7.3 0.8 copy-start.4
  7.3 1.0 copy-start.3
  7.3 7.1 copy-start.1
  7.3 799.0 %all-gather.5.cloned.1.call-start = ((), (), s32[]{:S(2)}) async-start(), calls=%async_computation.1 | async-start | bytes 146800640 | tf_op jit(solution)/shard_map/all_gather | solution.py:49
  8.0 899.5 %all-reduce.2.cloned.1.call-start = ((), (), s32[]{:S(2)}) async-start(), calls=%async_computation.2 | async-start | bytes 786432 | tf_op jit(solution)/shard_map/psum | solution.py:59
  25.3 839.8 %copy-start.2 = (bf16[7168,64]{0,1:T(8,128)(2,1)S(1)}, bf16[7168,64]{0,1:T(8,128)(2,1)}, u32[]{:S(2)}) copy-start(bf16[7168,64]{0,1:T(8,128)(2,1)} %param.19) | copy-start | bytes 2752516
Sparse Core Ops, SparseCore 0:
  8.9 118.0 all-gather.2
  128.6 677.6 all-gather.4
  870.4 37.0 all-reduce.1
where the time goes:
time: 920 us; the launch traced here: 919 us
  waiting for transfers between devices  820 us (89%)
  matrix products  77.9 us (8%)
  between operations  13.2 us (1%)
    all_gather x1, waiting for transfers between devices, body(): w_whole = lax.all_gather(down_weight, 'dp', axis=1, tiled=True)  679 us
    all_gather x1, waiting for transfers between devices, body(): lax.all_gather(output_grad, 'tensor', axis=1, tiled=True)  102 us
    dot_general x1, matrix products, body(): lax.dot_general(lax.all_gather(output_grad, 'tensor', axis=1, tiled=True)...  58.8 us
    psum x1, waiting for transfers between devices, body(): lax.psum(jnp.concatenate([jnp.dot(output_grad, output_basis, preferred_el...  37.1 us
  transfers between devices with their start and end apart: 3, of which 3 were waited for; matrix products, arithmetic and copies ran while one was open for 1% of the time, Pallas kernels for 0%

commit v1 on v0

v1 whole, which is shorter than its diff:
```python
import functools

import jax
import jax.numpy as jnp
from jax import lax
from jax.experimental import pallas as pl
from jax.experimental.pallas import tpu as pltpu
from jax.sharding import PartitionSpec as P

R = 64
EPS = 1e-06
AXES = ("dp", "tensor")
NT = (((1,), (1,)), ((), ()))
VMEM_BYTES = 48 * 1024 * 1024


def after(value, *others):
    return lax.optimization_barrier((value,) + others)[0]


def silu(gate):
    return gate / (1.0 + jnp.exp(-gate))


def pack(rows):
    half = rows.shape[0] // 2
    return jnp.concatenate([rows[:half], rows[half:]], axis=1)


def unpack(rows):
    return jnp.concatenate([rows[:, :R], rows[:, R:]], axis=0)


def project_kernel(pieces, parts, per_piece, *refs):
    gates = refs[:pieces]
    grads = refs[pieces : pieces + parts]
    weights = refs[pieces + parts : pieces + 2 * parts]
    basis, before, out, act, total = refs[pieces + 2 * parts :]
    step = pl.program_id(0)

    @pl.when(step == 0)
    def _():
        total[...] = jnp.zeros_like(total)

    for index, gate in enumerate(gates):

        @pl.when(step // per_piece == index)
        def _(gate=gate):
            act[...] = silu(gate[...].astype(jnp.float32))

    hidden_grad = sum(
        lax.dot_general(grad[...], weight[...], NT, preferred_element_type=jnp.float32)
        for grad, weight in zip(grads, weights, strict=True)
    )
    up_grad = (hidden_grad * act[...]).astype(jnp.bfloat16)
    total[...] += jnp.dot(up_grad, basis[...], preferred_element_type=jnp.float32)

    @pl.when(step == pl.num_programs(0) - 1)
    def _():
        out[...] = before[...] + pack(total[...])


def project(gates, grads, weights, basis, before, start, width, tile):
    pieces, parts = len(gates), len(grads)
    rows, depth = grads[0].shape
    per_piece = width // pieces // tile
    steps = width // tile
    first = start // tile

    def gate_spec(index, column):
        return pl.BlockSpec(
            (rows, tile),
            lambda i: (0, column // tile + jnp.clip(i - index * per_piece, 0, per_piece - 1)),
        )

    whole = lambda i: (0, 0)
    return pl.pallas_call(
        functools.partial(project_kernel, pieces, parts, per_piece),
        grid=(steps,),
        in_specs=[gate_spec(index, column) for index, (_, column) in enumerate(gates)]
        + [pl.BlockSpec((rows, depth), whole)] * parts
        + [pl.BlockSpec((tile, depth), lambda i, block=block: (first + i, block)) for _, block in weights]
        + [pl.BlockSpec((tile, R), lambda i: (first + i, 0)), pl.BlockSpec((rows // 2, 2 * R), whole)],
        out_specs=pl.BlockSpec((rows // 2, 2 * R), whole),
        out_shape=jax.ShapeDtypeStruct((rows // 2, 2 * R), jnp.float32),
        scratch_shapes=[pltpu.VMEM((rows, tile), jnp.float32), pltpu.VMEM((rows, R), jnp.float32)],
        compiler_params=pltpu.CompilerParams(vmem_limit_bytes=VMEM_BYTES),
        cost_estimate=pl.CostEstimate(
            flops=2 * rows * width * (parts * depth + R),
            bytes_accessed=2 * width * (parts * depth + rows) + 2 * rows * parts * depth,
            transcendentals=rows * width,
        ),
    )(*[g for g, _ in gates], *grads, *[w for w, _ in weights], basis, before)


def hidden_kernel(gate, up, basis, out):
    @pl.when(pl.program_id(0) == 0)
    def _():
        out[...] = jnp.zeros_like(out)

    hidden = (silu(gate[...].astype(jnp.float32)) * up[...].astype(jnp.float32)).astype(jnp.bfloat16)
    out[...] += jnp.dot(hidden, basis[...], preferred_element_type=jnp.float32)


def hidden_project(gate, up, basis, tile):
    rows, width = gate.shape
    return pl.pallas_call(
        hidden_kernel,
        grid=(width // tile,),
        in_specs=[
            pl.BlockSpec((rows, tile), lambda i: (0, i)),
            pl.BlockSpec((rows, tile), lambda i: (0, i)),
            pl.BlockSpec((tile, R), lambda i: (i, 0)),
        ],
        out_specs=pl.BlockSpec((rows, R), lambda i: (0, 0)),
        out_shape=jax.ShapeDtypeStruct((rows, R), jnp.float32),
        compiler_params=pltpu.CompilerParams(vmem_limit_bytes=VMEM_BYTES),
        cost_estimate=pl.CostEstimate(
            flops=2 * rows * width * R, bytes_accessed=4 * rows * width, transcendentals=rows * width
        ),
    )(gate, up, basis)


def score_kernel(examples, partials, masked, down_sum, down_val, up_val, out):
    up_out = unpack(sum(partials[n].astype(jnp.float32) for n in range(partials.shape[0])))
    up_sum = lax.dot_general(
        up_out.T,
        masked[...],
        (((1,), (0,)), ((), ())),
        precision=lax.Precision.HIGHEST,
        preferred_element_type=jnp.float32,
    )
    down = down_sum[...]
    squares = jnp.sum(up_sum * up_sum + down * down, axis=0, keepdims=True)
    lane = lax.broadcasted_iota(jnp.int32, (1, examples * R), 1) // R
    inverse = jnp.zeros_like(squares)
    for e in range(examples):
        mean = jnp.sum(jnp.where(lane == e, squares, 0.0), axis=1, keepdims=True) / (2 * R * R)
        inverse = jnp.where(lane == e, lax.rsqrt(mean + EPS), inverse)
    down = (down * inverse).astype(jnp.bfloat16).astype(jnp.float32)
    up_sum = (up_sum * inverse).astype(jnp.bfloat16).astype(jnp.float32)
    values = down_val.shape[0]
    columns = lax.broadcasted_iota(jnp.int32, (examples, values), 1)
    rows = lax.broadcasted_iota(jnp.int32, (examples, values), 0)
    scores = jnp.zeros((examples, values), jnp.float32)
    for v in range(values):
        both = down * down_val[v].astype(jnp.float32) + up_sum * up_val[v].astype(jnp.float32)
        by_lane = jnp.sum(both, axis=0, keepdims=True)
        for e in range(examples):
            one = jnp.sum(jnp.where(lane == e, by_lane, 0.0), axis=1, keepdims=True)
            scores = jnp.where((columns == v) & (rows == e), one, scores)
    out[...] = scores * float(2 * R * R) ** (-0.5)


def split(total, most, unit):
    for count in range(most, 0, -1):
        if total % (count * unit) == 0:
            return count
    return 1


def gather_line(grad, side, lane, place):
    depth = grad.shape[1] // 2
    ga, gb = grad[:, :depth], grad[:, depth:]
    spot = jnp.where(side == 0, place, 3 - place)

    def at(a, c, s):
        return (2 * a + c) * 4 + (s if a == 0 else 3 - s)

    def move(value, hops, other=False):
        pairs = [
            (at(1 - a if other else a, c, s), at(a, c, t)) for a in (0, 1) for c in (0, 1) for s, t in hops
        ]
        return lax.ppermute(value, AXES, pairs)

    def pick(*cases):
        value = cases[3]
        for s in (2, 1, 0):
            if cases[s] is not value:
                value = jnp.where(spot == s, cases[s], value)
        return value

    xa = move(ga, [(3, 0), (2, 1)], other=True)
    xb = move(gb, [(3, 2), (2, 3)], other=True)
    u1 = move(ga, [(0, 1), (1, 2)])
    v1 = move(ga, [(1, 0)])
    u2 = move(jnp.where(spot == 2, u1, xa), [(0, 1), (1, 2), (2, 3)])
    v2 = move(xa, [(1, 0)])
    u3 = move(jnp.where(spot == 1, u1, u2), [(1, 2), (2, 3)])
    v3 = move(after(gb, v2), [(1, 0)])
    u4 = move(jnp.where(spot == 1, u2, u3), [(1, 2), (2, 3)])
    v4 = move(after(xb, v2), [(2, 1), (3, 2)])
    u5 = move(jnp.where(spot == 2, u4, gb), [(0, 1), (1, 2), (2, 3)])
    v5 = move(after(v4, v3), [(1, 0), (2, 1)])
    u6 = move(u5, [(1, 2), (2, 3)])
    v6 = move(v5, [(1, 0)])
    u7 = move(after(xb, u6), [(2, 3)])
    u8 = move(after(u6, u7), [(2, 3)])

    swap = (side + lane) % 2 == 1

    def both(first, second):
        return (
            pick(*[jnp.where(swap, s, f) if s is not f else f for f, s in zip(first, second, strict=True)]),
            pick(*[jnp.where(swap, f, s) if s is not f else f for f, s in zip(first, second, strict=True)]),
        )

    return {
        "near_a": both((ga, u1, u3, u4), (v1, ga, u1, u2)),
        "far_a": both((xa, u2, u4, u5), (v2, xa, u2, u3)),
        "far_b": both((v5, v4, xb, u7), (v6, v5, v4, xb)),
        "near_b": both((gb, u5, u6, u8), (v3, gb, u5, u6)),
    }, xa


def gather_any(grad, side, lane):
    count = lax.axis_size("dp")
    whole = lax.all_gather(grad, "tensor", axis=1, tiled=True)
    block = whole.shape[1] // count
    far = lax.ppermute(
        lax.dynamic_slice_in_dim(whole, (1 - side) * 2 * block, 2 * block, axis=1),
        "dp",
        [(i, i ^ 2) for i in range(count)],
    )
    near = lax.dynamic_slice_in_dim(whole, side * 2 * block, 2 * block, axis=1)
    blocks = {}
    for name, value in (("near", near), ("far", far)):
        own = jnp.where(lane == 0, value[:, :block], value[:, block:])
        sibling = jnp.where(lane == 0, value[:, block:], value[:, :block])
        for half, cut in (("a", slice(0, block // 2)), ("b", slice(block // 2, block))):
            blocks[f"{name}_{half}"] = (own[:, cut], sibling[:, cut])
    return blocks, far


def sum_tensor(value):
    count = lax.axis_size("tensor")
    if count > 8:
        return lax.psum(value.astype(jnp.float32), "tensor")[None]
    return jnp.stack(
        [value]
        + [lax.ppermute(value, "tensor", [(i, (i + k) % count) for i in range(count)]) for k in range(1, count)]
    )


def body(
    gate_preact,
    up_output,
    normed_input,
    output_grad,
    down_weight,
    normed_basis,
    output_basis,
    hidden_basis,
    up_basis,
    val_bank,
    lengths,
):
    rows, width = gate_preact.shape
    examples = lengths.shape[1]
    index, place = lax.axis_index("dp"), lax.axis_index("tensor")
    side, lane = index // 2, index % 2
    count = lax.axis_size("dp")
    across = [(i, i ^ 2) for i in range(count)]
    beside = [(i, i ^ 1) for i in range(count)]

    if count == 4 and lax.axis_size("tensor") == 4:
        grads, first = gather_line(output_grad, side, lane, place)
    else:
        grads, first = gather_any(output_grad, side, lane)
    sibling = lax.ppermute(down_weight, "dp", beside)

    pieces = split(width, 7, 256)
    piece = width // pieces
    tile = piece // split(piece, max(1, piece // 512), 128)
    far_gates = []
    for n in range(pieces):
        own = after(gate_preact[:, n * piece : (n + 1) * piece], far_gates[n - 2] if n >= 2 else first)
        far_gates.append(lax.ppermute(own, "dp", across))

    totals = lax.psum(
        jnp.concatenate(
            [
                jnp.dot(output_grad, output_basis, preferred_element_type=jnp.float32),
                jnp.dot(normed_input, normed_basis, preferred_element_type=jnp.float32),
                hidden_project(gate_preact, up_output, hidden_basis, tile),
            ],
            axis=1,
        ),
        "tensor",
    )
    down_out, up_in, down_in = totals[:, :R], totals[:, R : 2 * R], totals[:, 2 * R :]
    ends = jnp.cumsum(lengths[0])
    owner = jnp.arange(examples * R, dtype=jnp.int32) // R
    token = jnp.arange(rows, dtype=jnp.int32)
    member = (token[:, None] >= (ends - lengths[0])[owner][None, :]) & (token[:, None] < ends[owner][None, :])
    masked_up = jnp.where(member, jnp.tile(up_in, (1, examples)), 0.0)
    down_sum = lax.dot_general(
        down_out,
        jnp.where(member, jnp.tile(down_in, (1, examples)), 0.0),
        (((0,), (0,)), ((), ())),
        precision=lax.Precision.HIGHEST,
        preferred_element_type=jnp.float32,
    )
    values = lax.all_gather(val_bank, "dp", axis=1, tiled=True)
    values = jnp.tile(values.reshape(values.shape[0], 2, R, R), (1, 1, 1, examples))

    def weights(*halves):
        return [(w, half) for half in halves for w in (down_weight, sibling)]

    zero = jnp.zeros((rows // 2, 2 * R), jnp.float32)
    near, far = zero, zero
    early = pieces - 1
    half = (pieces + 1) // 2

    def far_part(far, parts, begin, end):
        return project(
            [(far_gates[n], 0) for n in range(begin, end)],
            sum((grads["far_" + p] for p in parts), ()),
            weights(*[0 if p == "a" else 1 for p in parts]),
            up_basis,
            far,
            begin * piece,
            (end - begin) * piece,
            tile,
        )

    near = project([(gate_preact, 0)], grads["near_a"], weights(0), up_basis, near, 0, width, tile)
    if early > 0:
        far = far_part(far, "a", 0, half)
        if early > half:
            far = far_part(far, "a", half, early)
        far = far_part(far, "b", 0, early)
    far = far_part(far, "ab", early, pieces)
    back = lax.ppermute(far, "dp", across)
    near = project([(gate_preact, 0)], grads["near_b"], weights(1), up_basis, near, 0, width, tile)
    partials = sum_tensor((near + back).astype(jnp.bfloat16))
    return pl.pallas_call(
        functools.partial(score_kernel, examples),
        out_shape=jax.ShapeDtypeStruct((examples, val_bank.shape[0]), jnp.float32),
    )(partials, masked_up, down_sum, values[:, 0], values[:, 1])


def solution(mesh):
    placed = (
        P(("parts", "dp"), "tensor"),
        P(("parts", "dp"), "tensor"),
        P(("parts", "dp"), "tensor"),
        P(("parts", "dp"), "tensor"),
        P("tensor", "dp"),
        P("tensor", None),
        P("tensor", None),
        P("tensor", None),
        P("tensor", None),
        P("tensor", "dp"),
        P(("parts", "dp"), None),
    )
    return jax.shard_map(
        body, mesh=mesh, in_specs=placed, out_specs=P(("parts", "dp"), "tensor"), check_vma=False
    )
```

time: 920 us -> 365 us (0.40)
  waiting for transfers between devices: 820 us -> 110 us
  Pallas kernels: 0 us -> 110 us
  matrix products: 77.9 us -> 3.02 us
  starting transfers between devices: 0.08 us -> 72.4 us
  local copies, waits for them, and re-layouts: 1.21 us -> 24.3 us
  other arithmetic: 1.32 us -> 19.5 us
    all_gather x2 -> x0, waiting for transfers between devices: 781 us -> none  [the longest x1 679 us: body(): w_whole = lax.all_gather(down_weight, 'dp', axis=1, tiled=True)]
    pallas_call x0 -> x8, Pallas kernels: none -> 110 us  [the longest x6 96.1 us: project(): pl.pallas_call(functools.partial(project_kernel, pieces, parts, per_piece...]
    ppermute x0 -> x28, waiting for transfers between devices: none -> 97.9 us  [the longest x16 61 us: move(): return lax.ppermute(value, AXES, pairs)]
    dot_general x6 -> x1, matrix products: 74.8 us -> 1.23 us  [body(): lax.dot_general(down_out, jnp.where(member, jnp.tile(down_in, (1, example...]
    ppermute x0 -> x28, starting transfers between devices: none -> 72.4 us  [the longest x16 39.8 us: move(): return lax.ppermute(value, AXES, pairs)]
    psum x1, waiting for transfers between devices: 37.1 us -> 11.9 us  [body(): lax.psum(jnp.concatenate([jnp.dot(output_grad, output_basis, preferred_el...]
  transfers between devices with their start and end apart: 3 -> 29, of which waited for: 3 -> 10; matrix products, arithmetic and copies ran while one was open for 1% -> 11% of each run, Pallas kernels for 0% -> 28%
where the time goes in v1:
time: 365 us; the launch traced here: 363 us
  waiting for transfers between devices  110 us (30%)
  Pallas kernels  110 us (30%)
  starting transfers between devices  72.4 us (20%)
  local copies, waits for them, and re-layouts  24.3 us (7%)
  other arithmetic  19.5 us (5%)
  between operations  14 us (4%)
  blocking collectives  9.57 us (3%)
    pallas_call x6, Pallas kernels, project(): pl.pallas_call(functools.partial(project_kernel, pieces, parts, per_piece...  96.1 us
    ppermute x16, waiting for transfers between devices, move(): return lax.ppermute(value, AXES, pairs)  61 us
    ppermute x16, starting transfers between devices, move(): return lax.ppermute(value, AXES, pairs)  39.8 us
    ppermute x7, waiting for transfers between devices, body(): far_gates.append(lax.ppermute(own, 'dp', across))  32.9 us
    ppermute x7, starting transfers between devices, body(): far_gates.append(lax.ppermute(own, 'dp', across))  28 us
    psum x1, waiting for transfers between devices, body(): lax.psum(jnp.concatenate([jnp.dot(output_grad, output_basis, preferred_el...  11.9 us
    pallas_call x1, Pallas kernels, hidden_project(): pl.pallas_call(hidden_kernel, grid=(width // tile,), in_specs=[pl.BlockSp...  11.4 us
    all_gather x1, blocking collectives, body(): values = lax.all_gather(val_bank, 'dp', axis=1, tiled=True)  9.57 us
  transfers between devices with their start and end apart: 29, of which 10 were waited for; matrix products, arithmetic and copies ran while one was open for 11% of the time, Pallas kernels for 28%

profile of v1, /device:TPU:0, one launch (start us, length us, event | category | flops | bytes accessed | tf_op | source)
XLA Modules:
  0.0 362.9 jit_solution(8945576311366521998)
XLA Ops:
  7.0 2.1 slice.43
  9.1 4.6 %collective-permute-start.3 = (bf16[384,1024]{1,0:T(8,128)(2,1)}, bf16[384,1024]{1,0:T(8,128)(2,1)S(1)}, u32[]{:S(2)}, u32[]{:S(2)}) collective-permute-start(bf16[384,1024]{1,0:T(8,128)(2,1)} %slice.43), channel_id=1, source_target_pairs={{0,1},{1,2},{4,5},{5,6},{11,10},{10,9},{15,14},{14,13},{16,17},{17... | collective-permute-start | bytes 2359304 | tf_op jit(solution)/shard_map/ppermute | solution.py:174
  15.1 16.3 %collective-permute-done.3 = bf16[384,1024]{1,0:T(8,128)(2,1)S(1)} collective-permute-done((bf16[384,1024]{1,0:T(8,128)(2,1)}, bf16[384,1024]{1,0:T(8,128)(2,1)S(1)}, u32[]{:S(2)}, u32[]{:S(2)}) %collective-permute-start.3) | collective-permute-done | bytes 786464 | tf_op jit(solution)/shard_map/ppermute | solution.py:174
  31.3 4.1 %collective-permute-done = bf16[384,1024]{1,0:T(8,128)(2,1)S(1)} collective-permute-done((bf16[384,1024]{1,0:T(8,128)(2,1)}, bf16[384,1024]{1,0:T(8,128)(2,1)S(1)}, u32[]{:S(2)}, u32[]{:S(2)}) %collective-permute-start) | collective-permute-done | bytes 786464 | tf_op jit(solution)/shard_map/ppermute | solution.py:174
  37.3 3.5 collective-permute-start.4
  40.8 16.5 %collective-permute-done.4 = bf16[384,1024]{1,0:T(8,128)(2,1)S(1)} collective-permute-done((bf16[384,1024]{1,0:T(8,128)(2,1)}, bf16[384,1024]{1,0:T(8,128)(2,1)S(1)}, u32[]{:S(2)}, u32[]{:S(2)}) %collective-permute-start.4) | collective-permute-done | bytes 786464 | tf_op jit(solution)/shard_map/ppermute | solution.py:174
  60.0 4.6 %fusion.12 = (bf16[384,1024]{1,0:T(8,128)(2,1)}, bf16[384,1024]{1,0:T(8,128)(2,1)}, bf16[384,1024]{1,0:T(8,128)(2,1)S(1)}, bf16[384,1024]{1,0:T(8,128)(2,1)S(1)}...) fusion(bf16[384,7168]{1,0:T(8,128)(2,1)} %gate.1), kind=kLoop, calls=%fused_computation.48 | loop fusion | bytes 11010048 | tf_op jit(solution)/shard_map/slice | solution.py:277
  64.6 20.6 %collective-permute-start.14 = (bf16[384,1024]{1,0:T(8,128)(2,1)S(1)}, bf16[384,1024]{1,0:T(8,128)(2,1)S(1)}, u32[]{:S(2)}, u32[]{:S(2)}) collective-permute-start(bf16[384,1024]{1,0:T(8,128)(2,1)S(1)} %get-tuple-element.20), channel_id=1, source_target_pairs={{0,8},{4,12},{8,0},{12,4},{1,9},{5,13},{9,1},{13,5},{2,10},{6,14},... | collective-permute-start | bytes 2359304 | tf_op jit(solution)/shard_map/ppermute | solution.py:278
  86.4 14.4 %collective-permute-start.7 = (bf16[384,1024]{1,0:T(8,128)(2,1)S(1)}, bf16[384,1024]{1,0:T(8,128)(2,1)S(1)}, u32[]{:S(2)}, u32[]{:S(2)}) collective-permute-start(bf16[384,1024]{1,0:T(8,128)(2,1)S(1)} %get-tuple-element.49), channel_id=1, source_target_pairs={{0,1},{1,2},{2,3},{4,5},{5,6},{6,7},{11,10},{10,9},{9,8},{15,14},{... | collective-permute-start | bytes 2359304 | tf_op jit(solution)/shard_map/ppermute | solution.py:174
  104.9 9.5 %collective-permute-done.7 = bf16[384,1024]{1,0:T(8,128)(2,1)S(1)} collective-permute-done((bf16[384,1024]{1,0:T(8,128)(2,1)S(1)}, bf16[384,1024]{1,0:T(8,128)(2,1)S(1)}, u32[]{:S(2)}, u32[]{:S(2)}) %collective-permute-start.7) | collective-permute-done | bytes 786464 | tf_op jit(solution)/shard_map/ppermute | solution.py:174
  116.0 2.9 collective-permute-done.21.refs_1_
  119.9 2.5 collective-permute-start.15
  125.3 30.0 %collective-permute-done.15.refs_2_ = bf16[384,1024]{1,0:T(8,128)(2,1)S(1)} collective-permute-done((bf16[384,1024]{1,0:T(8,128)(2,1)S(1)}, bf16[384,1024]{1,0:T(8,128)(2,1)S(1)}, u32[]{:S(2)}, u32[]{:S(2)}) %collective-permute-start.15) | collective-permute-done | bytes 786464 | tf_op jit(solution)/shard_map/ppermute | solution.py:278
  159.0 1.9 copy.29.basis
  160.9 11.4 %shard_map.115 = f32[384,64]{1,0:T(8,128)S(1)} custom-call(bf16[384,7168]{1,0:T(8,128)(2,1)} %gate.1, bf16[384,7168]{1,0:T(8,128)(2,1)} %up.1, bf16[7168,64]{1,0:T(8,128)(2,1)S(1)} %copy.29.basis), custom_call_target="tpu_custom_call" | custom-call | flops 352321536 | bytes 11010048 | tf_op jit(solution)/shard_map/pallas_call | solution.py:107
  176.5 2.5 collective-permute-start.16
  182.5 9.6 %all_gather.3 = bf16[4,8192]{1,0:T(4,128)(2,1)S(1)} all-gather(bf16[4,2048]{1,0:T(4,128)(2,1)S(1)} %copy-done.28), channel_id=1, replica_groups=mesh['parts'=2,'dp'=4,'tensor'=4] {'dp'}, dimensions={1}, use_global_device_ids=true | all-gather | bytes 81920 | tf_op jit(solution)/shard_map/all_gather | solution.py:304
  194.7 7.5 %fusion.9 = (s32[384]{0:T(512)S(1)}, s32[384]{0:T(512)S(1)}) fusion(s32[]{:T(128)} %bitcast.13, s32[]{:T(128)} %bitcast.14, s32[]{:T(128)} %bitcast.15, s32[]{:T(128)} %bitcast.16, s32[]{:T(128)} %bitcast.18, s32[]{:T(128)} %bitcast.17, s32[]{:T(128)} %bitcast.12, s32[]{:T(128)} %bitcast.11, s32[]{:T(128)} %bitcast.10, s32[]{:T(128)} %bitcast.9, s32[]{:T(128)} %bitcast.8, ...), kind=kLoop, calls=%fused_computation.44 | loop fusion | flops 9984 | bytes 3120 | tf_op jit(solution)/shard_map/gather | solution.py:295
  202.9 11.9 %all-reduce.2.cloned.1.call-done = f32[384,192]{1,0:T(8,128)} async-done(((f32[384,192]{1,0:T(8,128)}), f32[384,192]{1,0:T(8,128)}) %all-reduce.2.cloned.1.call-update) | async-done | bytes 294928 | tf_op jit(solution)/shard_map/psum | solution.py:280
  217.4 2.1 copy.35
  223.9 3.8 %select_select_fusion.2 = (bf16[384,1024]{1,0:T(8,128)(2,1)S(1)}, bf16[384,1024]{1,0:T(8,128)(2,1)S(1)}, bf16[384,1024]{1,0:T(8,128)(2,1)S(1)}, bf16[384,1024]{1...) fusion(bf16[384,1024]{1,0:T(8,128)(2,1)S(1)} %copy-done.23, ...), kind=kLoop, calls=%fused_computation.2 | loop fusion | flops 15728640 | bytes 14942212 | tf_op jit(solution)/shard_map/jit(_where)/select_n | solution.py:180
  227.8 14.7 %collective-permute-done.20 = bf16[384,1024]{1,0:T(8,128)(2,1)S(1)} collective-permute-done((bf16[384,1024]{1,0:T(8,128)(2,1)}, bf16[384,1024]{1,0:T(8,128)(2,1)S(1)}, u32[]{:S(2)}, u32[]{:S(2)}) %collective-permute-start.20) | collective-permute-done | bytes 786464 | tf_op jit(solution)/shard_map/ppermute | solution.py:174
  242.4 3.1 select_select_fusion
  245.6 14.4 %shard_map.111.refs_7_ = f32[192,128]{1,0:T(8,128)S(1)} custom-call(bf16[384,1024]{1,0:T(8,128)(2,1)S(1)} %copy-done.6, bf16[384,1024]{1,0:T(8,128)(2,1)S(1)} %copy-done.8, bf16[384,1024]{1,0:T(8,128)(2,1)S(1)} %copy-done.10, bf16[384,1024]{1,0:T(8,128)(2,1)} %collective-permute-done.22.refs_3_, ...), custom_call_target="tpu_custom_call" | custom-call | flops 6643777536 | bytes 21495808 | tf_op jit(solution)/shard_map/pallas_call | solution.py:77
  260.1 7.5 %shard_map.112.refs_11_ = f32[192,128]{1,0:T(8,128)S(1)} custom-call(bf16[384,1024]{1,0:T(8,128)(2,1)S(1)} %collective-permute-done.16.refs_0_.refs_4_, bf16[384,1024]{1,0:T(8,128)(2,1)S(1)} %collective-permute-done.23.refs_1_.refs_5_, bf16[384,1024]{1,0:T(8,128)(2,1)S(1)} %get-tuple-element.39.refs_4_.refs_2_.refs_1_, ...), custom_call_target="tpu_custom_call" | custom-call | flops 3321888768 | bytes 11534336 | tf_op jit(solution)/shard_map/pallas_call | solution.py:77
  267.7 20.8 %shard_map.113.refs_10_ = f32[192,128]{1,0:T(8,128)S(1)} custom-call(bf16[384,1024]{1,0:T(8,128)(2,1)S(1)} %copy-done.6, bf16[384,1024]{1,0:T(8,128)(2,1)S(1)} %copy-done.8, bf16[384,1024]{1,0:T(8,128)(2,1)S(1)} %copy-done.10, bf16[384,1024]{1,0:T(8,128)(2,1)} %collective-permute-done.22.refs_3_, ...), custom_call_target="tpu_custom_call" | custom-call | flops 9965666304 | bytes 31457280 | tf_op jit(solution)/shard_map/pallas_call | solution.py:77
  288.5 6.9 %shard_map.114 = f32[192,128]{1,0:T(8,128)S(1)} custom-call(bf16[384,1024]{1,0:T(8,128)(2,1)} %collective-permute-done.17.refs_0_, bf16[384,1024]{1,0:T(8,128)(2,1)S(1)} %get-tuple-element.39.refs_4_.refs_2_.refs_1_, bf16[384,1024]{1,0:T(8,128)(2,1)S(1)} %get-tuple-element.38.refs_5_.refs_3_.refs_2_, ...), custom_call_target="tpu_custom_call" | custom-call | flops 3271557120 | bytes 12320768 | tf_op jit(solution)/shard_map/pallas_call | solution.py:77
  295.5 23.1 %shard_map.109.refs_6_ = f32[192,128]{1,0:T(8,128)S(1)} custom-call(bf16[384,7168]{1,0:T(8,128)(2,1)} %gate.1, bf16[384,1024]{1,0:T(8,128)(2,1)S(1)} %get-tuple-element.44.refs_1_, bf16[384,1024]{1,0:T(8,128)(2,1)S(1)} %get-tuple-element.45.refs_2_, bf16[7168,2048]{1,0:T(8,128)(2,1)} %refs_7_.1, ...), custom_call_target="tpu_custom_call" | custom-call | flops 11626610688 | bytes 36438016 | tf_op jit(solution)/shard_map/pallas_call | solution.py:77
  318.7 23.3 %shard_map.110 = f32[192,128]{1,0:T(8,128)S(1)} custom-call(bf16[384,7168]{1,0:T(8,128)(2,1)} %gate.1, bf16[384,1024]{1,0:T(8,128)(2,1)S(1)} %get-tuple-element.46.refs_1_, bf16[384,1024]{1,0:T(8,128)(2,1)S(1)} %get-tuple-element.47.refs_2_, bf16[7168,2048]{1,0:T(8,128)(2,1)} %refs_7_.1, ...), custom_call_target="tpu_custom_call" | custom-call | flops 11626610688 | bytes 36438016 | tf_op jit(solution)/shard_map/pallas_call | solution.py:77
  342.0 3.4 collective-permute-start.27
  347.3 3.1 collective-permute-done.26
  352.0 2.7 shard_map.116
  (131 shorter events, 43.5 us)
Async XLA Ops:
  6.5 165.8 %copy-start = (bf16[384,2048]{1,0:T(8,128)(2,1)S(1)}, bf16[384,2048]{1,0:T(8,128)(2,1)}, u32[]{:S(2)}) copy-start(bf16[384,2048]{1,0:T(8,128)(2,1)} %param.13) | copy-start | bytes 4718596
  6.5 208.3 %all-reduce.2.cloned.1.call-start = ((), (), s32[]{:S(2)}) async-start(), calls=%async_computation | async-start | bytes 786432 | tf_op jit(solution)/shard_map/psum | solution.py:280
  6.5 239.0 %collective-permute-start.12 = (bf16[7168,2048]{1,0:T(8,128)(2,1)}, bf16[7168,2048]{1,0:T(8,128)(2,1)}, u32[]{:S(2)}, u32[]{:S(2)}) collective-permute-start(bf16[7168,2048]{1,0:T(8,128)(2,1)} %refs_7_.1), channel_id=1, source_target_pairs={{0,4},{4,0},{8,12},{12,8},{1,5},{5,1},{9,13},{13,9},{2,6},{6,2},{1... | collective-permute-start | bytes 88080392 | tf_op jit(solution)/shard_map/ppermute | solution.py:270
  9.1 22.2 %collective-permute-start.3 = (bf16[384,1024]{1,0:T(8,128)(2,1)}, bf16[384,1024]{1,0:T(8,128)(2,1)S(1)}, u32[]{:S(2)}, u32[]{:S(2)}) collective-permute-start(bf16[384,1024]{1,0:T(8,128)(2,1)} %slice.43), channel_id=1, source_target_pairs={{0,1},{1,2},{4,5},{5,6},{11,10},{10,9},{15,14},{14,13},{16,17},{17... | collective-permute-start | bytes 2359304 | tf_op jit(solution)/shard_map/ppermute | solution.py:174
  13.7 21.6 %collective-permute-start = (bf16[384,1024]{1,0:T(8,128)(2,1)}, bf16[384,1024]{1,0:T(8,128)(2,1)S(1)}, u32[]{:S(2)}, u32[]{:S(2)}) collective-permute-start(bf16[384,1024]{1,0:T(8,128)(2,1)} %slice.43), channel_id=1, source_target_pairs={{8,0},{9,1},{12,4},{13,5},{3,11},{2,10},{7,15},{6,14},{24,16},{25,... | collective-permute-start | bytes 2359304 | tf_op jit(solution)/shard_map/ppermute | solution.py:174
  37.3 19.9 %collective-permute-start.4 = (bf16[384,1024]{1,0:T(8,128)(2,1)}, bf16[384,1024]{1,0:T(8,128)(2,1)S(1)}, u32[]{:S(2)}, u32[]{:S(2)}) collective-permute-start(bf16[384,1024]{1,0:T(8,128)(2,1)} %broadcast_select_fusion.1), channel_id=1, source_target_pairs={{0,1},{1,2},{2,3},{4,5},{5,6},{6,7},{11,10},{10,9},{9,8},{15,14},{... | collective-permute-start | bytes 2359304 | tf_op jit(solution)/shard_map/ppermute | solution.py:174
  57.3 0.7 collective-permute-start.5
  59.1 26.1 %collective-permute-start.6 = (bf16[384,1024]{1,0:T(8,128)(2,1)S(1)}, bf16[384,1024]{1,0:T(8,128)(2,1)S(1)}, u32[]{:S(2)}, u32[]{:S(2)}) collective-permute-start(bf16[384,1024]{1,0:T(8,128)(2,1)S(1)} %broadcast_select_fusion.2), channel_id=1, source_target_pairs={{1,2},{2,3},{5,6},{6,7},{10,9},{9,8},{14,13},{13,12},{17,18},{18,1... | collective-permute-start | bytes 2359304 | tf_op jit(solution)/shard_map/ppermute | solution.py:174
  64.6 93.2 %copy-start.26 = (bf16[2048,64]{0,1:T(8,128)(2,1)S(1)}, bf16[2048,64]{0,1:T(8,128)(2,1)}, u32[]{:S(2)}) copy-start(bf16[2048,64]{0,1:T(8,128)(2,1)} %param.17) | copy-start | bytes 786436
  64.6 37.8 %collective-permute-start.14 = (bf16[384,1024]{1,0:T(8,128)(2,1)S(1)}, bf16[384,1024]{1,0:T(8,128)(2,1)S(1)}, u32[]{:S(2)}, u32[]{:S(2)}) collective-permute-start(bf16[384,1024]{1,0:T(8,128)(2,1)S(1)} %get-tuple-element.20), channel_id=1, source_target_pairs={{0,8},{4,12},{8,0},{12,4},{1,9},{5,13},{9,1},{13,5},{2,10},{6,14},... | collective-permute-start | bytes 2359304 | tf_op jit(solution)/shard_map/ppermute | solution.py:278
  86.4 28.0 %collective-permute-start.7 = (bf16[384,1024]{1,0:T(8,128)(2,1)S(1)}, bf16[384,1024]{1,0:T(8,128)(2,1)S(1)}, u32[]{:S(2)}, u32[]{:S(2)}) collective-permute-start(bf16[384,1024]{1,0:T(8,128)(2,1)S(1)} %get-tuple-element.49), channel_id=1, source_target_pairs={{0,1},{1,2},{2,3},{4,5},{5,6},{6,7},{11,10},{10,9},{9,8},{15,14},{... | collective-permute-start | bytes 2359304 | tf_op jit(solution)/shard_map/ppermute | solution.py:174
  100.8 18.2 %collective-permute-start.21 = (bf16[384,1024]{1,0:T(8,128)(2,1)S(1)}, bf16[384,1024]{1,0:T(8,128)(2,1)S(1)}, u32[]{:S(2)}, u32[]{:S(2)}) collective-permute-start(bf16[384,1024]{1,0:T(8,128)(2,1)S(1)} %get-tuple-element.26), channel_id=1, source_target_pairs={{0,8},{4,12},{8,0},{12,4},{1,9},{5,13},{9,1},{13,5},{2,10},{6,14},... | collective-permute-start | bytes 2359304 | tf_op jit(solution)/shard_map/ppermute | solution.py:278
  101.1 21.3 %collective-permute-start.1 = (bf16[384,1024]{1,0:T(8,128)(2,1)S(1)}, bf16[384,1024]{1,0:T(8,128)(2,1)S(1)}, u32[]{:S(2)}, u32[]{:S(2)}) collective-permute-start(bf16[384,1024]{1,0:T(8,128)(2,1)S(1)} %copy-done.16), channel_id=1, source_target_pairs={{1,0},{5,4},{10,11},{14,15},{17,16},{21,20},{26,27},{30,31}} | collective-permute-start | bytes 2359304 | tf_op jit(solution)/shard_map/ppermute | solution.py:174
  103.3 19.2 %collective-permute-start.9 = (bf16[384,1024]{1,0:T(8,128)(2,1)}, bf16[384,1024]{1,0:T(8,128)(2,1)}, u32[]{:S(2)}, u32[]{:S(2)}) collective-permute-start(bf16[384,1024]{1,0:T(8,128)(2,1)} %get-tuple-element.17), channel_id=1, source_target_pairs={{8,2},{9,3},{12,6},{13,7},{3,9},{2,8},{7,13},{6,12},{24,18},{25,19... | collective-permute-start | bytes 2359304 | tf_op jit(solution)/shard_map/ppermute | solution.py:174
  114.4 43.3 %copy-start.22 = (bf16[384,1024]{1,0:T(8,128)(2,1)}, bf16[384,1024]{1,0:T(8,128)(2,1)S(1)}, u32[]{:S(2)}) copy-start(bf16[384,1024]{1,0:T(8,128)(2,1)S(1)} %collective-permute-done.7) | copy-start | bytes 2359300
  114.4 9.3 %collective-permute-start.8 = (bf16[384,1024]{1,0:T(8,128)(2,1)S(1)}, bf16[384,1024]{1,0:T(8,128)(2,1)}, u32[]{:S(2)}, u32[]{:S(2)}) collective-permute-start(bf16[384,1024]{1,0:T(8,128)(2,1)S(1)} %collective-permute-done.7), channel_id=1, source_target_pairs={{1,2},{2,3},{5,6},{6,7},{10,9},{9,8},{14,13},{13,12},{17,18},{18,1... | collective-permute-start | bytes 2359304 | tf_op jit(solution)/shard_map/ppermute | solution.py:174
  119.9 35.4 %collective-permute-start.15 = (bf16[384,1024]{1,0:T(8,128)(2,1)S(1)}, bf16[384,1024]{1,0:T(8,128)(2,1)S(1)}, u32[]{:S(2)}, u32[]{:S(2)}) collective-permute-start(bf16[384,1024]{1,0:T(8,128)(2,1)S(1)} %get-tuple-element.21), channel_id=1, source_target_pairs={{0,8},{4,12},{8,0},{12,4},{1,9},{5,13},{9,1},{13,5},{2,10},{6,14},... | collective-permute-start | bytes 2359304 | tf_op jit(solution)/shard_map/ppermute | solution.py:278
  122.4 57.8 %collective-permute-start.22 = (bf16[384,1024]{1,0:T(8,128)(2,1)}, bf16[384,1024]{1,0:T(8,128)(2,1)}, u32[]{:S(2)}, u32[]{:S(2)}) collective-permute-start(bf16[384,1024]{1,0:T(8,128)(2,1)} %get-tuple-element.27), channel_id=1, source_target_pairs={{0,8},{4,12},{8,0},{12,4},{1,9},{5,13},{9,1},{13,5},{2,10},{6,14},... | collective-permute-start | bytes 2359304 | tf_op jit(solution)/shard_map/ppermute | solution.py:278
  122.5 52.7 %collective-permute-start.2 = (bf16[384,1024]{1,0:T(8,128)(2,1)}, bf16[384,1024]{1,0:T(8,128)(2,1)}, u32[]{:S(2)}, u32[]{:S(2)}) collective-permute-start(bf16[384,1024]{1,0:T(8,128)(2,1)} %get-tuple-element.17), channel_id=1, source_target_pairs={{1,0},{5,4},{10,11},{14,15},{17,16},{21,20},{26,27},{30,31}} | collective-permute-start | bytes 2359304 | tf_op jit(solution)/shard_map/ppermute | solution.py:174
  123.8 52.7 %collective-permute-start.18 = (bf16[384,1024]{1,0:T(8,128)(2,1)}, bf16[384,1024]{1,0:T(8,128)(2,1)}, u32[]{:S(2)}, u32[]{:S(2)}) collective-permute-start(bf16[384,1024]{1,0:T(8,128)(2,1)} %collective-permute-done.9), channel_id=1, source_target_pairs={{2,1},{3,2},{6,5},{7,6},{9,10},{8,9},{13,14},{12,13},{18,17},{19,1... | collective-permute-start | bytes 2359304 | tf_op jit(solution)/shard_map/ppermute | solution.py:174
  156.2 22.7 %collective-permute-start.10 = (bf16[384,1024]{1,0:T(8,128)(2,1)}, bf16[384,1024]{1,0:T(8,128)(2,1)}, u32[]{:S(2)}, u32[]{:S(2)}) collective-permute-start(bf16[384,1024]{1,0:T(8,128)(2,1)} %collective-permute-done.9), channel_id=1, source_target_pairs={{2,3},{6,7},{9,8},{13,12},{18,19},{22,23},{25,24},{29,28}} | collective-permute-start | bytes 2359304 | tf_op jit(solution)/shard_map/ppermute | solution.py:174
  175.2 46.7 %collective-permute-start.13 = (bf16[384,1024]{1,0:T(8,128)(2,1)}, bf16[384,1024]{1,0:T(8,128)(2,1)}, u32[]{:S(2)}, u32[]{:S(2)}) collective-permute-start(bf16[384,1024]{1,0:T(8,128)(2,1)} %slice.43), channel_id=1, source_target_pairs={{1,0},{5,4},{10,11},{14,15},{17,16},{21,20},{26,27},{30,31}} | collective-permute-start | bytes 2359304 | tf_op jit(solution)/shard_map/ppermute | solution.py:174
  176.5 43.9 %collective-permute-start.16 = (bf16[384,1024]{1,0:T(8,128)(2,1)}, bf16[384,1024]{1,0:T(8,128)(2,1)S(1)}, u32[]{:S(2)}, u32[]{:S(2)}) collective-permute-start(bf16[384,1024]{1,0:T(8,128)(2,1)} %get-tuple-element.22), channel_id=1, source_target_pairs={{0,8},{4,12},{8,0},{12,4},{1,9},{5,13},{9,1},{13,5},{2,10},{6,14},... | collective-permute-start | bytes 2359304 | tf_op jit(solution)/shard_map/ppermute | solution.py:278
  178.9 43.5 %collective-permute-start.19 = (bf16[384,1024]{1,0:T(8,128)(2,1)}, bf16[384,1024]{1,0:T(8,128)(2,1)}, u32[]{:S(2)}, u32[]{:S(2)}) collective-permute-start(bf16[384,1024]{1,0:T(8,128)(2,1)} %collective-permute-done.18), channel_id=1, source_target_pairs={{1,0},{2,1},{5,4},{6,5},{10,11},{9,10},{14,15},{13,14},{17,16},{18... | collective-permute-start | bytes 2359304 | tf_op jit(solution)/shard_map/ppermute | solution.py:174
  180.2 43.7 %collective-permute-start.11 = (bf16[384,1024]{1,0:T(8,128)(2,1)}, bf16[384,1024]{1,0:T(8,128)(2,1)}, u32[]{:S(2)}, u32[]{:S(2)}) collective-permute-start(bf16[384,1024]{1,0:T(8,128)(2,1)} %collective-permute-done.8), channel_id=1, source_target_pairs={{2,3},{6,7},{9,8},{13,12},{18,19},{22,23},{25,24},{29,28}} | collective-permute-start | bytes 2359304 | tf_op jit(solution)/shard_map/ppermute | solution.py:174
  220.4 39.7 %collective-permute-start.23 = (bf16[384,1024]{1,0:T(8,128)(2,1)}, bf16[384,1024]{1,0:T(8,128)(2,1)S(1)}, u32[]{:S(2)}, u32[]{:S(2)}) collective-permute-start(bf16[384,1024]{1,0:T(8,128)(2,1)} %get-tuple-element.28), channel_id=1, source_target_pairs={{0,8},{4,12},{8,0},{12,4},{1,9},{5,13},{9,1},{13,5},{2,10},{6,14},... | collective-permute-start | bytes 2359304 | tf_op jit(solution)/shard_map/ppermute | solution.py:278
  221.8 66.7 %collective-permute-start.17 = (bf16[384,1024]{1,0:T(8,128)(2,1)}, bf16[384,1024]{1,0:T(8,128)(2,1)}, u32[]{:S(2)}, u32[]{:S(2)}) collective-permute-start(bf16[384,1024]{1,0:T(8,128)(2,1)} %get-tuple-element.23), channel_id=1, source_target_pairs={{0,8},{4,12},{8,0},{12,4},{1,9},{5,13},{9,1},{13,5},{2,10},{6,14},... | collective-permute-start | bytes 2359304 | tf_op jit(solution)/shard_map/ppermute | solution.py:278
  222.4 20.0 %collective-permute-start.20 = (bf16[384,1024]{1,0:T(8,128)(2,1)}, bf16[384,1024]{1,0:T(8,128)(2,1)S(1)}, u32[]{:S(2)}, u32[]{:S(2)}) collective-permute-start(bf16[384,1024]{1,0:T(8,128)(2,1)} %collective-permute-done.19), channel_id=1, source_target_pairs={{1,0},{5,4},{10,11},{14,15},{17,16},{21,20},{26,27},{30,31}} | collective-permute-start | bytes 2359304 | tf_op jit(solution)/shard_map/ppermute | solution.py:174
  295.4 46.6 %collective-permute-start.24 = (f32[192,128]{1,0:T(8,128)S(1)}, f32[192,128]{1,0:T(8,128)S(1)}, u32[]{:S(2)}, u32[]{:S(2)}) collective-permute-start(f32[192,128]{1,0:T(8,128)S(1)} %shard_map.114), channel_id=1, source_target_pairs={{0,8},{4,12},{8,0},{12,4},{1,9},{5,13},{9,1},{13,5},{2,10},{6,14},... | collective-permute-start | bytes 294920 | tf_op jit(solution)/shard_map/ppermute | solution.py:334
  342.0 5.3 %collective-permute-start.27 = (bf16[192,128]{1,0:T(8,128)(2,1)S(1)}, bf16[192,128]{1,0:T(8,128)(2,1)S(1)}, u32[]{:S(2)}, u32[]{:S(2)}) collective-permute-start(bf16[192,128]{1,0:T(8,128)(2,1)S(1)} %add_convert_fusion), channel_id=1, source_target_pairs={{0,3},{1,0},{2,1},{3,2},{4,7},{5,4},{6,5},{7,6},{8,11},{9,8},{10,9... | collective-permute-start | bytes 147464 | tf_op jit(solution)/shard_map/ppermute | solution.py:241
  345.4 5.0 %collective-permute-start.26 = (bf16[192,128]{1,0:T(8,128)(2,1)S(1)}, bf16[192,128]{1,0:T(8,128)(2,1)S(1)}, u32[]{:S(2)}, u32[]{:S(2)}) collective-permute-start(bf16[192,128]{1,0:T(8,128)(2,1)S(1)} %add_convert_fusion), channel_id=1, source_target_pairs={{0,2},{1,3},{2,0},{3,1},{4,6},{5,7},{6,4},{7,5},{8,10},{9,11},{10,... | collective-permute-start | bytes 147464 | tf_op jit(solution)/shard_map/ppermute | solution.py:241
  345.4 5.9 %collective-permute-start.25 = (bf16[192,128]{1,0:T(8,128)(2,1)S(1)}, bf16[192,128]{1,0:T(8,128)(2,1)S(1)}, u32[]{:S(2)}, u32[]{:S(2)}) collective-permute-start(bf16[192,128]{1,0:T(8,128)(2,1)S(1)} %add_convert_fusion), channel_id=1, source_target_pairs={{0,1},{1,2},{2,3},{3,0},{4,5},{5,6},{6,7},{7,4},{8,9},{9,10},{10,1... | collective-permute-start | bytes 147464 | tf_op jit(solution)/shard_map/ppermute | solution.py:241
  (27 other events, 388.6 us)
Sparse Core Ops, SparseCore 0:
  174.4 40.3 all-reduce.1

commit v2 on v0

v2 whole, which is shorter than its diff:
```python
import functools

import jax
import jax.numpy as jnp
from jax import lax
from jax.experimental import pallas as pl
from jax.experimental.pallas import tpu as pltpu
from jax.sharding import PartitionSpec as P

R = 64
EPS = 1e-06
AXES = ("dp", "tensor")
NT = (((1,), (1,)), ((), ()))
VMEM_BYTES = 48 * 1024 * 1024


def after(value, *others):
    return lax.optimization_barrier((value,) + others)[0]


def silu(gate):
    return gate / (1.0 + jnp.exp(-gate))


def pack(rows):
    half = rows.shape[0] // 2
    return jnp.concatenate([rows[:half], rows[half:]], axis=1)


def unpack(rows):
    return jnp.concatenate([rows[:, :R], rows[:, R:]], axis=0)


def project_kernel(pieces, parts, per_piece, _, *refs):
    gates = refs[:pieces]
    grads = refs[pieces : pieces + parts]
    weights = refs[pieces + parts : pieces + 2 * parts]
    basis, before, out, act, total = refs[pieces + 2 * parts :]
    step = pl.program_id(0)

    @pl.when(step == 0)
    def _():
        total[...] = jnp.zeros_like(total)

    for index, gate in enumerate(gates):

        @pl.when(step // per_piece == index)
        def _(gate=gate):
            act[...] = silu(gate[...].astype(jnp.float32))

    hidden_grad = sum(
        lax.dot_general(grad[...], weight[...], NT, preferred_element_type=jnp.float32)
        for grad, weight in zip(grads, weights, strict=True)
    )
    up_grad = (hidden_grad * act[...]).astype(jnp.bfloat16)
    total[...] += jnp.dot(up_grad, basis[...], preferred_element_type=jnp.float32)

    @pl.when(step == pl.num_programs(0) - 1)
    def _():
        out[...] = before[...] + pack(total[...])


def project(gates, grads, weights, half, basis, before, start, width, tile):
    pieces = len(gates)
    pairs = [(g, block, w) for w, group in zip(weights, grads, strict=True) for g, block in group]
    parts = len(pairs)
    rows, depth = pairs[0][0].shape
    own = gates[0].shape[1] * pieces == width
    per_piece = width // pieces // tile
    first = start // tile
    whole = lambda i, _: (0, 0)

    def gate_spec(index):
        if own:
            return pl.BlockSpec((rows, tile), lambda i, _: (0, jnp.clip(i - index * per_piece, 0, per_piece - 1)))
        return pl.BlockSpec((rows, tile), lambda i, _: (0, first + i))

    def weight_spec(block):
        if block is None:
            return pl.BlockSpec((tile, depth), lambda i, half: (first + i, half[0]))
        if block == "other":
            return pl.BlockSpec((tile, depth), lambda i, half: (first + i, 1 - half[0]))
        return pl.BlockSpec((tile, depth), lambda i, _: (first + i, block))

    return pl.pallas_call(
        functools.partial(project_kernel, pieces, parts, per_piece),
        grid_spec=pltpu.PrefetchScalarGridSpec(
            num_scalar_prefetch=1,
            grid=(width // tile,),
            in_specs=[gate_spec(index) for index in range(pieces)]
            + [pl.BlockSpec((rows, depth), whole)] * parts
            + [weight_spec(block) for _, block, _ in pairs]
            + [pl.BlockSpec((tile, R), lambda i, _: (first + i, 0)), pl.BlockSpec((rows // 2, 2 * R), whole)],
            out_specs=pl.BlockSpec((rows // 2, 2 * R), whole),
            scratch_shapes=[pltpu.VMEM((rows, tile), jnp.float32), pltpu.VMEM((rows, R), jnp.float32)],
        ),
        out_shape=jax.ShapeDtypeStruct((rows // 2, 2 * R), jnp.float32),
        compiler_params=pltpu.CompilerParams(vmem_limit_bytes=VMEM_BYTES),
        cost_estimate=pl.CostEstimate(flops=0, bytes_accessed=0, transcendentals=0),
    )(half, *gates, *[g for g, _, _ in pairs], *[w for _, _, w in pairs], basis, before)


def local_kernel(gate, up, grad, normed, hidden_basis, output_basis, normed_basis, out):
    half = grad.shape[0] // 2

    @pl.when(pl.program_id(0) == 0)
    def _():
        out[:half] = pack(jnp.dot(grad[...], output_basis[...], preferred_element_type=jnp.float32))
        out[half : 2 * half] = pack(jnp.dot(normed[...], normed_basis[...], preferred_element_type=jnp.float32))
        out[2 * half :] = jnp.zeros((half, 2 * R), jnp.float32)

    hidden = (silu(gate[...].astype(jnp.float32)) * up[...].astype(jnp.float32)).astype(jnp.bfloat16)
    out[2 * half :] += pack(jnp.dot(hidden, hidden_basis[...], preferred_element_type=jnp.float32))


def local_products(gate, up, grad, normed, hidden_basis, output_basis, normed_basis, tile):
    rows, width = gate.shape
    whole = lambda i: (0, 0)
    return pl.pallas_call(
        local_kernel,
        grid=(width // tile,),
        in_specs=[
            pl.BlockSpec((rows, tile), lambda i: (0, i)),
            pl.BlockSpec((rows, tile), lambda i: (0, i)),
            pl.BlockSpec(grad.shape, whole),
            pl.BlockSpec(normed.shape, whole),
            pl.BlockSpec((tile, R), lambda i: (i, 0)),
            pl.BlockSpec(output_basis.shape, whole),
            pl.BlockSpec(normed_basis.shape, whole),
        ],
        out_specs=pl.BlockSpec((rows * 3 // 2, 2 * R), whole),
        out_shape=jax.ShapeDtypeStruct((rows * 3 // 2, 2 * R), jnp.float32),
        compiler_params=pltpu.CompilerParams(vmem_limit_bytes=VMEM_BYTES),
        cost_estimate=pl.CostEstimate(flops=0, bytes_accessed=0, transcendentals=0),
    )(gate, up, grad, normed, hidden_basis, output_basis, normed_basis)


def member_kernel(examples, lengths, *refs):
    parts, masked_up, down_sum = refs[:-2], refs[-2], refs[-1]
    totals = sum(part[n].astype(jnp.float32) for part in parts for n in range(part.shape[0]))
    half = totals.shape[0] // 3
    down_out, up_in, down_in = (unpack(totals[n * half : (n + 1) * half]) for n in range(3))
    token = lax.broadcasted_iota(jnp.int32, (2 * half, R), 0)
    begin = 0
    up, down = [], []
    for e in range(examples):
        end = begin + lengths[0, e]
        inside = (token >= begin) & (token < end)
        up.append(jnp.where(inside, up_in, 0.0))
        down.append(jnp.where(inside, down_in, 0.0))
        begin = end
    masked_up[...] = jnp.concatenate(up, axis=1)
    down_sum[...] = lax.dot_general(
        down_out.T,
        jnp.concatenate(down, axis=1),
        (((1,), (0,)), ((), ())),
        precision=lax.Precision.HIGHEST,
        preferred_element_type=jnp.float32,
    )


def member_products(lengths, parts, rows):
    examples = lengths.shape[1]
    return pl.pallas_call(
        functools.partial(member_kernel, examples),
        in_specs=[pl.BlockSpec(memory_space=pltpu.SMEM)] + [pl.BlockSpec(memory_space=pltpu.VMEM)] * len(parts),
        out_shape=(
            jax.ShapeDtypeStruct((rows, examples * R), jnp.float32),
            jax.ShapeDtypeStruct((R, examples * R), jnp.float32),
        ),
        cost_estimate=pl.CostEstimate(flops=0, bytes_accessed=0, transcendentals=0),
    )(lengths, *parts)


def score_kernel(examples, masked, down_sum, bank, *refs):
    partials, out = refs[:-1], refs[-1]
    up_out = unpack(sum(part[n].astype(jnp.float32) for part in partials for n in range(part.shape[0])))
    up_sum = lax.dot_general(
        up_out.T,
        masked[...],
        (((1,), (0,)), ((), ())),
        precision=lax.Precision.HIGHEST,
        preferred_element_type=jnp.float32,
    )
    down = down_sum[...]
    squares = jnp.sum(up_sum * up_sum + down * down, axis=0, keepdims=True)
    lane = lax.broadcasted_iota(jnp.int32, (1, examples * R), 1) // R
    inverse = jnp.zeros_like(squares)
    for e in range(examples):
        mean = jnp.sum(jnp.where(lane == e, squares, 0.0), axis=1, keepdims=True) / (2 * R * R)
        inverse = jnp.where(lane == e, lax.rsqrt(mean + EPS), inverse)
    down = (down * inverse).astype(jnp.bfloat16).astype(jnp.float32)
    up_sum = (up_sum * inverse).astype(jnp.bfloat16).astype(jnp.float32)
    values = bank.shape[0]
    columns = lax.broadcasted_iota(jnp.int32, (examples, values), 1)
    rows = lax.broadcasted_iota(jnp.int32, (examples, values), 0)
    scores = jnp.zeros((examples, values), jnp.float32)
    for v in range(values):
        row = jnp.concatenate([bank[v].astype(jnp.float32)] * examples, axis=1)
        both = down * row[:R] + up_sum * row[R:]
        by_lane = jnp.sum(both, axis=0, keepdims=True)
        for e in range(examples):
            one = jnp.sum(jnp.where(lane == e, by_lane, 0.0), axis=1, keepdims=True)
            scores = jnp.where((columns == v) & (rows == e), one, scores)
    out[...] = scores * float(2 * R * R) ** (-0.5)


def split(total, most, unit):
    for count in range(most, 0, -1):
        if total % (count * unit) == 0:
            return count
    return 1


class Line:
    def __init__(self, side, lane, place):
        self.spot = jnp.where(side == 0, place, 3 - place)
        self.even = (side + lane) % 2

    @staticmethod
    def at(a, c, s):
        return (2 * a + c) * 4 + (s if a == 0 else 3 - s)

    def move(self, value, hops, other=False):
        pairs = [
            (self.at(1 - a if other else a, c, s), self.at(a, c, t)) for a in (0, 1) for c in (0, 1) for s, t in hops
        ]
        return lax.ppermute(value, AXES, pairs)

    def pair(self, value):
        return self.move(value, [(0, 1), (1, 0), (2, 3), (3, 2)])

    def middle(self, value):
        return self.move(value, [(1, 2), (2, 1)])

    def outward(self, value):
        return self.move(value, [(1, 0), (2, 3)])

    def by_block(self, first, second, parity):
        keep = parity == self.even
        return jnp.where(keep, first, second), jnp.where(keep, second, first)


def gather_any(grad, side, lane):
    count = lax.axis_size("dp")
    whole = lax.all_gather(grad, "tensor", axis=1, tiled=True)
    block = whole.shape[1] // count
    far = lax.ppermute(
        lax.dynamic_slice_in_dim(whole, (1 - side) * 2 * block, 2 * block, axis=1),
        "dp",
        [(i, i ^ 2) for i in range(count)],
    )
    near = lax.dynamic_slice_in_dim(whole, side * 2 * block, 2 * block, axis=1)
    return [
        (jnp.where(lane == 0, v[:, :block], v[:, block:]), jnp.where(lane == 0, v[:, block:], v[:, :block]))
        for v in (near, far)
    ]


def all_tensor(value):
    count = lax.axis_size("tensor")
    if count > 8:
        return [lax.psum(value.astype(jnp.float32), "tensor")[None]]
    return [value[None]] + [
        lax.ppermute(value, "tensor", [(i, (i + k) % count) for i in range(count)])[None] for k in range(1, count)
    ]


def body(
    gate_preact,
    up_output,
    normed_input,
    output_grad,
    down_weight,
    normed_basis,
    output_basis,
    hidden_basis,
    up_basis,
    val_bank,
    lengths,
):
    rows, width = gate_preact.shape
    examples = lengths.shape[1]
    index, place = lax.axis_index("dp"), lax.axis_index("tensor")
    side, lane = index // 2, index % 2
    count = lax.axis_size("dp")
    across = [(i, i ^ 2) for i in range(count)]
    beside = [(i, i ^ 1) for i in range(count)]

    def local(tile):
        return local_products(
            gate_preact, up_output, output_grad, normed_input, hidden_basis, output_basis, normed_basis, tile
        )

    def turned_bank(value):
        return [value] + [
            lax.ppermute(value, "dp", [((i + k) % count, i) for i in range(count)]) for k in range(1, count)
        ]

    def straight_bank(turned):
        turned = jnp.stack(turned + turned)
        blocks = lax.dynamic_slice_in_dim(turned, (count - index) % count, count, axis=0)
        return jnp.concatenate([blocks[n] for n in range(count)], axis=1).reshape(val_bank.shape[0], 2 * R, R)

    zero = jnp.zeros((rows // 2, 2 * R), jnp.float32)
    sibling = lax.ppermute(down_weight, "dp", beside)
    both = (down_weight, sibling)

    if count == 4 and lax.axis_size("tensor") == 4 and width % (7 * 128) == 0:
        line = Line(side, lane, place)
        depth = output_grad.shape[1] // 2
        ga, gb = output_grad[:, :depth], output_grad[:, depth:]
        half = (line.spot // 2).astype(jnp.int32)[None]
        inner = (line.spot == 1) | (line.spot == 2)
        piece = width // 7
        tile = piece

        def cut(source, begin, end):
            return source[:, begin * piece : end * piece]

        def project_far(far, sources, grads, start):
            width = sum(source.shape[1] for source in sources)
            return project(sources, grads, both, half, up_basis, far, start * piece, width, tile)

        def project_near(near, grads):
            return project([gate_preact], grads, both, half, up_basis, near, 0, width, tile)

        xb = line.move(gb, [(3, 2), (2, 3)], other=True)
        ns = line.move(gb, [(0, 2), (1, 3)])
        xa = line.move(ga, [(3, 0), (2, 1)], other=True)
        s0 = lax.ppermute(cut(gate_preact, 0, 2), "dp", across)
        sums = local(piece)

        xa, xb, ns, sums, rest = lax.optimization_barrier((xa, xb, ns, sums, gate_preact))
        own_f = jnp.where(line.spot < 2, xa, xb)
        own_n = jnp.where(line.spot < 2, ga, ns)
        e_f, m_f = line.pair(own_f), line.middle(own_f)
        s2 = lax.ppermute(cut(rest, 2, 3), "dp", across)

        e_f, m_f, own_n, s0, sibling, rest = lax.optimization_barrier((e_f, m_f, own_n, s0, sibling, rest))
        both = (down_weight, sibling)
        mm_f, o_f = line.middle(e_f), line.outward(m_f)
        e_n, m_n = line.pair(own_n), line.middle(own_n)
        s3 = lax.ppermute(cut(rest, 3, 5), "dp", across)
        first_f = [[(g, None)] for g in line.by_block(own_f, e_f, line.spot % 2)]
        far = project_far(zero, [s0], first_f, 0)
        far = project_far(far, [s2], first_f, 2)

        mm_f, o_f, e_n, m_n, rest, far = lax.optimization_barrier((mm_f, o_f, e_n, m_n, rest, far))
        oo_f = line.outward(mm_f)
        mm_n, o_n = line.middle(e_n), line.outward(m_n)
        s5 = lax.ppermute(cut(rest, 5, 7), "dp", across)
        first_n = [[(g, None)] for g in line.by_block(own_n, e_n, line.spot % 2)]
        near = project_near(zero, first_n)
        far = project_far(far, [s3], first_f, 3)

        oo_f, mm_n, o_n, near, far, bank = lax.optimization_barrier((oo_f, mm_n, o_n, near, far, val_bank))
        oo_n = line.outward(mm_n)
        turned = turned_bank(bank)
        rest_f = line.by_block(jnp.where(inner, m_f, o_f), jnp.where(inner, mm_f, oo_f), line.spot // 2)
        rest_f = [[(g, "other")] for g in rest_f]
        all_f = [a + b for a, b in zip(first_f, rest_f, strict=True)]
        far = project_far(far, [s0], rest_f, 0)
        far = project_far(far, [s2], rest_f, 2)
        far = project_far(far, [s3], rest_f, 3)
        far = project_far(far, [s5], all_f, 5)
        back = lax.ppermute(far, "dp", across)

        oo_n, far, sums, turned = lax.optimization_barrier((oo_n, far, sums, turned))
        sums = all_tensor(sums.astype(jnp.bfloat16))
        bank = straight_bank(turned)
        rest_n = line.by_block(jnp.where(inner, m_n, o_n), jnp.where(inner, mm_n, oo_n), line.spot // 2)
        near = project_near(after(near, far), [[(g, "other")] for g in rest_n])
        partials = all_tensor((near + back).astype(jnp.bfloat16))
        masked_up, down_sum = member_products(lengths, list(lax.optimization_barrier((*sums, near))[:-1]), rows)
    else:
        half = jnp.zeros((1,), jnp.int32)
        near_grads, far_grads = gather_any(output_grad, side, lane)
        far_gate = lax.ppermute(gate_preact, "dp", across)
        tile = width // split(width, max(1, width // 512), 128)
        masked_up, down_sum = member_products(lengths, all_tensor(local(tile)), rows)
        bank = straight_bank(turned_bank(val_bank))
        far = project([far_gate], [[(g, 0)] for g in far_grads], both, half, up_basis, zero, 0, width, tile)
        back = lax.ppermute(far, "dp", across)
        near = project([gate_preact], [[(g, 0)] for g in near_grads], both, half, up_basis, zero, 0, width, tile)
        partials = all_tensor((near + back).astype(jnp.bfloat16))

    return pl.pallas_call(
        functools.partial(score_kernel, examples),
        out_shape=jax.ShapeDtypeStruct((examples, val_bank.shape[0]), jnp.float32),
    )(masked_up, down_sum, bank, *partials)


def solution(mesh):
    placed = (
        P(("parts", "dp"), "tensor"),
        P(("parts", "dp"), "tensor"),
        P(("parts", "dp"), "tensor"),
        P(("parts", "dp"), "tensor"),
        P("tensor", "dp"),
        P("tensor", None),
        P("tensor", None),
        P("tensor", None),
        P("tensor", None),
        P("tensor", "dp"),
        P(("parts", "dp"), None),
    )
    return jax.shard_map(
        body, mesh=mesh, in_specs=placed, out_specs=P(("parts", "dp"), "tensor"), check_vma=False
    )
```

time: 920 us -> 240 us (0.26)
  waiting for transfers between devices: 820 us -> 27.3 us
  Pallas kernels: 0 us -> 107 us
  matrix products: 77.9 us -> 0 us
  starting transfers between devices: 0.08 us -> 60.7 us
  local copies, waits for them, and re-layouts: 1.21 us -> 31.2 us
  between operations: 13.2 us -> 0.58 us
  other arithmetic: 1.32 us -> 12 us
    all_gather x2 -> x0, waiting for transfers between devices: 781 us -> none  [the longest x1 679 us: body(): w_whole = lax.all_gather(down_weight, 'dp', axis=1, tiled=True)]
    pallas_call x0 -> x12, Pallas kernels: none -> 107 us  [the longest x9 91.8 us: project(): pl.pallas_call(functools.partial(project_kernel, pieces, parts, per_piece...]
    dot_general x8 -> x0, matrix products: 77.9 us -> none  [the longest x1 58.8 us: body(): lax.dot_general(lax.all_gather(output_grad, 'tensor', axis=1, tiled=True)...]
    ppermute x0 -> x28, starting transfers between devices: none -> 60.7 us  [the longest x13 35.7 us: move(): return lax.ppermute(value, AXES, pairs)]
    psum x1 -> x0, waiting for transfers between devices: 37.1 us -> none  [body(): lax.psum(jnp.concatenate([jnp.dot(output_grad, output_basis, preferred_el...]
    ppermute x0 -> x28, waiting for transfers between devices: none -> 27.3 us  [the longest x13 19.5 us: move(): return lax.ppermute(value, AXES, pairs)]
    unnamed x11 -> x65, local copies, waits for them, and re-layouts: 0.03 us -> 12.8 us
    slice x1 -> x6, local copies, waits for them, and re-layouts: 0.95 us -> 12.7 us  [the longest x4 9.41 us: cut(): return source[:, begin * piece:end * piece]]
  transfers between devices with their start and end apart: 3 -> 28, of which waited for: 3 -> 4; matrix products, arithmetic and copies ran while one was open for 1% -> 15% of each run, Pallas kernels for 0% -> 44%
where the time goes in v2:
time: 240 us; the launch traced here: 239 us
  Pallas kernels  107 us (45%)
  starting transfers between devices  60.7 us (25%)
  local copies, waits for them, and re-layouts  31.2 us (13%)
  waiting for transfers between devices  27.3 us (11%)
  other arithmetic  12 us (5%)
    pallas_call x9, Pallas kernels, project(): pl.pallas_call(functools.partial(project_kernel, pieces, parts, per_piece...  91.8 us
    ppermute x13, starting transfers between devices, move(): return lax.ppermute(value, AXES, pairs)  35.7 us
    ppermute x13, waiting for transfers between devices, move(): return lax.ppermute(value, AXES, pairs)  19.5 us
    ppermute x6, starting transfers between devices, all_tensor(): lax.ppermute(value, 'tensor', [(i, (i + k) % count) for i in range(count)])  13.7 us
    unnamed x65, local copies, waits for them, and re-layouts  12.8 us
    pallas_call x1, Pallas kernels, local_products(): pl.pallas_call(local_kernel, grid=(width // tile,), in_specs=[pl.BlockSpe...  9.69 us
    slice x4, local copies, waits for them, and re-layouts, cut(): return source[:, begin * piece:end * piece]  9.41 us
    select_n x4, other arithmetic, by_block(): return (jnp.where(keep, first, second), jnp.where(keep, second, first))  6.86 us
  transfers between devices with their start and end apart: 28, of which 4 were waited for; matrix products, arithmetic and copies ran while one was open for 15% of the time, Pallas kernels for 44%

profile of v2, /device:TPU:0, one launch (start us, length us, event | category | flops | bytes accessed | tf_op | source)
XLA Modules:
  0.0 238.8 jit_solution(16189070521229182419)
XLA Ops:
  0.5 2.6 %fusion = (bf16[384,1024]{1,0:T(8,128)(2,1)}, bf16[384,1024]{1,0:T(8,128)(2,1)}) fusion(bf16[384,2048]{1,0:T(8,128)(2,1)} %grad.1), kind=kLoop, calls=%fused_computation.28 | loop fusion | bytes 3145728 | tf_op jit(solution)/shard_map/slice | solution.py:312
  4.6 8.1 %collective-permute-start.2 = (bf16[384,1024]{1,0:T(8,128)(2,1)}, bf16[384,1024]{1,0:T(8,128)(2,1)}, u32[]{:S(2)}, u32[]{:S(2)}) collective-permute-start(bf16[384,1024]{1,0:T(8,128)(2,1)} %get-tuple-element.83), channel_id=1, source_target_pairs={{0,2},{1,3},{4,6},{5,7},{11,9},{10,8},{15,13},{14,12},{16,18},{17,... | collective-permute-start | bytes 2359304 | tf_op jit(solution)/shard_map/ppermute | solution.py:228
  14.0 2.7 %slice.32 = bf16[384,2048]{1,0:T(8,128)(2,1)} slice(bf16[384,7168]{1,0:T(8,128)(2,1)} %refs_0_.3), slice={[0:384], [0:2048]} | slice | bytes 3145728 | tf_op jit(solution)/shard_map/slice | solution.py:319
  16.7 3.5 %collective-permute-start.5 = (bf16[384,2048]{1,0:T(8,128)(2,1)}, bf16[384,2048]{1,0:T(8,128)(2,1)S(1)}, u32[]{:S(2)}, u32[]{:S(2)}) collective-permute-start(bf16[384,2048]{1,0:T(8,128)(2,1)} %slice.32), channel_id=1, source_target_pairs={{0,8},{4,12},{8,0},{12,4},{1,9},{5,13},{9,1},{13,5},{2,10},{6,14},... | collective-permute-start | bytes 4718600 | tf_op jit(solution)/shard_map/ppermute | solution.py:331
  20.2 2.7 %copy.12.hidden_basis = bf16[7168,64]{1,0:T(8,128)(2,1)} copy(bf16[7168,64]{0,1:T(8,128)(2,1)} %param.18) | data formatting | bytes 1835008 | tf_op args[7]
  23.9 2.0 copy.14.normed_basis
  29.4 9.7 %shard_map.109 = f32[576,128]{1,0:T(8,128)S(1)} custom-call(bf16[384,7168]{1,0:T(8,128)(2,1)} %refs_0_.3, bf16[384,7168]{1,0:T(8,128)(2,1)} %up.1, bf16[384,2048]{1,0:T(8,128)(2,1)S(1)} %copy-done.2, bf16[384,2048]{1,0:T(8,128)(2,1)S(1)} %copy-done.13, bf16[7168,64]{1,0:T(8,128)(2,1)} %copy.12.hidden_basis, bf16[2048,64]{1,0:T(8,128)(2,1)S(1)} %copy-done.11, ...), custom_call_target="tpu_custom_call" | custom-call | tf_op jit(solution)/shard_map/pallas_call | solution.py:119
  40.4 8.4 %collective-permute-start.3 = (bf16[384,1024]{1,0:T(8,128)(2,1)S(1)}, bf16[384,1024]{1,0:T(8,128)(2,1)}, u32[]{:S(2)}, u32[]{:S(2)}) collective-permute-start(bf16[384,1024]{1,0:T(8,128)(2,1)S(1)} %broadcast_select_fusion.13), channel_id=1, source_target_pairs={{0,1},{1,0},{2,3},{3,2},{4,5},{5,4},{6,7},{7,6},{11,10},{10,11},{9... | collective-permute-start | bytes 2359304 | tf_op jit(solution)/shard_map/ppermute | solution.py:228
  51.6 2.2 collective-permute-start.11
  54.8 11.9 %collective-permute-done.3 = bf16[384,1024]{1,0:T(8,128)(2,1)} collective-permute-done((bf16[384,1024]{1,0:T(8,128)(2,1)S(1)}, bf16[384,1024]{1,0:T(8,128)(2,1)}, u32[]{:S(2)}, u32[]{:S(2)}) %collective-permute-start.3) | collective-permute-done | bytes 786464 | tf_op jit(solution)/shard_map/ppermute | solution.py:228
  66.7 4.4 %collective-permute-done.5.refs_0_ = bf16[384,2048]{1,0:T(8,128)(2,1)S(1)} collective-permute-done((bf16[384,2048]{1,0:T(8,128)(2,1)}, bf16[384,2048]{1,0:T(8,128)(2,1)S(1)}, u32[]{:S(2)}, u32[]{:S(2)}) %collective-permute-start.5) | collective-permute-done | bytes 1572896 | tf_op jit(solution)/shard_map/ppermute | solution.py:331
  75.5 4.8 %collective-permute-start.9 = (bf16[384,1024]{1,0:T(8,128)(2,1)}, bf16[384,1024]{1,0:T(8,128)(2,1)}, u32[]{:S(2)}, u32[]{:S(2)}) collective-permute-start(bf16[384,1024]{1,0:T(8,128)(2,1)} %broadcast_select_fusion.12), channel_id=1, source_target_pairs={{0,1},{1,0},{2,3},{3,2},{4,5},{5,4},{6,7},{7,6},{11,10},{10,11},{9... | collective-permute-start | bytes 2359304 | tf_op jit(solution)/shard_map/ppermute | solution.py:228
  80.3 2.7 %slice.34 = bf16[384,2048]{1,0:T(8,128)(2,1)} slice(bf16[384,7168]{1,0:T(8,128)(2,1)} %refs_0_.3), slice={[0:384], [3072:5120]} | slice | bytes 3145728 | tf_op jit(solution)/shard_map/slice | solution.py:319
  83.1 3.4 %collective-permute-done.11.refs_0_ = bf16[384,1024]{1,0:T(8,128)(2,1)S(1)} collective-permute-done((bf16[384,1024]{1,0:T(8,128)(2,1)S(1)}, bf16[384,1024]{1,0:T(8,128)(2,1)S(1)}, u32[]{:S(2)}, u32[]{:S(2)}) %collective-permute-start.11) | collective-permute-done | bytes 786464 | tf_op jit(solution)/shard_map/ppermute | solution.py:338
  87.4 2.5 %collective-permute-start.15 = (bf16[384,2048]{1,0:T(8,128)(2,1)}, bf16[384,2048]{1,0:T(8,128)(2,1)}, u32[]{:S(2)}, u32[]{:S(2)}) collective-permute-start(bf16[384,2048]{1,0:T(8,128)(2,1)} %slice.34), channel_id=1, source_target_pairs={{0,8},{4,12},{8,0},{12,4},{1,9},{5,13},{9,1},{13,5},{2,10},{6,14},... | collective-permute-start | bytes 4718600 | tf_op jit(solution)/shard_map/ppermute | solution.py:344
  90.9 2.2 broadcast_select_fusion.10
  93.4 7.4 %shard_map.110.refs_6_ = f32[192,128]{1,0:T(8,128)S(1)} custom-call(s32[1]{0:T(128)} %bitcast._, bf16[384,2048]{1,0:T(8,128)(2,1)S(1)} %copy-done.4, bf16[384,1024]{1,0:T(8,128)(2,1)S(1)} %get-tuple-element.82.refs_1_, bf16[384,1024]{1,0:T(8,128)(2,1)S(1)} %get-tuple-element.81.refs_2_.refs_3_, bf16[7168,2048]{1,0:T(8,128)(2,1)} %refs_3_.15, ...), custom_call_target="tpu_custom_call" | custom-call | tf_op jit(solution)/shard_map/pallas_call | solution.py:85
  100.9 4.5 %shard_map.111.refs_6_ = f32[192,128]{1,0:T(8,128)S(1)} custom-call(s32[1]{0:T(128)} %bitcast._, bf16[384,1024]{1,0:T(8,128)(2,1)S(1)} %copy-done.7, bf16[384,1024]{1,0:T(8,128)(2,1)S(1)} %get-tuple-element.82.refs_1_, bf16[384,1024]{1,0:T(8,128)(2,1)S(1)} %get-tuple-element.81.refs_2_.refs_3_, bf16[7168,2048]{1,0:T(8,128)(2,1)} %refs_3_.15, ...), custom_call_target="tpu_custom_call" | custom-call | tf_op jit(solution)/shard_map/pallas_call | solution.py:85
  105.4 7.5 %collective-permute-done.9 = bf16[384,1024]{1,0:T(8,128)(2,1)} collective-permute-done((bf16[384,1024]{1,0:T(8,128)(2,1)}, bf16[384,1024]{1,0:T(8,128)(2,1)}, u32[]{:S(2)}, u32[]{:S(2)}) %collective-permute-start.9) | collective-permute-done | bytes 786464 | tf_op jit(solution)/shard_map/ppermute | solution.py:228
  115.8 2.8 %slice.35 = bf16[384,2048]{1,0:T(8,128)(2,1)} slice(bf16[384,7168]{1,0:T(8,128)(2,1)} %refs_0_.3), slice={[0:384], [5120:7168]} | slice | bytes 3145728 | tf_op jit(solution)/shard_map/slice | solution.py:319
  121.8 20.0 %shard_map.112.refs_6_ = f32[192,128]{1,0:T(8,128)S(1)} custom-call(s32[1]{0:T(128)} %bitcast._, bf16[384,7168]{1,0:T(8,128)(2,1)} %refs_0_.3, bf16[384,1024]{1,0:T(8,128)(2,1)S(1)} %get-tuple-element.80.refs_1_, bf16[384,1024]{1,0:T(8,128)(2,1)S(1)} %get-tuple-element.79.refs_2_, bf16[7168,2048]{1,0:T(8,128)(2,1)} %refs_3_.15, ...), custom_call_target="tpu_custom_call" | custom-call | tf_op jit(solution)/shard_map/pallas_call | solution.py:85
  141.9 7.6 %shard_map.113.refs_6_ = f32[192,128]{1,0:T(8,128)S(1)} custom-call(s32[1]{0:T(128)} %bitcast._, bf16[384,2048]{1,0:T(8,128)(2,1)} %collective-permute-done.15.refs_0_, bf16[384,1024]{1,0:T(8,128)(2,1)S(1)} %get-tuple-element.82.refs_1_, bf16[384,1024]{1,0:T(8,128)(2,1)S(1)} %get-tuple-element.81.refs_2_.refs_3_, bf16[7168,2048]{1,0:T(8,128)(2,1)} %refs_3_.15, ...), custom_call_target="tpu_custom_call" | custom-call | tf_op jit(solution)/shard_map/pallas_call | solution.py:85
  155.0 7.4 %shard_map.114.refs_6_ = f32[192,128]{1,0:T(8,128)S(1)} custom-call(s32[1]{0:T(128)} %bitcast._, bf16[384,2048]{1,0:T(8,128)(2,1)S(1)} %copy-done.5, bf16[384,1024]{1,0:T(8,128)(2,1)S(1)} %get-tuple-element.78.refs_1_.refs_2_, bf16[384,1024]{1,0:T(8,128)(2,1)S(1)} %get-tuple-element.77.refs_2_.refs_4_, bf16[7168,2048]{1,0:T(8,128)(2,1)} %refs_3_.15, ...), custom_call_target="tpu_custom_call" | custom-call | tf_op jit(solution)/shard_map/pallas_call | solution.py:85
  162.5 4.5 %shard_map.115.refs_6_ = f32[192,128]{1,0:T(8,128)S(1)} custom-call(s32[1]{0:T(128)} %bitcast._, bf16[384,1024]{1,0:T(8,128)(2,1)S(1)} %copy-done.8, bf16[384,1024]{1,0:T(8,128)(2,1)S(1)} %get-tuple-element.78.refs_1_.refs_2_, bf16[384,1024]{1,0:T(8,128)(2,1)S(1)} %get-tuple-element.77.refs_2_.refs_4_, bf16[7168,2048]{1,0:T(8,128)(2,1)} %refs_3_.15, ...), custom_call_target="tpu_custom_call" | custom-call | tf_op jit(solution)/shard_map/pallas_call | solution.py:85
  167.0 7.6 %shard_map.116.refs_10_ = f32[192,128]{1,0:T(8,128)S(1)} custom-call(s32[1]{0:T(128)} %bitcast._, bf16[384,2048]{1,0:T(8,128)(2,1)} %collective-permute-done.15.refs_0_, bf16[384,1024]{1,0:T(8,128)(2,1)S(1)} %get-tuple-element.78.refs_1_.refs_2_, bf16[384,1024]{1,0:T(8,128)(2,1)S(1)} %get-tuple-element.77.refs_2_.refs_4_, bf16[7168,2048]{1,0:T(8,128)(2,1)} %refs_3_.15, ...), custom_call_target="tpu_custom_call" | custom-call | tf_op jit(solution)/shard_map/pallas_call | solution.py:85
  174.6 12.7 %shard_map.117 = f32[192,128]{1,0:T(8,128)} custom-call(s32[1]{0:T(128)} %bitcast._, bf16[384,2048]{1,0:T(8,128)(2,1)} %collective-permute-done.17.refs_0_, bf16[384,1024]{1,0:T(8,128)(2,1)S(1)} %get-tuple-element.82.refs_1_, bf16[384,1024]{1,0:T(8,128)(2,1)S(1)} %get-tuple-element.78.refs_1_.refs_2_, ...), custom_call_target="tpu_custom_call" | custom-call | tf_op jit(solution)/shard_map/pallas_call | solution.py:85
  188.3 7.3 %collective-permute-start.21 = (bf16[576,128]{1,0:T(8,128)(2,1)}, bf16[576,128]{1,0:T(8,128)(2,1)}, u32[]{:S(2)}, u32[]{:S(2)}) collective-permute-start(bf16[576,128]{1,0:T(8,128)(2,1)} %convert_element_type.6), channel_id=1, source_target_pairs={{0,1},{1,2},{2,3},{3,0},{4,5},{5,6},{6,7},{7,4},{8,9},{9,10},{10,1... | collective-permute-start | bytes 442376 | tf_op jit(solution)/shard_map/ppermute | solution.py:265
  195.6 2.6 %collective-permute-start.23 = (bf16[576,128]{1,0:T(8,128)(2,1)}, bf16[576,128]{1,0:T(8,128)(2,1)}, u32[]{:S(2)}, u32[]{:S(2)}) collective-permute-start(bf16[576,128]{1,0:T(8,128)(2,1)} %convert_element_type.6), channel_id=1, source_target_pairs={{0,3},{1,0},{2,1},{3,2},{4,7},{5,4},{6,5},{7,6},{8,11},{9,8},{10,9... | collective-permute-start | bytes 442376 | tf_op jit(solution)/shard_map/ppermute | solution.py:265
  205.7 20.1 %shard_map.118 = f32[192,128]{1,0:T(8,128)S(1)} custom-call(s32[1]{0:T(128)} %bitcast._, bf16[384,7168]{1,0:T(8,128)(2,1)} %refs_0_.3, bf16[384,1024]{1,0:T(8,128)(2,1)S(1)} %get-tuple-element.76.refs_1_, bf16[384,1024]{1,0:T(8,128)(2,1)S(1)} %get-tuple-element.75.refs_2_, bf16[7168,2048]{1,0:T(8,128)(2,1)} %refs_3_.15, ...), custom_call_target="tpu_custom_call" | custom-call | tf_op jit(solution)/shard_map/pallas_call | solution.py:85
  226.8 2.4 collective-permute-start.26
  231.3 2.9 %shard_map.119 = (f32[384,384]{1,0:T(8,128)}, f32[64,384]{1,0:T(8,128)}) custom-call(s32[1,6]{1,0:T(1,128)} %lengths.1, bf16[1,576,128]{2,1,0:T(8,128)(2,1)} %convert_bitcast_fusion.refs_0_, bf16[1,576,128]{2,1,0:T(8,128)(2,1)} %bitcast.2.refs_1_, bf16[1,576,128]{2,1,0:T(8,128)(2,1)} %bitcast.3.refs_2_, bf16[1,576,128]{2,1,0:T(8,128)(2,1)} %bitcast.4.refs_3_), custom_call_target="tpu_custom_call" | custom-call | tf_op jit(solution)/shard_map/pallas_call | solution.py:164
  234.8 2.7 %shard_map.120 = f32[6,4]{1,0:T(8,128)} custom-call(f32[384,384]{1,0:T(8,128)} %get-tuple-element.69.masked, f32[64,384]{1,0:T(8,128)} %get-tuple-element.70.down_sum, bf16[4,128,64]{2,1,0:T(8,128)(2,1)} %pad_maximum_fusion.bank, bf16[1,192,128]{2,1,0:T(8,128)(2,1)} %bitcast.22, bf16[1,192,128]{2,1,0:T(8,128)(2,1)} %bitcast.23, ...), custom_call_target="tpu_custom_call" | custom-call | tf_op jit(solution)/shard_map/pallas_call | solution.py:388
  (124 shorter events, 44.6 us)
Async XLA Ops:
  0.0 71.1 %collective-permute-start.6 = (bf16[7168,2048]{1,0:T(8,128)(2,1)}, bf16[7168,2048]{1,0:T(8,128)(2,1)}, u32[]{:S(2)}, u32[]{:S(2)}) collective-permute-start(bf16[7168,2048]{1,0:T(8,128)(2,1)} %refs_3_.15), channel_id=1, source_target_pairs={{0,4},{4,0},{8,12},{12,8},{1,5},{5,1},{9,13},{13,9},{2,6},{6,2},{1... | collective-permute-start | bytes 88080392 | tf_op jit(solution)/shard_map/ppermute | solution.py:306
  3.1 36.0 %collective-permute-start.1 = (bf16[384,1024]{1,0:T(8,128)(2,1)}, bf16[384,1024]{1,0:T(8,128)(2,1)}, u32[]{:S(2)}, u32[]{:S(2)}) collective-permute-start(bf16[384,1024]{1,0:T(8,128)(2,1)} %get-tuple-element.83), channel_id=1, source_target_pairs={{8,2},{9,3},{12,6},{13,7},{3,9},{2,8},{7,13},{6,12},{24,18},{25,19... | collective-permute-start | bytes 2359304 | tf_op jit(solution)/shard_map/ppermute | solution.py:228
  4.6 34.5 %collective-permute-start.2 = (bf16[384,1024]{1,0:T(8,128)(2,1)}, bf16[384,1024]{1,0:T(8,128)(2,1)}, u32[]{:S(2)}, u32[]{:S(2)}) collective-permute-start(bf16[384,1024]{1,0:T(8,128)(2,1)} %get-tuple-element.83), channel_id=1, source_target_pairs={{0,2},{1,3},{4,6},{5,7},{11,9},{10,8},{15,13},{14,12},{16,18},{17,... | collective-permute-start | bytes 2359304 | tf_op jit(solution)/shard_map/ppermute | solution.py:228
  12.7 26.4 %collective-permute-start = (bf16[384,1024]{1,0:T(8,128)(2,1)}, bf16[384,1024]{1,0:T(8,128)(2,1)}, u32[]{:S(2)}, u32[]{:S(2)}) collective-permute-start(bf16[384,1024]{1,0:T(8,128)(2,1)} %get-tuple-element.84), channel_id=1, source_target_pairs={{8,0},{9,1},{12,4},{13,5},{3,11},{2,10},{7,15},{6,14},{24,16},{25,... | collective-permute-start | bytes 2359304 | tf_op jit(solution)/shard_map/ppermute | solution.py:228
  16.7 54.4 %collective-permute-start.5 = (bf16[384,2048]{1,0:T(8,128)(2,1)}, bf16[384,2048]{1,0:T(8,128)(2,1)S(1)}, u32[]{:S(2)}, u32[]{:S(2)}) collective-permute-start(bf16[384,2048]{1,0:T(8,128)(2,1)} %slice.32), channel_id=1, source_target_pairs={{0,8},{4,12},{8,0},{12,4},{1,9},{5,13},{9,1},{13,5},{2,10},{6,14},... | collective-permute-start | bytes 4718600 | tf_op jit(solution)/shard_map/ppermute | solution.py:331
  40.4 26.3 %collective-permute-start.3 = (bf16[384,1024]{1,0:T(8,128)(2,1)S(1)}, bf16[384,1024]{1,0:T(8,128)(2,1)}, u32[]{:S(2)}, u32[]{:S(2)}) collective-permute-start(bf16[384,1024]{1,0:T(8,128)(2,1)S(1)} %broadcast_select_fusion.13), channel_id=1, source_target_pairs={{0,1},{1,0},{2,3},{3,2},{4,5},{5,4},{6,7},{7,6},{11,10},{10,11},{9... | collective-permute-start | bytes 2359304 | tf_op jit(solution)/shard_map/ppermute | solution.py:228
  48.9 17.9 %collective-permute-start.4 = (bf16[384,1024]{1,0:T(8,128)(2,1)S(1)}, bf16[384,1024]{1,0:T(8,128)(2,1)}, u32[]{:S(2)}, u32[]{:S(2)}) collective-permute-start(bf16[384,1024]{1,0:T(8,128)(2,1)S(1)} %broadcast_select_fusion.13), channel_id=1, source_target_pairs={{1,2},{2,1},{5,6},{6,5},{10,9},{9,10},{14,13},{13,14},{17,18},{18,... | collective-permute-start | bytes 2359304 | tf_op jit(solution)/shard_map/ppermute | solution.py:228
  51.6 34.9 %collective-permute-start.11 = (bf16[384,1024]{1,0:T(8,128)(2,1)S(1)}, bf16[384,1024]{1,0:T(8,128)(2,1)S(1)}, u32[]{:S(2)}, u32[]{:S(2)}) collective-permute-start(bf16[384,1024]{1,0:T(8,128)(2,1)S(1)} %slice.33), channel_id=1, source_target_pairs={{0,8},{4,12},{8,0},{12,4},{1,9},{5,13},{9,1},{13,5},{2,10},{6,14},... | collective-permute-start | bytes 2359304 | tf_op jit(solution)/shard_map/ppermute | solution.py:338
  54.8 35.1 %copy-start.17 = (bf16[7168,64]{0,1:T(8,128)(2,1)S(1)}, bf16[7168,64]{0,1:T(8,128)(2,1)}, u32[]{:S(2)}) copy-start(bf16[7168,64]{0,1:T(8,128)(2,1)} %param.19) | copy-start | bytes 2752516
  71.1 34.3 %collective-permute-start.10 = (bf16[384,1024]{1,0:T(8,128)(2,1)}, bf16[384,1024]{1,0:T(8,128)(2,1)}, u32[]{:S(2)}, u32[]{:S(2)}) collective-permute-start(bf16[384,1024]{1,0:T(8,128)(2,1)} %broadcast_select_fusion.12), channel_id=1, source_target_pairs={{1,2},{2,1},{5,6},{6,5},{10,9},{9,10},{14,13},{13,14},{17,18},{18,... | collective-permute-start | bytes 2359304 | tf_op jit(solution)/shard_map/ppermute | solution.py:228
  72.7 32.7 %collective-permute-start.7 = (bf16[384,1024]{1,0:T(8,128)(2,1)}, bf16[384,1024]{1,0:T(8,128)(2,1)}, u32[]{:S(2)}, u32[]{:S(2)}) collective-permute-start(bf16[384,1024]{1,0:T(8,128)(2,1)} %collective-permute-done.3), channel_id=1, source_target_pairs={{1,2},{2,1},{5,6},{6,5},{10,9},{9,10},{14,13},{13,14},{17,18},{18,... | collective-permute-start | bytes 2359304 | tf_op jit(solution)/shard_map/ppermute | solution.py:228
  74.2 31.2 %collective-permute-start.8 = (bf16[384,1024]{1,0:T(8,128)(2,1)}, bf16[384,1024]{1,0:T(8,128)(2,1)}, u32[]{:S(2)}, u32[]{:S(2)}) collective-permute-start(bf16[384,1024]{1,0:T(8,128)(2,1)} %collective-permute-done.4), channel_id=1, source_target_pairs={{1,0},{2,3},{5,4},{6,7},{10,11},{9,8},{14,15},{13,12},{17,16},{18,... | collective-permute-start | bytes 2359304 | tf_op jit(solution)/shard_map/ppermute | solution.py:228
  75.5 37.4 %collective-permute-start.9 = (bf16[384,1024]{1,0:T(8,128)(2,1)}, bf16[384,1024]{1,0:T(8,128)(2,1)}, u32[]{:S(2)}, u32[]{:S(2)}) collective-permute-start(bf16[384,1024]{1,0:T(8,128)(2,1)} %broadcast_select_fusion.12), channel_id=1, source_target_pairs={{0,1},{1,0},{2,3},{3,2},{4,5},{5,4},{6,7},{7,6},{11,10},{10,11},{9... | collective-permute-start | bytes 2359304 | tf_op jit(solution)/shard_map/ppermute | solution.py:228
  87.4 54.4 %collective-permute-start.15 = (bf16[384,2048]{1,0:T(8,128)(2,1)}, bf16[384,2048]{1,0:T(8,128)(2,1)}, u32[]{:S(2)}, u32[]{:S(2)}) collective-permute-start(bf16[384,2048]{1,0:T(8,128)(2,1)} %slice.34), channel_id=1, source_target_pairs={{0,8},{4,12},{8,0},{12,4},{1,9},{5,13},{9,1},{13,5},{2,10},{6,14},... | collective-permute-start | bytes 4718600 | tf_op jit(solution)/shard_map/ppermute | solution.py:344
  90.9 76.1 %copy-start = (bf16[7168,64]{1,0:T(8,128)(2,1)}, bf16[7168,64]{1,0:T(8,128)(2,1)S(1)}, u32[]{:S(2)}) copy-start(bf16[7168,64]{1,0:T(8,128)(2,1)S(1)} %copy.16.refs_5_.refs_9_) | copy-start | bytes 2752516
  112.9 37.1 %collective-permute-start.12 = (bf16[384,1024]{1,0:T(8,128)(2,1)}, bf16[384,1024]{1,0:T(8,128)(2,1)}, u32[]{:S(2)}, u32[]{:S(2)}) collective-permute-start(bf16[384,1024]{1,0:T(8,128)(2,1)} %collective-permute-done.7), channel_id=1, source_target_pairs={{1,0},{2,3},{5,4},{6,7},{10,11},{9,8},{14,15},{13,12},{17,16},{18,... | collective-permute-start | bytes 2359304 | tf_op jit(solution)/shard_map/ppermute | solution.py:228
  114.2 35.9 %collective-permute-start.13 = (bf16[384,1024]{1,0:T(8,128)(2,1)}, bf16[384,1024]{1,0:T(8,128)(2,1)}, u32[]{:S(2)}, u32[]{:S(2)}) collective-permute-start(bf16[384,1024]{1,0:T(8,128)(2,1)} %collective-permute-done.9), channel_id=1, source_target_pairs={{1,2},{2,1},{5,6},{6,5},{10,9},{9,10},{14,13},{13,14},{17,18},{18,... | collective-permute-start | bytes 2359304 | tf_op jit(solution)/shard_map/ppermute | solution.py:228
  118.5 56.0 %collective-permute-start.17 = (bf16[384,2048]{1,0:T(8,128)(2,1)}, bf16[384,2048]{1,0:T(8,128)(2,1)}, u32[]{:S(2)}, u32[]{:S(2)}) collective-permute-start(bf16[384,2048]{1,0:T(8,128)(2,1)} %slice.35), channel_id=1, source_target_pairs={{0,8},{4,12},{8,0},{12,4},{1,9},{5,13},{9,1},{13,5},{2,10},{6,14},... | collective-permute-start | bytes 4718600 | tf_op jit(solution)/shard_map/ppermute | solution.py:352
  118.8 31.2 %collective-permute-start.14 = (bf16[384,1024]{1,0:T(8,128)(2,1)}, bf16[384,1024]{1,0:T(8,128)(2,1)}, u32[]{:S(2)}, u32[]{:S(2)}) collective-permute-start(bf16[384,1024]{1,0:T(8,128)(2,1)} %collective-permute-done.10), channel_id=1, source_target_pairs={{1,0},{2,3},{5,4},{6,7},{10,11},{9,8},{14,15},{13,12},{17,16},{18,... | collective-permute-start | bytes 2359304 | tf_op jit(solution)/shard_map/ppermute | solution.py:228
  150.1 37.6 %collective-permute-start.16 = (bf16[384,1024]{1,0:T(8,128)(2,1)}, bf16[384,1024]{1,0:T(8,128)(2,1)}, u32[]{:S(2)}, u32[]{:S(2)}) collective-permute-start(bf16[384,1024]{1,0:T(8,128)(2,1)} %collective-permute-done.13), channel_id=1, source_target_pairs={{1,0},{2,3},{5,4},{6,7},{10,11},{9,8},{14,15},{13,12},{17,16},{18,... | collective-permute-start | bytes 2359304 | tf_op jit(solution)/shard_map/ppermute | solution.py:228
  151.4 36.2 %collective-permute-start.18 = (bf16[4,2048]{1,0:T(4,128)(2,1)S(1)}, bf16[4,2048]{1,0:T(4,128)(2,1)S(1)}, u32[]{:S(2)}, u32[]{:S(2)}) collective-permute-start(bf16[4,2048]{1,0:T(4,128)(2,1)S(1)} %copy-done.23), channel_id=1, source_target_pairs={{4,0},{8,4},{12,8},{0,12},{5,1},{9,5},{13,9},{1,13},{6,2},{10,6},{... | collective-permute-start | bytes 49160 | tf_op jit(solution)/shard_map/ppermute | solution.py:297
  151.5 36.1 %collective-permute-start.19 = (bf16[4,2048]{1,0:T(4,128)(2,1)S(1)}, bf16[4,2048]{1,0:T(4,128)(2,1)S(1)}, u32[]{:S(2)}, u32[]{:S(2)}) collective-permute-start(bf16[4,2048]{1,0:T(4,128)(2,1)S(1)} %copy-done.23), channel_id=1, source_target_pairs={{8,0},{12,4},{0,8},{4,12},{9,1},{13,5},{1,9},{5,13},{10,2},{14,6},... | collective-permute-start | bytes 49160 | tf_op jit(solution)/shard_map/ppermute | solution.py:297
  153.3 34.3 %collective-permute-start.20 = (bf16[4,2048]{1,0:T(4,128)(2,1)S(1)}, bf16[4,2048]{1,0:T(4,128)(2,1)S(1)}, u32[]{:S(2)}, u32[]{:S(2)}) collective-permute-start(bf16[4,2048]{1,0:T(4,128)(2,1)S(1)} %copy-done.23), channel_id=1, source_target_pairs={{12,0},{0,4},{4,8},{8,12},{13,1},{1,5},{5,9},{9,13},{14,2},{2,6},{... | collective-permute-start | bytes 49160 | tf_op jit(solution)/shard_map/ppermute | solution.py:297
  187.3 38.4 %collective-permute-start.24 = (f32[192,128]{1,0:T(8,128)}, f32[192,128]{1,0:T(8,128)}, u32[]{:S(2)}, u32[]{:S(2)}) collective-permute-start(f32[192,128]{1,0:T(8,128)} %shard_map.117), channel_id=1, source_target_pairs={{0,8},{4,12},{8,0},{12,4},{1,9},{5,13},{9,1},{13,5},{2,10},{6,14},... | collective-permute-start | bytes 294920 | tf_op jit(solution)/shard_map/ppermute | solution.py:367
  188.3 40.8 %collective-permute-start.21 = (bf16[576,128]{1,0:T(8,128)(2,1)}, bf16[576,128]{1,0:T(8,128)(2,1)}, u32[]{:S(2)}, u32[]{:S(2)}) collective-permute-start(bf16[576,128]{1,0:T(8,128)(2,1)} %convert_element_type.6), channel_id=1, source_target_pairs={{0,1},{1,2},{2,3},{3,0},{4,5},{5,6},{6,7},{7,4},{8,9},{9,10},{10,1... | collective-permute-start | bytes 442376 | tf_op jit(solution)/shard_map/ppermute | solution.py:265
  195.6 35.7 %collective-permute-start.22 = (bf16[576,128]{1,0:T(8,128)(2,1)}, bf16[576,128]{1,0:T(8,128)(2,1)}, u32[]{:S(2)}, u32[]{:S(2)}) collective-permute-start(bf16[576,128]{1,0:T(8,128)(2,1)} %convert_element_type.6), channel_id=1, source_target_pairs={{0,2},{1,3},{2,0},{3,1},{4,6},{5,7},{6,4},{7,5},{8,10},{9,11},{10,... | collective-permute-start | bytes 442376 | tf_op jit(solution)/shard_map/ppermute | solution.py:265
  195.6 35.7 %collective-permute-start.23 = (bf16[576,128]{1,0:T(8,128)(2,1)}, bf16[576,128]{1,0:T(8,128)(2,1)}, u32[]{:S(2)}, u32[]{:S(2)}) collective-permute-start(bf16[576,128]{1,0:T(8,128)(2,1)} %convert_element_type.6), channel_id=1, source_target_pairs={{0,3},{1,0},{2,1},{3,2},{4,7},{5,4},{6,5},{7,6},{8,11},{9,8},{10,9... | collective-permute-start | bytes 442376 | tf_op jit(solution)/shard_map/ppermute | solution.py:265
  205.7 24.9 %copy-start.21 = (bf16[4,32,64]{2,1,0:T(8,128)(2,1)S(1)}, bf16[4,32,64]{2,1,0:T(8,128)(2,1)}, u32[]{:S(2)}) copy-start(bf16[4,32,64]{2,1,0:T(8,128)(2,1)} %concatenate.14) | copy-start | bytes 49156
  205.7 24.9 %copy-start.22 = (bf16[4,32,64]{2,1,0:T(8,128)(2,1)S(1)}, bf16[4,32,64]{2,1,0:T(8,128)(2,1)}, u32[]{:S(2)}) copy-start(bf16[4,32,64]{2,1,0:T(8,128)(2,1)} %concatenate.15) | copy-start | bytes 49156
  226.7 7.5 %collective-permute-start.25 = (bf16[192,128]{1,0:T(8,128)(2,1)S(1)}, bf16[192,128]{1,0:T(8,128)(2,1)S(1)}, u32[]{:S(2)}, u32[]{:S(2)}) collective-permute-start(bf16[192,128]{1,0:T(8,128)(2,1)S(1)} %add_convert_fusion), channel_id=1, source_target_pairs={{0,1},{1,2},{2,3},{3,0},{4,5},{5,6},{6,7},{7,4},{8,9},{9,10},{10,1... | collective-permute-start | bytes 147464 | tf_op jit(solution)/shard_map/ppermute | solution.py:265
  226.8 7.4 %collective-permute-start.26 = (bf16[192,128]{1,0:T(8,128)(2,1)S(1)}, bf16[192,128]{1,0:T(8,128)(2,1)S(1)}, u32[]{:S(2)}, u32[]{:S(2)}) collective-permute-start(bf16[192,128]{1,0:T(8,128)(2,1)S(1)} %add_convert_fusion), channel_id=1, source_target_pairs={{0,2},{1,3},{2,0},{3,1},{4,6},{5,7},{6,4},{7,5},{8,10},{9,11},{10,... | collective-permute-start | bytes 147464 | tf_op jit(solution)/shard_map/ppermute | solution.py:265
  229.1 5.1 %collective-permute-start.27 = (bf16[192,128]{1,0:T(8,128)(2,1)S(1)}, bf16[192,128]{1,0:T(8,128)(2,1)S(1)}, u32[]{:S(2)}, u32[]{:S(2)}) collective-permute-start(bf16[192,128]{1,0:T(8,128)(2,1)S(1)} %add_convert_fusion), channel_id=1, source_target_pairs={{0,3},{1,0},{2,1},{3,2},{4,7},{5,4},{6,5},{7,6},{8,11},{9,8},{10,9... | collective-permute-start | bytes 147464 | tf_op jit(solution)/shard_map/ppermute | solution.py:265
  (23 other events, 144.0 us)

commit v3 on v2

v3 whole, which is shorter than its diff:
```python
import functools

import jax
import jax.numpy as jnp
from jax import lax
from jax.experimental import pallas as pl
from jax.experimental.pallas import tpu as pltpu
from jax.sharding import PartitionSpec as P

R = 64
EPS = 1e-06
AXES = ("dp", "tensor")
NT = (((1,), (1,)), ((), ()))
VMEM_BYTES = 48 * 1024 * 1024


def after(value, *others):
    return lax.optimization_barrier((value,) + others)[0]


def silu(gate):
    return 0.5 * gate * (1.0 + jnp.tanh(0.5 * gate))


def project_kernel(bounds, parts, _, *refs):
    pieces = len(bounds) - 1
    gates = refs[:pieces]
    grads = refs[pieces : pieces + parts]
    weights = refs[pieces + parts : pieces + 2 * parts]
    basis, before, out, act = refs[pieces + 2 * parts :]
    step = pl.program_id(0)

    @pl.when(step == 0)
    def _():
        out[...] = before[...]

    for index, gate in enumerate(gates):

        @pl.when((step >= bounds[index]) & (step < bounds[index + 1]))
        def _(gate=gate):
            act[...] = silu(gate[...].astype(jnp.float32))

    hidden_grad = sum(
        lax.dot_general(grad[...], weight[...], NT, preferred_element_type=jnp.float32)
        for grad, weight in zip(grads, weights, strict=True)
    )
    up_grad = (hidden_grad * act[...]).astype(jnp.bfloat16)
    out[...] += lax.dot_general(basis[...], up_grad, NT, preferred_element_type=jnp.float32)


def project(gates, grads, weights, half, basis, before, start, tile):
    gates = [gate if isinstance(gate, tuple) else (gate, 0, gate.shape[1]) for gate in gates]
    bounds = [0]
    for _, _, width in gates:
        bounds.append(bounds[-1] + width // tile)
    pairs = [(g, block, w) for w, group in zip(weights, grads, strict=True) for g, block in group]
    parts = len(pairs)
    rows, depth = pairs[0][0].shape
    first = start // tile
    whole = lambda i, _: (0, 0)

    def gate_spec(index):
        low, high, skip = bounds[index], bounds[index + 1], gates[index][1] // tile
        return pl.BlockSpec((rows, tile), lambda i, _: (0, skip + jnp.clip(i - low, 0, high - low - 1)))

    def weight_spec(block):
        if block is None:
            return pl.BlockSpec((tile, depth), lambda i, half: (first + i, half[0]))
        if block == "other":
            return pl.BlockSpec((tile, depth), lambda i, half: (first + i, 1 - half[0]))
        return pl.BlockSpec((tile, depth), lambda i, _: (first + i, block))

    return pl.pallas_call(
        functools.partial(project_kernel, bounds, parts),
        grid_spec=pltpu.PrefetchScalarGridSpec(
            num_scalar_prefetch=1,
            grid=(bounds[-1],),
            in_specs=[gate_spec(index) for index in range(len(gates))]
            + [pl.BlockSpec((rows, depth), whole)] * parts
            + [weight_spec(block) for _, block, _ in pairs]
            + [pl.BlockSpec((R, tile), lambda i, _: (0, first + i)), pl.BlockSpec((R, rows), whole)],
            out_specs=pl.BlockSpec((R, rows), whole),
            scratch_shapes=[pltpu.VMEM((rows, tile), jnp.float32)],
        ),
        out_shape=jax.ShapeDtypeStruct((R, rows), jnp.float32),
        compiler_params=pltpu.CompilerParams(vmem_limit_bytes=VMEM_BYTES),
        cost_estimate=pl.CostEstimate(flops=1, bytes_accessed=1, transcendentals=0),
    )(half, *[gate for gate, _, _ in gates], *[g for g, _, _ in pairs], *[w for _, _, w in pairs], basis, before)


def local_kernel(cuts, gate, up, grad, normed, hidden_basis, output_basis, normed_basis, out, *cut_gates):
    step = pl.program_id(0)

    @pl.when(step == 0)
    def _():
        out[:R] = lax.dot_general(output_basis[...], grad[...], NT, preferred_element_type=jnp.float32)
        out[R : 2 * R] = lax.dot_general(normed_basis[...], normed[...], NT, preferred_element_type=jnp.float32)
        out[2 * R :] = jnp.zeros((R, out.shape[1]), jnp.float32)

    value = gate[...].astype(jnp.float32)
    hidden = (silu(value) * up[...].astype(jnp.float32)).astype(jnp.bfloat16)
    out[2 * R :] += lax.dot_general(hidden_basis[...], hidden, NT, preferred_element_type=jnp.float32)
    for (low, high), piece in zip(cuts, cut_gates, strict=True):

        @pl.when((step >= low) & (step < high))
        def _(piece=piece):
            piece[...] = gate[...]


def local_products(gate, up, grad, normed, hidden_basis, output_basis, normed_basis, tile, cuts=()):
    rows, width = gate.shape
    whole = lambda i: (0, 0)

    def cut_spec(low, high):
        return pl.BlockSpec((rows, tile), lambda i: (0, jnp.clip(i - low, 0, high - low - 1)))

    return pl.pallas_call(
        functools.partial(local_kernel, cuts),
        grid=(width // tile,),
        in_specs=[
            pl.BlockSpec((rows, tile), lambda i: (0, i)),
            pl.BlockSpec((rows, tile), lambda i: (0, i)),
            pl.BlockSpec(grad.shape, whole),
            pl.BlockSpec(normed.shape, whole),
            pl.BlockSpec((R, tile), lambda i: (0, i)),
            pl.BlockSpec(output_basis.shape, whole),
            pl.BlockSpec(normed_basis.shape, whole),
        ],
        out_specs=[pl.BlockSpec((3 * R, rows), whole)] + [cut_spec(*cut) for cut in cuts],
        out_shape=[jax.ShapeDtypeStruct((3 * R, rows), jnp.float32)]
        + [jax.ShapeDtypeStruct((rows, (high - low) * tile), gate.dtype) for low, high in cuts],
        compiler_params=pltpu.CompilerParams(vmem_limit_bytes=VMEM_BYTES),
        cost_estimate=pl.CostEstimate(flops=1, bytes_accessed=1, transcendentals=0),
    )(gate, up, grad, normed, hidden_basis, output_basis, normed_basis)


def by_example(lengths, value):
    token = lax.broadcasted_iota(jnp.int32, value.shape, 1)
    begin, members = 0, []
    for e in range(lengths.shape[1]):
        end = begin + lengths[0, e]
        members.append(jnp.where((token >= begin) & (token < end), value, 0.0))
        begin = end
    return jnp.concatenate(members, axis=0)


def outer_sums(lengths, left, right):
    return lax.dot_general(
        by_example(lengths, left),
        right,
        NT,
        precision=lax.Precision.HIGHEST,
        preferred_element_type=jnp.float32,
    )


def down_kernel(lengths, *refs):
    parts, (blocks, up_in, down_sum, bank) = refs[:-4], refs[-4:]
    totals = sum(part[...] for part in parts)
    up_in[...] = totals[R : 2 * R]
    down_sum[...] = outer_sums(lengths, totals[:R], totals[2 * R :])
    count, _, block, _ = blocks.shape
    for n in range(count):
        bank[:, n * block : (n + 1) * block, :] = blocks[n].astype(jnp.float32)


def down_products(lengths, parts, blocks):
    examples = lengths.shape[1]
    count, values, block, _ = blocks.shape
    return pl.pallas_call(
        down_kernel,
        in_specs=[pl.BlockSpec(memory_space=pltpu.SMEM)] + [pl.BlockSpec(memory_space=pltpu.VMEM)] * (len(parts) + 1),
        out_shape=(
            jax.ShapeDtypeStruct((R, parts[0].shape[1]), jnp.float32),
            jax.ShapeDtypeStruct((examples * R, R), jnp.float32),
            jax.ShapeDtypeStruct((values, count * block, R), jnp.float32),
        ),
        compiler_params=pltpu.CompilerParams(vmem_limit_bytes=VMEM_BYTES),
        cost_estimate=pl.CostEstimate(flops=1, bytes_accessed=1, transcendentals=0),
    )(lengths, *parts, blocks)


def score_kernel(lengths, up_in, down_sum, bank, *refs):
    partials, out = refs[:-1], refs[-1]
    up_sum = outer_sums(lengths, sum(part[...].astype(jnp.float32) for part in partials), up_in[...])
    values, examples = out.shape
    rows = lax.broadcasted_iota(jnp.int32, out.shape, 0)
    columns = lax.broadcasted_iota(jnp.int32, out.shape, 1)
    scores = jnp.zeros(out.shape, jnp.float32)
    for e in range(examples):
        down, up = down_sum[e * R : (e + 1) * R], up_sum[e * R : (e + 1) * R]
        mean = jnp.sum(down * down + up * up, axis=(0, 1), keepdims=True) / (2 * R * R)
        inverse = lax.rsqrt(mean + EPS)
        down = (down * inverse).astype(jnp.bfloat16).astype(jnp.float32)
        up = (up * inverse).astype(jnp.bfloat16).astype(jnp.float32)
        for v in range(values):
            one = jnp.sum(down * bank[v, :R] + up * bank[v, R:], axis=(0, 1), keepdims=True)
            scores = jnp.where((rows == v) & (columns == e), one, scores)
    out[...] = scores * float(2 * R * R) ** (-0.5)


def split(total, most, unit):
    for count in range(most, 0, -1):
        if total % (count * unit) == 0:
            return count
    return 1


class Line:
    def __init__(self, side, lane, place):
        self.spot = jnp.where(side == 0, place, 3 - place)
        self.even = (side + lane) % 2

    @staticmethod
    def at(a, c, s):
        return (2 * a + c) * 4 + (s if a == 0 else 3 - s)

    def move(self, value, hops, other=False):
        pairs = [
            (self.at(1 - a if other else a, c, s), self.at(a, c, t)) for a in (0, 1) for c in (0, 1) for s, t in hops
        ]
        return lax.ppermute(value, AXES, pairs)

    def pair(self, value):
        return self.move(value, [(0, 1), (1, 0), (2, 3), (3, 2)])

    def middle(self, value):
        return self.move(value, [(1, 2), (2, 1)])

    def outward(self, value):
        return self.move(value, [(1, 0), (2, 3)])

    def by_block(self, first, second, parity):
        keep = parity == self.even
        return jnp.where(keep, first, second), jnp.where(keep, second, first)


def gather_any(grad, side, lane):
    count = lax.axis_size("dp")
    whole = lax.all_gather(grad, "tensor", axis=1, tiled=True)
    block = whole.shape[1] // count
    far = lax.ppermute(
        lax.dynamic_slice_in_dim(whole, (1 - side) * 2 * block, 2 * block, axis=1),
        "dp",
        [(i, i ^ 2) for i in range(count)],
    )
    near = lax.dynamic_slice_in_dim(whole, side * 2 * block, 2 * block, axis=1)
    return [
        (jnp.where(lane == 0, v[:, :block], v[:, block:]), jnp.where(lane == 0, v[:, block:], v[:, :block]))
        for v in (near, far)
    ]


def all_tensor(value):
    count = lax.axis_size("tensor")
    if count > 8:
        return [lax.psum(value.astype(jnp.float32), "tensor")]
    return [value] + [
        lax.ppermute(value, "tensor", [(i, (i + k) % count) for i in range(count)]) for k in range(1, count)
    ]


def body(
    gate_preact,
    up_output,
    normed_input,
    output_grad,
    down_weight,
    normed_basis,
    output_basis,
    hidden_basis,
    up_basis,
    val_bank,
    lengths,
):
    rows, width = gate_preact.shape
    index, place = lax.axis_index("dp"), lax.axis_index("tensor")
    side, lane = index // 2, index % 2
    count = lax.axis_size("dp")
    across = [(i, i ^ 2) for i in range(count)]
    beside = [(i, i ^ 1) for i in range(count)]

    def local(tile, cuts=()):
        return local_products(
            gate_preact, up_output, output_grad, normed_input, hidden_basis.T, output_basis.T, normed_basis.T, tile, cuts
        )

    values = val_bank.reshape(val_bank.shape[0], -1, R)
    basis = up_basis.T
    zero = jnp.zeros((R, rows), jnp.float32)
    sibling = lax.ppermute(down_weight, "dp", beside)
    both = (down_weight, sibling)

    if count == 4 and lax.axis_size("tensor") == 4 and width % (7 * 128) == 0:
        line = Line(side, lane, place)
        depth = output_grad.shape[1] // 2
        ga, gb = output_grad[:, :depth], output_grad[:, depth:]
        half = (line.spot // 2).astype(jnp.int32)[None]
        inner = (line.spot == 1) | (line.spot == 2)
        tile = width // 7

        def exchange(value, apart):
            return lax.ppermute(value, "tensor", [(i, i ^ apart) for i in range(4)])

        def project_far(far, sources, grads, start):
            return project(sources, grads, both, half, basis, far, start * tile, tile)

        def project_near(near, grads, start, end):
            gate = (gate_preact, start * tile, (end - start) * tile)
            return project([gate], grads, both, half, basis, near, start * tile, tile)

        blocks = lax.all_gather(values, "dp", axis=0)
        xb = line.move(gb, [(3, 2), (2, 3)], other=True)
        ns = line.move(gb, [(0, 2), (1, 3)])
        xa = line.move(ga, [(3, 0), (2, 1)], other=True)
        s0 = lax.ppermute(gate_preact[:, : 2 * tile], "dp", across)
        sums, t2, t3, t5 = local(tile, ((2, 3), (3, 5), (5, 7)))

        ns, xa, xb, sums, t2, t3, t5 = lax.optimization_barrier((ns, xa, xb, sums, t2, t3, t5))
        own = jnp.concatenate([jnp.where(line.spot < 2, ga, ns), jnp.where(line.spot < 2, xa, xb)], axis=0)
        e, m = line.pair(own), line.middle(own)
        s2 = lax.ppermute(t2, "dp", across)

        e, m, sibling, s0, s2, t3, blocks = lax.optimization_barrier((e, m, sibling, s0, s2, t3, blocks))
        both = (down_weight, sibling)
        mm, o = line.middle(e), line.outward(m)
        first_n = line.by_block(own[:rows], e[:rows], line.spot % 2)
        first_f = line.by_block(own[rows:], e[rows:], line.spot % 2)
        first_n, first_f = [[(g, None)] for g in first_n], [[(g, None)] for g in first_f]
        s3 = lax.ppermute(t3, "dp", across)
        near = project_near(zero, first_n, 0, 7)
        far = project_far(zero, [s0, s2], first_f, 0)

        mm, o, s3, near, far, sums, t5 = lax.optimization_barrier((mm, o, s3, near, far, sums, t5))
        oo_f = line.outward(mm[rows:])
        s5 = lax.ppermute(t5, "dp", across)
        paired = exchange(sums, 1)
        third = jnp.where(inner, m, o)
        far = project_far(far, [s3], first_f, 3)

        oo_f, far, third, rest = lax.optimization_barrier((oo_f, far, third, mm))
        oo_n = line.outward(rest[:rows])
        rest_f = line.by_block(third[rows:], jnp.where(inner, rest[rows:], oo_f), line.spot // 2)
        rest_f = [[(g, "other")] for g in rest_f]
        all_f = [a + b for a, b in zip(first_f, rest_f, strict=True)]
        far = project_far(far, [s0, s2, s3], rest_f, 0)
        far = project_far(far, [s5], all_f, 5)

        oo_n, far, paired, sums, near = lax.optimization_barrier((oo_n, far, paired, sums, near))
        back = lax.ppermute(far, "dp", across)
        sums = sums + paired
        other = exchange(sums, 2)
        rest_n = line.by_block(third[:rows], jnp.where(inner, rest[:rows], oo_n), line.spot // 2)
        near = project_near(near, [[(g, "other")] for g in rest_n], 0, 7)

        near, back = lax.optimization_barrier((near, back))
        partials = all_tensor((near + back).astype(jnp.bfloat16))
        up_in, down_sum, bank = down_products(lengths, [sums, other], blocks)
    else:
        half = jnp.zeros((1,), jnp.int32)
        near_grads, far_grads = gather_any(output_grad, side, lane)
        far_gate = lax.ppermute(gate_preact, "dp", across)
        tile = width // split(width, max(1, width // 512), 128)
        up_in, down_sum, bank = down_products(
            lengths, all_tensor(local(tile)[0]), lax.all_gather(values, "dp", axis=0)
        )
        far = project([far_gate], [[(g, 0)] for g in far_grads], both, half, basis, zero, 0, tile)
        back = lax.ppermute(far, "dp", across)
        near = project([gate_preact], [[(g, 0)] for g in near_grads], both, half, basis, zero, 0, tile)
        partials = all_tensor((near + back).astype(jnp.bfloat16))

    return pl.pallas_call(
        score_kernel,
        in_specs=[pl.BlockSpec(memory_space=pltpu.SMEM)]
        + [pl.BlockSpec(memory_space=pltpu.VMEM)] * (3 + len(partials)),
        out_shape=jax.ShapeDtypeStruct((val_bank.shape[0], lengths.shape[1]), jnp.float32),
        compiler_params=pltpu.CompilerParams(vmem_limit_bytes=VMEM_BYTES),
    )(lengths, up_in, down_sum, bank, *partials).T


def solution(mesh):
    placed = (
        P(("parts", "dp"), "tensor"),
        P(("parts", "dp"), "tensor"),
        P(("parts", "dp"), "tensor"),
        P(("parts", "dp"), "tensor"),
        P("tensor", "dp"),
        P("tensor", None),
        P("tensor", None),
        P("tensor", None),
        P("tensor", None),
        P("tensor", "dp"),
        P(("parts", "dp"), None),
    )
    return jax.shard_map(
        body, mesh=mesh, in_specs=placed, out_specs=P(("parts", "dp"), "tensor"), check_vma=False
    )
```

time: 240 us -> 219 us (0.912)
  blocking collectives: 0 us -> 32.4 us
  local copies, waits for them, and re-layouts: 31.2 us -> 12.4 us
  starting transfers between devices: 60.7 us -> 48.7 us
  Pallas kernels: 107 us -> 95.6 us
  waiting for transfers between devices: 27.3 us -> 18.8 us
    all_gather x0 -> x1, blocking collectives: none -> 32.4 us  [body(): blocks = lax.all_gather(values, 'dp', axis=0)]
    pallas_call x12 -> x9, Pallas kernels: 107 us -> 95.6 us  [the longest x6 80.6 us: project(): pl.pallas_call(functools.partial(project_kernel, bounds, parts), grid_spe...]
    ppermute x6 -> x3, starting transfers between devices: 13.7 us -> 4.46 us  [all_tensor(): lax.ppermute(value, 'tensor', [(i, (i + k) % count) for i in range(count)])]
    unnamed x65 -> x32, local copies, waits for them, and re-layouts: 12.8 us -> 4.84 us
    ppermute x13 -> x9, starting transfers between devices: 35.7 us -> 27.9 us  [move(): return lax.ppermute(value, AXES, pairs)]
    ppermute x7 -> x6, waiting for transfers between devices: 7.81 us -> 0.78 us  [the longest x1 0.77 us: body(): s3 = lax.ppermute(t3, 'dp', across)]
    ppermute x7 -> x6, starting transfers between devices: 10.5 us -> 15.8 us  [the longest x2 5.25 us: exchange(): return lax.ppermute(value, 'tensor', [(i, i ^ apart) for i in range(4)])]
    slice x5 -> x2, local copies, waits for them, and re-layouts: 10.1 us -> 4.85 us  [the longest x1 2.78 us: body(): s0 = lax.ppermute(gate_preact[:, :2 * tile], 'dp', across)]
  transfers between devices with their start and end apart: 28 -> 20, of which waited for: 4 -> 6; matrix products, arithmetic and copies ran while one was open for 15% -> 7% of each run, Pallas kernels for 44% -> 43%
where the time goes in v3:
time: 219 us; the launch traced here: 218 us
  Pallas kernels  95.6 us (44%)
  starting transfers between devices  48.7 us (22%)
  blocking collectives  32.4 us (15%)
  waiting for transfers between devices  18.8 us (9%)
  local copies, waits for them, and re-layouts  12.4 us (6%)
  other arithmetic  9.74 us (4%)
    pallas_call x6, Pallas kernels, project(): pl.pallas_call(functools.partial(project_kernel, bounds, parts), grid_spe...  80.6 us
    all_gather x1, blocking collectives, body(): blocks = lax.all_gather(values, 'dp', axis=0)  32.4 us
    ppermute x9, starting transfers between devices, move(): return lax.ppermute(value, AXES, pairs)  27.9 us
    ppermute x9, waiting for transfers between devices, move(): return lax.ppermute(value, AXES, pairs)  16.6 us
    pallas_call x1, Pallas kernels, local_products(): pl.pallas_call(functools.partial(local_kernel, cuts), grid=(width // tile...  11.1 us
    ppermute x2, starting transfers between devices, exchange(): return lax.ppermute(value, 'tensor', [(i, i ^ apart) for i in range(4)])  5.25 us
    select_n x3, other arithmetic, by_block(): return (jnp.where(keep, first, second), jnp.where(keep, second, first))  5.19 us
    unnamed x32, local copies, waits for them, and re-layouts  4.84 us
  transfers between devices with their start and end apart: 20, of which 6 were waited for; matrix products, arithmetic and copies ran while one was open for 7% of the time, Pallas kernels for 43%

profile of v3, /device:TPU:0, one launch (start us, length us, event | category | flops | bytes accessed | tf_op | source)
XLA Modules:
  0.0 218.0 jit_solution(999769340877577375)
XLA Ops:
  0.5 2.6 %fusion = (bf16[384,1024]{1,0:T(8,128)(2,1)}, bf16[384,1024]{1,0:T(8,128)(2,1)}) fusion(bf16[384,2048]{1,0:T(8,128)(2,1)} %grad.1), kind=kLoop, calls=%fused_computation.15 | loop fusion | bytes 3145728 | tf_op jit(solution)/shard_map/slice | solution.py:297
  3.1 5.5 %collective-permute-start = (bf16[384,1024]{1,0:T(8,128)(2,1)}, bf16[384,1024]{1,0:T(8,128)(2,1)S(1)}, u32[]{:S(2)}, u32[]{:S(2)}) collective-permute-start(bf16[384,1024]{1,0:T(8,128)(2,1)} %get-tuple-element.95), channel_id=1, source_target_pairs={{0,2},{1,3},{4,6},{5,7},{11,9},{10,8},{15,13},{14,12},{16,18},{17,... | collective-permute-start | bytes 2359304 | tf_op jit(solution)/shard_map/ppermute | solution.py:222
  8.6 1.6 collective-permute-start.2
  11.7 2.8 %slice.33 = bf16[384,2048]{1,0:T(8,128)(2,1)} slice(bf16[384,7168]{1,0:T(8,128)(2,1)} %refs_0_.3), slice={[0:384], [0:2048]} | slice | bytes 3145728 | tf_op jit(solution)/shard_map/slice | solution.py:316
  14.4 3.6 %collective-permute-start.6 = (bf16[384,2048]{1,0:T(8,128)(2,1)}, bf16[384,2048]{1,0:T(8,128)(2,1)S(1)}, u32[]{:S(2)}, u32[]{:S(2)}) collective-permute-start(bf16[384,2048]{1,0:T(8,128)(2,1)} %slice.33), channel_id=1, source_target_pairs={{0,8},{4,12},{8,0},{12,4},{1,9},{5,13},{9,1},{13,5},{2,10},{6,14},... | collective-permute-start | bytes 4718600 | tf_op jit(solution)/shard_map/ppermute | solution.py:316
  18.0 11.1 %shard_map.109 = (f32[192,384]{1,0:T(8,128)S(1)}, bf16[384,1024]{1,0:T(8,128)(2,1)S(1)}, bf16[384,2048]{1,0:T(8,128)(2,1)S(1)}, bf16[384,2048]{1,0:T(8,128)(2,1)}) custom-call(bf16[384,7168]{1,0:T(8,128)(2,1)} %refs_0_.3, bf16[384,7168]{1,0:T(8,128)(2,1)} %up.1, bf16[384,2048]{1,0:T(8,128)(2,1)} %grad.1, bf16[384,2048]{1,0:T(8,128)(2,1)} %normed.1, ...), custom_call_target="tpu_custom_call" | custom-call | flops 1 | bytes 1 | tf_op jit(solution)/shard_map/pallas_call | solution.py:117
  31.0 1.9 collective-permute-done.1
  32.9 1.5 broadcast_select_fusion.10
  36.1 11.7 %collective-permute-start.3 = (bf16[768,1024]{1,0:T(8,128)(2,1)}, bf16[768,1024]{1,0:T(8,128)(2,1)}, u32[]{:S(2)}, u32[]{:S(2)}) collective-permute-start(bf16[768,1024]{1,0:T(8,128)(2,1)} %pad_maximum_fusion), channel_id=1, source_target_pairs={{0,1},{1,0},{2,3},{3,2},{4,5},{5,4},{6,7},{7,6},{11,10},{10,11},{9... | collective-permute-start | bytes 4718600 | tf_op jit(solution)/shard_map/ppermute | solution.py:222
  47.9 1.8 collective-permute-start.4
  49.7 3.1 %collective-permute-start.7 = (bf16[384,1024]{1,0:T(8,128)(2,1)S(1)}, bf16[384,1024]{1,0:T(8,128)(2,1)S(1)}, u32[]{:S(2)}, u32[]{:S(2)}) collective-permute-start(bf16[384,1024]{1,0:T(8,128)(2,1)S(1)} %get-tuple-element.51), channel_id=1, source_target_pairs={{0,8},{4,12},{8,0},{12,4},{1,9},{5,13},{9,1},{13,5},{2,10},{6,14},... | collective-permute-start | bytes 2359304 | tf_op jit(solution)/shard_map/ppermute | solution.py:322
  52.9 32.4 %all_gather.3.refs_2_ = bf16[4,4,32,64]{3,2,1,0:T(8,128)(2,1)S(1)} all-gather(bf16[1,4,32,64]{3,2,1,0:T(8,128)(2,1)S(1)} %all_gather_reshape.3), channel_id=1, replica_groups=mesh['parts'=2,'dp'=4,'tensor'=4] {'dp'}, dimensions={0}, use_global_device_ids=true | all-gather | bytes 81920 | tf_op jit(solution)/shard_map/all_gather | solution.py:312
  86.4 3.4 %collective-permute-start.10 = (bf16[384,2048]{1,0:T(8,128)(2,1)}, bf16[384,2048]{1,0:T(8,128)(2,1)}, u32[]{:S(2)}, u32[]{:S(2)}) collective-permute-start(bf16[384,2048]{1,0:T(8,128)(2,1)} %copy-done.12), channel_id=1, source_target_pairs={{0,8},{4,12},{8,0},{12,4},{1,9},{5,13},{9,1},{13,5},{2,10},{6,14},... | collective-permute-start | bytes 4718600 | tf_op jit(solution)/shard_map/ppermute | solution.py:330
  89.8 1.8 collective-permute-start.8
  93.0 2.1 broadcast_select_fusion.6
  95.2 19.2 %shard_map.110.refs_6_ = f32[64,384]{1,0:T(8,128)S(1)} custom-call(s32[1]{0:T(128)} %bitcast.3._, bf16[384,7168]{1,0:T(8,128)(2,1)} %refs_0_.3, bf16[384,1024]{1,0:T(8,128)(2,1)S(1)} %get-tuple-element.92.refs_1_, bf16[384,1024]{1,0:T(8,128)(2,1)S(1)} %get-tuple-element.93.refs_2_, bf16[7168,2048]{1,0:T(8,128)(2,1)} %refs_3_.5, ...), custom_call_target="tpu_custom_call" | custom-call | flops 1 | bytes 1 | tf_op jit(solution)/shard_map/pallas_call | solution.py:73
  114.4 9.3 %shard_map.111.refs_6_ = f32[64,384]{1,0:T(8,128)S(1)} custom-call(s32[1]{0:T(128)} %bitcast.3._, bf16[384,2048]{1,0:T(8,128)(2,1)S(1)} %copy-done.2, bf16[384,1024]{1,0:T(8,128)(2,1)S(1)} %collective-permute-done.7.refs_1_, bf16[384,1024]{1,0:T(8,128)(2,1)S(1)} %get-tuple-element.88.refs_2_.refs_1_, ...), custom_call_target="tpu_custom_call" | custom-call | flops 1 | bytes 1 | tf_op jit(solution)/shard_map/pallas_call | solution.py:73
  125.0 5.2 %collective-permute-done.9 = bf16[768,1024]{1,0:T(8,128)(2,1)} collective-permute-done((bf16[768,1024]{1,0:T(8,128)(2,1)}, bf16[768,1024]{1,0:T(8,128)(2,1)}, u32[]{:S(2)}, u32[]{:S(2)}) %collective-permute-start.9) | collective-permute-done | bytes 1572896 | tf_op jit(solution)/shard_map/ppermute | solution.py:222
  130.2 2.1 slice.36
  134.9 7.1 %shard_map.112.refs_8_ = f32[64,384]{1,0:T(8,128)S(1)} custom-call(s32[1]{0:T(128)} %bitcast.3._, bf16[384,2048]{1,0:T(8,128)(2,1)} %collective-permute-done.10.refs_0_.refs_2_, bf16[384,1024]{1,0:T(8,128)(2,1)S(1)} %get-tuple-element.88.refs_2_.refs_1_, bf16[384,1024]{1,0:T(8,128)(2,1)S(1)} %get-tuple-element.87.refs_3_.refs_2_, ...), custom_call_target="tpu_custom_call" | custom-call | flops 1 | bytes 1 | tf_op jit(solution)/shard_map/pallas_call | solution.py:73
  142.0 1.6 broadcast_select_fusion
  143.6 9.5 %collective-permute-done.11 = bf16[384,1024]{1,0:T(8,128)(2,1)} collective-permute-done((bf16[384,1024]{1,0:T(8,128)(2,1)}, bf16[384,1024]{1,0:T(8,128)(2,1)}, u32[]{:S(2)}, u32[]{:S(2)}) %collective-permute-start.11) | collective-permute-done | bytes 786464 | tf_op jit(solution)/shard_map/ppermute | solution.py:222
  153.1 1.8 broadcast_select_fusion.4
  154.9 1.5 collective-permute-start.12
  156.4 2.8 %collective-permute-start.14 = (f32[192,384]{1,0:T(8,128)S(1)}, f32[192,384]{1,0:T(8,128)S(1)}, u32[]{:S(2)}, u32[]{:S(2)}) collective-permute-start(f32[192,384]{1,0:T(8,128)S(1)} %copy-done.8), channel_id=1, source_target_pairs={{0,1},{1,0},{2,3},{3,2},{4,5},{5,4},{6,7},{7,6},{8,9},{9,8},{10,11... | collective-permute-start | bytes 884744 | tf_op jit(solution)/shard_map/ppermute | solution.py:303
  159.2 14.3 %shard_map.113.refs_10_ = f32[64,384]{1,0:T(8,128)S(1)} custom-call(s32[1]{0:T(128)} %bitcast.3._, bf16[384,2048]{1,0:T(8,128)(2,1)S(1)} %copy-done.3, bf16[384,1024]{1,0:T(8,128)(2,1)S(1)} %collective-permute-done.7.refs_1_, bf16[384,2048]{1,0:T(8,128)(2,1)} %collective-permute-done.10.refs_0_.refs_2_, ...), custom_call_target="tpu_custom_call" | custom-call | flops 1 | bytes 1 | tf_op jit(solution)/shard_map/pallas_call | solution.py:73
  173.5 11.6 %shard_map.114 = f32[64,384]{1,0:T(8,128)S(1)} custom-call(s32[1]{0:T(128)} %bitcast.3._, bf16[384,2048]{1,0:T(8,128)(2,1)} %collective-permute-done.13.refs_0_, bf16[384,1024]{1,0:T(8,128)(2,1)S(1)} %get-tuple-element.88.refs_2_.refs_1_, bf16[384,1024]{1,0:T(8,128)(2,1)S(1)} %get-tuple-element.86.refs_3_.refs_2_, ...), custom_call_target="tpu_custom_call" | custom-call | flops 1 | bytes 1 | tf_op jit(solution)/shard_map/pallas_call | solution.py:73
  185.3 2.5 %collective-permute-start.15 = (f32[192,384]{1,0:T(8,128)S(1)}, f32[192,384]{1,0:T(8,128)S(1)}, u32[]{:S(2)}, u32[]{:S(2)}) collective-permute-start(f32[192,384]{1,0:T(8,128)S(1)} %add.26.refs_0_), channel_id=1, source_target_pairs={{0,2},{1,3},{2,0},{3,1},{4,6},{5,7},{6,4},{7,5},{8,10},{9,11},{10,... | collective-permute-start | bytes 884744 | tf_op jit(solution)/shard_map/ppermute | solution.py:303
  189.1 19.1 %shard_map.116 = f32[64,384]{1,0:T(8,128)S(1)} custom-call(s32[1]{0:T(128)} %bitcast.3._, bf16[384,7168]{1,0:T(8,128)(2,1)} %refs_0_.3, bf16[384,1024]{1,0:T(8,128)(2,1)S(1)} %get-tuple-element.84.refs_1_, bf16[384,1024]{1,0:T(8,128)(2,1)S(1)} %get-tuple-element.83.refs_2_, bf16[7168,2048]{1,0:T(8,128)(2,1)} %refs_3_.5, ...), custom_call_target="tpu_custom_call" | custom-call | flops 1 | bytes 1 | tf_op jit(solution)/shard_map/pallas_call | solution.py:73
  208.2 2.0 collective-permute-start.17
  210.2 2.4 %collective-permute-start.19 = (bf16[64,384]{1,0:T(8,128)(2,1)S(1)}, bf16[64,384]{1,0:T(8,128)(2,1)S(1)}, u32[]{:S(2)}, u32[]{:S(2)}) collective-permute-start(bf16[64,384]{1,0:T(8,128)(2,1)S(1)} %add_convert_fusion.refs_0_), channel_id=1, source_target_pairs={{0,3},{1,0},{2,1},{3,2},{4,7},{5,4},{6,5},{7,6},{8,11},{9,8},{10,9... | collective-permute-start | bytes 147464 | tf_op jit(solution)/shard_map/ppermute | solution.py:259
  215.2 2.8 %shard_map.117 = f32[4,6]{1,0:T(4,128)} custom-call(s32[1,6]{1,0:T(1,128)S(1)} %copy-done.11, f32[64,384]{1,0:T(8,128)S(1)} %get-tuple-element.75.up_in, f32[384,64]{1,0:T(8,128)S(1)} %get-tuple-element.76.down_sum, f32[4,128,64]{2,1,0:T(8,128)S(1)} %get-tuple-element.77.bank, bf16[64,384]{1,0:T(8,128)(2,1)S(1)} %add_convert_fusion.refs_0_, ...), custom_call_target="tpu_custom_call" | custom-call | tf_op jit(solution)/shard_map/pallas_call | solution.py:372
  (63 shorter events, 16.0 us)
Async XLA Ops:
  0.0 86.4 %collective-permute-start.5 = (bf16[7168,2048]{1,0:T(8,128)(2,1)}, bf16[7168,2048]{1,0:T(8,128)(2,1)}, u32[]{:S(2)}, u32[]{:S(2)}) collective-permute-start(bf16[7168,2048]{1,0:T(8,128)(2,1)} %refs_3_.5), channel_id=1, source_target_pairs={{0,4},{4,0},{8,12},{12,8},{1,5},{5,1},{9,13},{13,9},{2,6},{6,2},{1... | collective-permute-start | bytes 88080392 | tf_op jit(solution)/shard_map/ppermute | solution.py:291
  3.1 27.9 %collective-permute-start = (bf16[384,1024]{1,0:T(8,128)(2,1)}, bf16[384,1024]{1,0:T(8,128)(2,1)S(1)}, u32[]{:S(2)}, u32[]{:S(2)}) collective-permute-start(bf16[384,1024]{1,0:T(8,128)(2,1)} %get-tuple-element.95), channel_id=1, source_target_pairs={{0,2},{1,3},{4,6},{5,7},{11,9},{10,8},{15,13},{14,12},{16,18},{17,... | collective-permute-start | bytes 2359304 | tf_op jit(solution)/shard_map/ppermute | solution.py:222
  8.6 22.4 %collective-permute-start.2 = (bf16[384,1024]{1,0:T(8,128)(2,1)}, bf16[384,1024]{1,0:T(8,128)(2,1)}, u32[]{:S(2)}, u32[]{:S(2)}) collective-permute-start(bf16[384,1024]{1,0:T(8,128)(2,1)} %get-tuple-element.95), channel_id=1, source_target_pairs={{8,2},{9,3},{12,6},{13,7},{3,9},{2,8},{7,13},{6,12},{24,18},{25,19... | collective-permute-start | bytes 2359304 | tf_op jit(solution)/shard_map/ppermute | solution.py:222
  10.2 7.8 %copy-start.4 = (bf16[7168,64]{0,1:T(8,128)(2,1)S(1)}, bf16[7168,64]{0,1:T(8,128)(2,1)}, u32[]{:S(2)}) copy-start(bf16[7168,64]{0,1:T(8,128)(2,1)} %param.18) | copy-start | bytes 2752516
  10.2 7.8 %copy-start.9 = (bf16[2048,64]{0,1:T(8,128)(2,1)S(1)}, bf16[2048,64]{0,1:T(8,128)(2,1)}, u32[]{:S(2)}) copy-start(bf16[2048,64]{0,1:T(8,128)(2,1)} %param.17) | copy-start | bytes 786436
  10.2 7.8 %copy-start.10 = (bf16[2048,64]{0,1:T(8,128)(2,1)S(1)}, bf16[2048,64]{0,1:T(8,128)(2,1)}, u32[]{:S(2)}) copy-start(bf16[2048,64]{0,1:T(8,128)(2,1)} %param.16) | copy-start | bytes 786436
  10.2 22.7 %collective-permute-start.1 = (bf16[384,1024]{1,0:T(8,128)(2,1)}, bf16[384,1024]{1,0:T(8,128)(2,1)}, u32[]{:S(2)}, u32[]{:S(2)}) collective-permute-start(bf16[384,1024]{1,0:T(8,128)(2,1)} %get-tuple-element.94), channel_id=1, source_target_pairs={{8,0},{9,1},{12,4},{13,5},{3,11},{2,10},{7,15},{6,14},{24,16},{25,... | collective-permute-start | bytes 2359304 | tf_op jit(solution)/shard_map/ppermute | solution.py:222
  14.4 70.8 %collective-permute-start.6 = (bf16[384,2048]{1,0:T(8,128)(2,1)}, bf16[384,2048]{1,0:T(8,128)(2,1)S(1)}, u32[]{:S(2)}, u32[]{:S(2)}) collective-permute-start(bf16[384,2048]{1,0:T(8,128)(2,1)} %slice.33), channel_id=1, source_target_pairs={{0,8},{4,12},{8,0},{12,4},{1,9},{5,13},{9,1},{13,5},{2,10},{6,14},... | collective-permute-start | bytes 4718600 | tf_op jit(solution)/shard_map/ppermute | solution.py:316
  29.8 1.2 copy-start.12
  34.5 1.4 copy-start.13
  34.5 1.6 copy-start.14
  34.5 18.3 %copy-start.15 = (bf16[4,2048]{1,0:T(4,128)(2,1)S(1)}, bf16[4,2048]{1,0:T(4,128)(2,1)}, u32[]{:S(2)}) copy-start(bf16[4,2048]{1,0:T(4,128)(2,1)} %param.20) | copy-start | bytes 49156
  36.1 50.3 %collective-permute-start.3 = (bf16[768,1024]{1,0:T(8,128)(2,1)}, bf16[768,1024]{1,0:T(8,128)(2,1)}, u32[]{:S(2)}, u32[]{:S(2)}) collective-permute-start(bf16[768,1024]{1,0:T(8,128)(2,1)} %pad_maximum_fusion), channel_id=1, source_target_pairs={{0,1},{1,0},{2,3},{3,2},{4,5},{5,4},{6,7},{7,6},{11,10},{10,11},{9... | collective-permute-start | bytes 4718600 | tf_op jit(solution)/shard_map/ppermute | solution.py:222
  47.9 38.6 %collective-permute-start.4 = (bf16[768,1024]{1,0:T(8,128)(2,1)}, bf16[768,1024]{1,0:T(8,128)(2,1)}, u32[]{:S(2)}, u32[]{:S(2)}) collective-permute-start(bf16[768,1024]{1,0:T(8,128)(2,1)} %pad_maximum_fusion), channel_id=1, source_target_pairs={{1,2},{2,1},{5,6},{6,5},{10,9},{9,10},{14,13},{13,14},{17,18},{18,... | collective-permute-start | bytes 4718600 | tf_op jit(solution)/shard_map/ppermute | solution.py:222
  49.7 35.6 %collective-permute-start.7 = (bf16[384,1024]{1,0:T(8,128)(2,1)S(1)}, bf16[384,1024]{1,0:T(8,128)(2,1)S(1)}, u32[]{:S(2)}, u32[]{:S(2)}) collective-permute-start(bf16[384,1024]{1,0:T(8,128)(2,1)S(1)} %get-tuple-element.51), channel_id=1, source_target_pairs={{0,8},{4,12},{8,0},{12,4},{1,9},{5,13},{9,1},{13,5},{2,10},{6,14},... | collective-permute-start | bytes 2359304 | tf_op jit(solution)/shard_map/ppermute | solution.py:322
  86.4 38.6 %collective-permute-start.10 = (bf16[384,2048]{1,0:T(8,128)(2,1)}, bf16[384,2048]{1,0:T(8,128)(2,1)}, u32[]{:S(2)}, u32[]{:S(2)}) collective-permute-start(bf16[384,2048]{1,0:T(8,128)(2,1)} %copy-done.12), channel_id=1, source_target_pairs={{0,8},{4,12},{8,0},{12,4},{1,9},{5,13},{9,1},{13,5},{2,10},{6,14},... | collective-permute-start | bytes 4718600 | tf_op jit(solution)/shard_map/ppermute | solution.py:330
  89.8 35.2 %collective-permute-start.8 = (bf16[768,1024]{1,0:T(8,128)(2,1)}, bf16[768,1024]{1,0:T(8,128)(2,1)}, u32[]{:S(2)}, u32[]{:S(2)}) collective-permute-start(bf16[768,1024]{1,0:T(8,128)(2,1)} %collective-permute-done.3), channel_id=1, source_target_pairs={{1,2},{2,1},{5,6},{6,5},{10,9},{9,10},{14,13},{13,14},{17,18},{18,... | collective-permute-start | bytes 4718600 | tf_op jit(solution)/shard_map/ppermute | solution.py:222
  91.6 38.6 %collective-permute-start.9 = (bf16[768,1024]{1,0:T(8,128)(2,1)}, bf16[768,1024]{1,0:T(8,128)(2,1)}, u32[]{:S(2)}, u32[]{:S(2)}) collective-permute-start(bf16[768,1024]{1,0:T(8,128)(2,1)} %collective-permute-done.4), channel_id=1, source_target_pairs={{1,0},{2,3},{5,4},{6,7},{10,11},{9,8},{14,15},{13,12},{17,16},{18,... | collective-permute-start | bytes 4718600 | tf_op jit(solution)/shard_map/ppermute | solution.py:222
  93.0 2.2 copy-start
  95.1 19.2 %copy-start.2 = (bf16[384,2048]{1,0:T(8,128)(2,1)S(1)}, bf16[384,2048]{1,0:T(8,128)(2,1)}, u32[]{:S(2)}) copy-start(bf16[384,2048]{1,0:T(8,128)(2,1)} %copy-done.1) | copy-start | bytes 4718596
  132.3 20.9 %collective-permute-start.11 = (bf16[384,1024]{1,0:T(8,128)(2,1)}, bf16[384,1024]{1,0:T(8,128)(2,1)}, u32[]{:S(2)}, u32[]{:S(2)}) collective-permute-start(bf16[384,1024]{1,0:T(8,128)(2,1)} %slice.36), channel_id=1, source_target_pairs={{1,0},{2,3},{5,4},{6,7},{10,11},{9,8},{14,15},{13,12},{17,16},{18,... | collective-permute-start | bytes 2359304 | tf_op jit(solution)/shard_map/ppermute | solution.py:222
  133.6 40.0 %collective-permute-start.13 = (bf16[384,2048]{1,0:T(8,128)(2,1)}, bf16[384,2048]{1,0:T(8,128)(2,1)}, u32[]{:S(2)}, u32[]{:S(2)}) collective-permute-start(bf16[384,2048]{1,0:T(8,128)(2,1)} %get-tuple-element.66), channel_id=1, source_target_pairs={{0,8},{4,12},{8,0},{12,4},{1,9},{5,13},{9,1},{13,5},{2,10},{6,14},... | collective-permute-start | bytes 4718600 | tf_op jit(solution)/shard_map/ppermute | solution.py:336
  143.6 12.8 %copy-start.8 = (f32[192,384]{1,0:T(8,128)S(1)}, f32[192,384]{1,0:T(8,128)}, u32[]{:S(2)}) copy-start(f32[192,384]{1,0:T(8,128)} %copy-done.7) | copy-start | bytes 884740
  143.6 15.5 %copy-start.3 = (bf16[384,2048]{1,0:T(8,128)(2,1)S(1)}, bf16[384,2048]{1,0:T(8,128)(2,1)}, u32[]{:S(2)}) copy-start(bf16[384,2048]{1,0:T(8,128)(2,1)} %copy-done.1) | copy-start | bytes 4718596
  154.9 30.2 %collective-permute-start.12 = (bf16[384,1024]{1,0:T(8,128)(2,1)S(1)}, bf16[384,1024]{1,0:T(8,128)(2,1)S(1)}, u32[]{:S(2)}, u32[]{:S(2)}) collective-permute-start(bf16[384,1024]{1,0:T(8,128)(2,1)S(1)} %get-tuple-element.91), channel_id=1, source_target_pairs={{1,0},{2,3},{5,4},{6,7},{10,11},{9,8},{14,15},{13,12},{17,16},{18,... | collective-permute-start | bytes 2359304 | tf_op jit(solution)/shard_map/ppermute | solution.py:222
  156.4 28.7 %collective-permute-start.14 = (f32[192,384]{1,0:T(8,128)S(1)}, f32[192,384]{1,0:T(8,128)S(1)}, u32[]{:S(2)}, u32[]{:S(2)}) collective-permute-start(f32[192,384]{1,0:T(8,128)S(1)} %copy-done.8), channel_id=1, source_target_pairs={{0,1},{1,0},{2,3},{3,2},{4,5},{5,4},{6,7},{7,6},{8,9},{9,8},{10,11... | collective-permute-start | bytes 884744 | tf_op jit(solution)/shard_map/ppermute | solution.py:303
  185.2 23.0 %collective-permute-start.16 = (f32[64,384]{1,0:T(8,128)S(1)}, f32[64,384]{1,0:T(8,128)S(1)}, u32[]{:S(2)}, u32[]{:S(2)}) collective-permute-start(f32[64,384]{1,0:T(8,128)S(1)} %shard_map.114), channel_id=1, source_target_pairs={{0,8},{4,12},{8,0},{12,4},{1,9},{5,13},{9,1},{13,5},{2,10},{6,14},... | collective-permute-start | bytes 294920 | tf_op jit(solution)/shard_map/ppermute | solution.py:350
  185.3 27.4 %collective-permute-start.15 = (f32[192,384]{1,0:T(8,128)S(1)}, f32[192,384]{1,0:T(8,128)S(1)}, u32[]{:S(2)}, u32[]{:S(2)}) collective-permute-start(f32[192,384]{1,0:T(8,128)S(1)} %add.26.refs_0_), channel_id=1, source_target_pairs={{0,2},{1,3},{2,0},{3,1},{4,6},{5,7},{6,4},{7,5},{8,10},{9,11},{10,... | collective-permute-start | bytes 884744 | tf_op jit(solution)/shard_map/ppermute | solution.py:303
  189.1 23.6 %copy-start.11 = (s32[1,6]{1,0:T(1,128)S(1)}, s32[1,6]{1,0:T(1,128)}, u32[]{:S(2)}) copy-start(s32[1,6]{1,0:T(1,128)} %lengths.3) | copy-start | bytes 76
  208.2 5.9 %collective-permute-start.17 = (bf16[64,384]{1,0:T(8,128)(2,1)S(1)}, bf16[64,384]{1,0:T(8,128)(2,1)S(1)}, u32[]{:S(2)}, u32[]{:S(2)}) collective-permute-start(bf16[64,384]{1,0:T(8,128)(2,1)S(1)} %add_convert_fusion.refs_0_), channel_id=1, source_target_pairs={{0,1},{1,2},{2,3},{3,0},{4,5},{5,6},{6,7},{7,4},{8,9},{9,10},{10,1... | collective-permute-start | bytes 147464 | tf_op jit(solution)/shard_map/ppermute | solution.py:259
  210.2 5.0 %collective-permute-start.18 = (bf16[64,384]{1,0:T(8,128)(2,1)S(1)}, bf16[64,384]{1,0:T(8,128)(2,1)S(1)}, u32[]{:S(2)}, u32[]{:S(2)}) collective-permute-start(bf16[64,384]{1,0:T(8,128)(2,1)S(1)} %add_convert_fusion.refs_0_), channel_id=1, source_target_pairs={{0,2},{1,3},{2,0},{3,1},{4,6},{5,7},{6,4},{7,5},{8,10},{9,11},{10,... | collective-permute-start | bytes 147464 | tf_op jit(solution)/shard_map/ppermute | solution.py:259
  210.2 5.0 %collective-permute-start.19 = (bf16[64,384]{1,0:T(8,128)(2,1)S(1)}, bf16[64,384]{1,0:T(8,128)(2,1)S(1)}, u32[]{:S(2)}, u32[]{:S(2)}) collective-permute-start(bf16[64,384]{1,0:T(8,128)(2,1)S(1)} %add_convert_fusion.refs_0_), channel_id=1, source_target_pairs={{0,3},{1,0},{2,1},{3,2},{4,7},{5,4},{6,5},{7,6},{8,11},{9,8},{10,9... | collective-permute-start | bytes 147464 | tf_op jit(solution)/shard_map/ppermute | solution.py:259
  (4 other events, 3.4 us)

commit v4 on v3

--- a/solution.py
+++ b/solution.py
@@ -11,7 +11,7 @@
 EPS = 1e-06
 AXES = ("dp", "tensor")
 NT = (((1,), (1,)), ((), ()))
-VMEM_BYTES = 48 * 1024 * 1024
+VMEM_BYTES = 50 * 1024 * 1024
 
 
 def after(value, *others):
@@ -184,18 +184,19 @@
     partials, out = refs[:-1], refs[-1]
     up_sum = outer_sums(lengths, sum(part[...].astype(jnp.float32) for part in partials), up_in[...])
     values, examples = out.shape
-    rows = lax.broadcasted_iota(jnp.int32, out.shape, 0)
     columns = lax.broadcasted_iota(jnp.int32, out.shape, 1)
     scores = jnp.zeros(out.shape, jnp.float32)
     for e in range(examples):
         down, up = down_sum[e * R : (e + 1) * R], up_sum[e * R : (e + 1) * R]
-        mean = jnp.sum(down * down + up * up, axis=(0, 1), keepdims=True) / (2 * R * R)
+        mean = jnp.sum(jnp.sum(down * down + up * up, axis=0, keepdims=True), axis=1, keepdims=True) / (2 * R * R)
         inverse = lax.rsqrt(mean + EPS)
         down = (down * inverse).astype(jnp.bfloat16).astype(jnp.float32)
         up = (up * inverse).astype(jnp.bfloat16).astype(jnp.float32)
-        for v in range(values):
-            one = jnp.sum(down * bank[v, :R] + up * bank[v, R:], axis=(0, 1), keepdims=True)
-            scores = jnp.where((rows == v) & (columns == e), one, scores)
+        by_column = [
+            jnp.sum(down * bank[v, :R] + up * bank[v, R:], axis=0, keepdims=True) for v in range(values)
+        ]
+        one = jnp.sum(jnp.concatenate(by_column, axis=0), axis=1, keepdims=True)
+        scores = jnp.where(columns == e, one, scores)
     out[...] = scores * float(2 * R * R) ** (-0.5)
 
 

time: 219 us -> 217 us (level)
    unnamed x32 -> x28, local copies, waits for them, and re-layouts: 4.84 us -> 3.34 us
  transfers between devices with their start and end apart: 20 -> 20, of which waited for: 6 -> 6; matrix products, arithmetic and copies ran while one was open for 7% -> 6% of each run, Pallas kernels for 43% -> 43%
where the time goes in v4:
time: 217 us; the launch traced here: 216 us
  Pallas kernels  95.7 us (44%)
  starting transfers between devices  49.4 us (23%)
  blocking collectives  32.9 us (15%)
  waiting for transfers between devices  18.8 us (9%)
  local copies, waits for them, and re-layouts  11 us (5%)
  other arithmetic  8.24 us (4%)
    pallas_call x6, Pallas kernels, project(): pl.pallas_call(functools.partial(project_kernel, bounds, parts), grid_spe...  80.9 us
    all_gather x1, blocking collectives, body(): blocks = lax.all_gather(values, 'dp', axis=0)  32.9 us
    ppermute x9, starting transfers between devices, move(): return lax.ppermute(value, AXES, pairs)  27.9 us
    ppermute x9, waiting for transfers between devices, move(): return lax.ppermute(value, AXES, pairs)  16.7 us
    pallas_call x1, Pallas kernels, local_products(): pl.pallas_call(functools.partial(local_kernel, cuts), grid=(width // tile...  11.5 us
    ppermute x2, starting transfers between devices, exchange(): return lax.ppermute(value, 'tensor', [(i, i ^ apart) for i in range(4)])  5.65 us
    select_n x3, other arithmetic, by_block(): return (jnp.where(keep, first, second), jnp.where(keep, second, first))  5.19 us
    ppermute x3, starting transfers between devices, all_tensor(): lax.ppermute(value, 'tensor', [(i, (i + k) % count) for i in range(count)])  4.47 us
  transfers between devices with their start and end apart: 20, of which 6 were waited for; matrix products, arithmetic and copies ran while one was open for 6% of the time, Pallas kernels for 43%

profile of v4, /device:TPU:0, one launch (start us, length us, event | category | flops | bytes accessed | tf_op | source)
XLA Modules:
  0.0 216.3 jit_solution(189984217499631304)
XLA Ops:
  0.5 2.7 %fusion = (bf16[384,1024]{1,0:T(8,128)(2,1)}, bf16[384,1024]{1,0:T(8,128)(2,1)}) fusion(bf16[384,2048]{1,0:T(8,128)(2,1)} %grad.1), kind=kLoop, calls=%fused_computation.15 | loop fusion | bytes 3145728 | tf_op jit(solution)/shard_map/slice | solution.py:298
  3.1 5.5 %collective-permute-start = (bf16[384,1024]{1,0:T(8,128)(2,1)}, bf16[384,1024]{1,0:T(8,128)(2,1)S(1)}, u32[]{:S(2)}, u32[]{:S(2)}) collective-permute-start(bf16[384,1024]{1,0:T(8,128)(2,1)} %get-tuple-element.95), channel_id=1, source_target_pairs={{0,2},{1,3},{4,6},{5,7},{11,9},{10,8},{15,13},{14,12},{16,18},{17,... | collective-permute-start | bytes 2359304 | tf_op jit(solution)/shard_map/ppermute | solution.py:223
  8.7 1.5 collective-permute-start.2
  10.2 1.4 collective-permute-start.1
  11.7 2.7 %slice.33 = bf16[384,2048]{1,0:T(8,128)(2,1)} slice(bf16[384,7168]{1,0:T(8,128)(2,1)} %refs_0_.3), slice={[0:384], [0:2048]} | slice | bytes 3145728 | tf_op jit(solution)/shard_map/slice | solution.py:317
  14.4 3.5 %collective-permute-start.6 = (bf16[384,2048]{1,0:T(8,128)(2,1)}, bf16[384,2048]{1,0:T(8,128)(2,1)}, u32[]{:S(2)}, u32[]{:S(2)}) collective-permute-start(bf16[384,2048]{1,0:T(8,128)(2,1)} %slice.33), channel_id=1, source_target_pairs={{0,8},{4,12},{8,0},{12,4},{1,9},{5,13},{9,1},{13,5},{2,10},{6,14},... | collective-permute-start | bytes 4718600 | tf_op jit(solution)/shard_map/ppermute | solution.py:317
  17.9 11.5 %shard_map.109 = (f32[192,384]{1,0:T(8,128)S(1)}, bf16[384,1024]{1,0:T(8,128)(2,1)S(1)}, bf16[384,2048]{1,0:T(8,128)(2,1)}, bf16[384,2048]{1,0:T(8,128)(2,1)}) custom-call(bf16[384,7168]{1,0:T(8,128)(2,1)} %refs_0_.3, bf16[384,7168]{1,0:T(8,128)(2,1)} %up.1, bf16[384,2048]{1,0:T(8,128)(2,1)} %grad.1, bf16[384,2048]{1,0:T(8,128)(2,1)} %normed.1, ...), custom_call_target="tpu_custom_call" | custom-call | flops 1 | bytes 1 | tf_op jit(solution)/shard_map/pallas_call | solution.py:117
  30.1 2.8 %collective-permute-done.1 = bf16[384,1024]{1,0:T(8,128)(2,1)} collective-permute-done((bf16[384,1024]{1,0:T(8,128)(2,1)}, bf16[384,1024]{1,0:T(8,128)(2,1)}, u32[]{:S(2)}, u32[]{:S(2)}) %collective-permute-start.1) | collective-permute-done | bytes 786464 | tf_op jit(solution)/shard_map/ppermute | solution.py:223
  35.4 11.8 %collective-permute-start.3 = (bf16[768,1024]{1,0:T(8,128)(2,1)S(1)}, bf16[768,1024]{1,0:T(8,128)(2,1)}, u32[]{:S(2)}, u32[]{:S(2)}) collective-permute-start(bf16[768,1024]{1,0:T(8,128)(2,1)S(1)} %pad_maximum_fusion), channel_id=1, source_target_pairs={{0,1},{1,0},{2,3},{3,2},{4,5},{5,4},{6,7},{7,6},{11,10},{10,11},{9... | collective-permute-start | bytes 4718600 | tf_op jit(solution)/shard_map/ppermute | solution.py:223
  47.2 1.8 collective-permute-start.4
  49.0 3.1 %collective-permute-start.7 = (bf16[384,1024]{1,0:T(8,128)(2,1)S(1)}, bf16[384,1024]{1,0:T(8,128)(2,1)S(1)}, u32[]{:S(2)}, u32[]{:S(2)}) collective-permute-start(bf16[384,1024]{1,0:T(8,128)(2,1)S(1)} %get-tuple-element.51), channel_id=1, source_target_pairs={{0,8},{4,12},{8,0},{12,4},{1,9},{5,13},{9,1},{13,5},{2,10},{6,14},... | collective-permute-start | bytes 2359304 | tf_op jit(solution)/shard_map/ppermute | solution.py:323
  52.3 32.9 %all_gather.3.refs_2_ = bf16[4,4,32,64]{3,2,1,0:T(8,128)(2,1)S(1)} all-gather(bf16[1,4,32,64]{3,2,1,0:T(8,128)(2,1)S(1)} %all_gather_reshape.3), channel_id=1, replica_groups=mesh['parts'=2,'dp'=4,'tensor'=4] {'dp'}, dimensions={0}, use_global_device_ids=true | all-gather | bytes 81920 | tf_op jit(solution)/shard_map/all_gather | solution.py:313
  85.2 3.4 %collective-permute-start.10 = (bf16[384,2048]{1,0:T(8,128)(2,1)}, bf16[384,2048]{1,0:T(8,128)(2,1)}, u32[]{:S(2)}, u32[]{:S(2)}) collective-permute-start(bf16[384,2048]{1,0:T(8,128)(2,1)} %get-tuple-element.55), channel_id=1, source_target_pairs={{0,8},{4,12},{8,0},{12,4},{1,9},{5,13},{9,1},{13,5},{2,10},{6,14},... | collective-permute-start | bytes 4718600 | tf_op jit(solution)/shard_map/ppermute | solution.py:331
  88.6 1.8 collective-permute-start.8
  91.7 2.1 broadcast_select_fusion.6
  93.9 19.1 %shard_map.110.refs_6_ = f32[64,384]{1,0:T(8,128)S(1)} custom-call(s32[1]{0:T(128)} %bitcast.3._, bf16[384,7168]{1,0:T(8,128)(2,1)} %refs_0_.3, bf16[384,1024]{1,0:T(8,128)(2,1)S(1)} %get-tuple-element.92.refs_1_, bf16[384,1024]{1,0:T(8,128)(2,1)S(1)} %get-tuple-element.93.refs_2_, bf16[7168,2048]{1,0:T(8,128)(2,1)} %refs_3_.5, ...), custom_call_target="tpu_custom_call" | custom-call | flops 1 | bytes 1 | tf_op jit(solution)/shard_map/pallas_call | solution.py:73
  113.0 9.5 %shard_map.111.refs_6_ = f32[64,384]{1,0:T(8,128)S(1)} custom-call(s32[1]{0:T(128)} %bitcast.3._, bf16[384,2048]{1,0:T(8,128)(2,1)} %collective-permute-done.6.refs_0_, bf16[384,1024]{1,0:T(8,128)(2,1)S(1)} %collective-permute-done.7.refs_1_, bf16[384,1024]{1,0:T(8,128)(2,1)S(1)} %get-tuple-element.88.refs_2_.refs_1_, ...), custom_call_target="tpu_custom_call" | custom-call | flops 1 | bytes 1 | tf_op jit(solution)/shard_map/pallas_call | solution.py:73
  123.8 5.1 %collective-permute-done.9 = bf16[768,1024]{1,0:T(8,128)(2,1)} collective-permute-done((bf16[768,1024]{1,0:T(8,128)(2,1)}, bf16[768,1024]{1,0:T(8,128)(2,1)}, u32[]{:S(2)}, u32[]{:S(2)}) %collective-permute-start.9) | collective-permute-done | bytes 1572896 | tf_op jit(solution)/shard_map/ppermute | solution.py:223
  128.9 2.1 slice.36
  134.0 7.1 %shard_map.112.refs_8_ = f32[64,384]{1,0:T(8,128)S(1)} custom-call(s32[1]{0:T(128)} %bitcast.3._, bf16[384,2048]{1,0:T(8,128)(2,1)} %collective-permute-done.10.refs_0_.refs_2_, bf16[384,1024]{1,0:T(8,128)(2,1)S(1)} %get-tuple-element.88.refs_2_.refs_1_, bf16[384,1024]{1,0:T(8,128)(2,1)S(1)} %get-tuple-element.87.refs_3_.refs_2_, ...), custom_call_target="tpu_custom_call" | custom-call | flops 1 | bytes 1 | tf_op jit(solution)/shard_map/pallas_call | solution.py:73
  141.1 1.6 broadcast_select_fusion
  142.7 8.8 %collective-permute-done.11 = bf16[384,1024]{1,0:T(8,128)(2,1)} collective-permute-done((bf16[384,1024]{1,0:T(8,128)(2,1)}, bf16[384,1024]{1,0:T(8,128)(2,1)}, u32[]{:S(2)}, u32[]{:S(2)}) %collective-permute-start.11) | collective-permute-done | bytes 786464 | tf_op jit(solution)/shard_map/ppermute | solution.py:223
  151.5 1.8 broadcast_select_fusion.4
  153.3 1.5 collective-permute-start.12
  154.8 2.8 %collective-permute-start.14 = (f32[192,384]{1,0:T(8,128)S(1)}, f32[192,384]{1,0:T(8,128)S(1)}, u32[]{:S(2)}, u32[]{:S(2)}) collective-permute-start(f32[192,384]{1,0:T(8,128)S(1)} %copy-done.6), channel_id=1, source_target_pairs={{0,1},{1,0},{2,3},{3,2},{4,5},{5,4},{6,7},{7,6},{8,9},{9,8},{10,11... | collective-permute-start | bytes 884744 | tf_op jit(solution)/shard_map/ppermute | solution.py:304
  157.5 14.5 %shard_map.113.refs_10_ = f32[64,384]{1,0:T(8,128)S(1)} custom-call(s32[1]{0:T(128)} %bitcast.3._, bf16[384,2048]{1,0:T(8,128)(2,1)} %collective-permute-done.6.refs_0_, bf16[384,1024]{1,0:T(8,128)(2,1)S(1)} %collective-permute-done.7.refs_1_, bf16[384,2048]{1,0:T(8,128)(2,1)} %collective-permute-done.10.refs_0_.refs_2_, ...), custom_call_target="tpu_custom_call" | custom-call | flops 1 | bytes 1 | tf_op jit(solution)/shard_map/pallas_call | solution.py:73
  172.1 11.7 %shard_map.114 = f32[64,384]{1,0:T(8,128)S(1)} custom-call(s32[1]{0:T(128)} %bitcast.3._, bf16[384,2048]{1,0:T(8,128)(2,1)} %collective-permute-done.13.refs_0_, bf16[384,1024]{1,0:T(8,128)(2,1)S(1)} %get-tuple-element.88.refs_2_.refs_1_, bf16[384,1024]{1,0:T(8,128)(2,1)S(1)} %get-tuple-element.86.refs_3_.refs_2_, ...), custom_call_target="tpu_custom_call" | custom-call | flops 1 | bytes 1 | tf_op jit(solution)/shard_map/pallas_call | solution.py:73
  183.9 2.9 %collective-permute-start.15 = (f32[192,384]{1,0:T(8,128)S(1)}, f32[192,384]{1,0:T(8,128)S(1)}, u32[]{:S(2)}, u32[]{:S(2)}) collective-permute-start(f32[192,384]{1,0:T(8,128)S(1)} %add.26.refs_0_), channel_id=1, source_target_pairs={{0,2},{1,3},{2,0},{3,1},{4,6},{5,7},{6,4},{7,5},{8,10},{9,11},{10,... | collective-permute-start | bytes 884744 | tf_op jit(solution)/shard_map/ppermute | solution.py:304
  188.1 19.1 %shard_map.116 = f32[64,384]{1,0:T(8,128)S(1)} custom-call(s32[1]{0:T(128)} %bitcast.3._, bf16[384,7168]{1,0:T(8,128)(2,1)} %refs_0_.3, bf16[384,1024]{1,0:T(8,128)(2,1)S(1)} %get-tuple-element.84.refs_1_, bf16[384,1024]{1,0:T(8,128)(2,1)S(1)} %get-tuple-element.83.refs_2_, bf16[7168,2048]{1,0:T(8,128)(2,1)} %refs_3_.5, ...), custom_call_target="tpu_custom_call" | custom-call | flops 1 | bytes 1 | tf_op jit(solution)/shard_map/pallas_call | solution.py:73
  207.2 2.0 collective-permute-start.17
  209.3 2.4 %collective-permute-start.19 = (bf16[64,384]{1,0:T(8,128)(2,1)S(1)}, bf16[64,384]{1,0:T(8,128)(2,1)S(1)}, u32[]{:S(2)}, u32[]{:S(2)}) collective-permute-start(bf16[64,384]{1,0:T(8,128)(2,1)S(1)} %add_convert_fusion.refs_0_), channel_id=1, source_target_pairs={{0,3},{1,0},{2,1},{3,2},{4,7},{5,4},{6,5},{7,6},{8,11},{9,8},{10,9... | collective-permute-start | bytes 147464 | tf_op jit(solution)/shard_map/ppermute | solution.py:260
  214.3 2.1 shard_map.117
  (59 shorter events, 13.5 us)
Async XLA Ops:
  0.0 85.2 %collective-permute-start.5 = (bf16[7168,2048]{1,0:T(8,128)(2,1)}, bf16[7168,2048]{1,0:T(8,128)(2,1)}, u32[]{:S(2)}, u32[]{:S(2)}) collective-permute-start(bf16[7168,2048]{1,0:T(8,128)(2,1)} %refs_3_.5), channel_id=1, source_target_pairs={{0,4},{4,0},{8,12},{12,8},{1,5},{5,1},{9,13},{13,9},{2,6},{6,2},{1... | collective-permute-start | bytes 88080392 | tf_op jit(solution)/shard_map/ppermute | solution.py:292
  3.1 27.0 %collective-permute-start = (bf16[384,1024]{1,0:T(8,128)(2,1)}, bf16[384,1024]{1,0:T(8,128)(2,1)S(1)}, u32[]{:S(2)}, u32[]{:S(2)}) collective-permute-start(bf16[384,1024]{1,0:T(8,128)(2,1)} %get-tuple-element.95), channel_id=1, source_target_pairs={{0,2},{1,3},{4,6},{5,7},{11,9},{10,8},{15,13},{14,12},{16,18},{17,... | collective-permute-start | bytes 2359304 | tf_op jit(solution)/shard_map/ppermute | solution.py:223
  8.7 21.5 %collective-permute-start.2 = (bf16[384,1024]{1,0:T(8,128)(2,1)}, bf16[384,1024]{1,0:T(8,128)(2,1)}, u32[]{:S(2)}, u32[]{:S(2)}) collective-permute-start(bf16[384,1024]{1,0:T(8,128)(2,1)} %get-tuple-element.95), channel_id=1, source_target_pairs={{8,2},{9,3},{12,6},{13,7},{3,9},{2,8},{7,13},{6,12},{24,18},{25,19... | collective-permute-start | bytes 2359304 | tf_op jit(solution)/shard_map/ppermute | solution.py:223
  10.2 7.7 %copy-start.2 = (bf16[7168,64]{0,1:T(8,128)(2,1)S(1)}, bf16[7168,64]{0,1:T(8,128)(2,1)}, u32[]{:S(2)}) copy-start(bf16[7168,64]{0,1:T(8,128)(2,1)} %param.18) | copy-start | bytes 2752516
  10.2 7.7 %copy-start.7 = (bf16[2048,64]{0,1:T(8,128)(2,1)S(1)}, bf16[2048,64]{0,1:T(8,128)(2,1)}, u32[]{:S(2)}) copy-start(bf16[2048,64]{0,1:T(8,128)(2,1)} %param.17) | copy-start | bytes 786436
  10.2 7.7 %copy-start.8 = (bf16[2048,64]{0,1:T(8,128)(2,1)S(1)}, bf16[2048,64]{0,1:T(8,128)(2,1)}, u32[]{:S(2)}) copy-start(bf16[2048,64]{0,1:T(8,128)(2,1)} %param.16) | copy-start | bytes 786436
  10.2 22.7 %collective-permute-start.1 = (bf16[384,1024]{1,0:T(8,128)(2,1)}, bf16[384,1024]{1,0:T(8,128)(2,1)}, u32[]{:S(2)}, u32[]{:S(2)}) collective-permute-start(bf16[384,1024]{1,0:T(8,128)(2,1)} %get-tuple-element.94), channel_id=1, source_target_pairs={{8,0},{9,1},{12,4},{13,5},{3,11},{2,10},{7,15},{6,14},{24,16},{25,... | collective-permute-start | bytes 2359304 | tf_op jit(solution)/shard_map/ppermute | solution.py:223
  14.4 70.8 %collective-permute-start.6 = (bf16[384,2048]{1,0:T(8,128)(2,1)}, bf16[384,2048]{1,0:T(8,128)(2,1)}, u32[]{:S(2)}, u32[]{:S(2)}) collective-permute-start(bf16[384,2048]{1,0:T(8,128)(2,1)} %slice.33), channel_id=1, source_target_pairs={{0,8},{4,12},{8,0},{12,4},{1,9},{5,13},{9,1},{13,5},{2,10},{6,14},... | collective-permute-start | bytes 4718600 | tf_op jit(solution)/shard_map/ppermute | solution.py:317
  17.9 15.0 %copy-start.10 = (bf16[384,2048]{1,0:T(8,128)(2,1)S(1)}, bf16[384,2048]{1,0:T(8,128)(2,1)}, u32[]{:S(2)}) copy-start(bf16[384,2048]{1,0:T(8,128)(2,1)} %grad.1) | copy-start | bytes 4718596
  34.2 0.9 copy-start.11
  34.3 1.2 copy-start.12
  34.3 17.9 %copy-start.13 = (bf16[4,2048]{1,0:T(4,128)(2,1)S(1)}, bf16[4,2048]{1,0:T(4,128)(2,1)}, u32[]{:S(2)}) copy-start(bf16[4,2048]{1,0:T(4,128)(2,1)} %param.20) | copy-start | bytes 49156
  35.4 49.7 %collective-permute-start.3 = (bf16[768,1024]{1,0:T(8,128)(2,1)S(1)}, bf16[768,1024]{1,0:T(8,128)(2,1)}, u32[]{:S(2)}, u32[]{:S(2)}) collective-permute-start(bf16[768,1024]{1,0:T(8,128)(2,1)S(1)} %pad_maximum_fusion), channel_id=1, source_target_pairs={{0,1},{1,0},{2,3},{3,2},{4,5},{5,4},{6,7},{7,6},{11,10},{10,11},{9... | collective-permute-start | bytes 4718600 | tf_op jit(solution)/shard_map/ppermute | solution.py:223
  47.2 37.9 %collective-permute-start.4 = (bf16[768,1024]{1,0:T(8,128)(2,1)S(1)}, bf16[768,1024]{1,0:T(8,128)(2,1)}, u32[]{:S(2)}, u32[]{:S(2)}) collective-permute-start(bf16[768,1024]{1,0:T(8,128)(2,1)S(1)} %pad_maximum_fusion), channel_id=1, source_target_pairs={{1,2},{2,1},{5,6},{6,5},{10,9},{9,10},{14,13},{13,14},{17,18},{18,... | collective-permute-start | bytes 4718600 | tf_op jit(solution)/shard_map/ppermute | solution.py:223
  49.0 36.1 %collective-permute-start.7 = (bf16[384,1024]{1,0:T(8,128)(2,1)S(1)}, bf16[384,1024]{1,0:T(8,128)(2,1)S(1)}, u32[]{:S(2)}, u32[]{:S(2)}) collective-permute-start(bf16[384,1024]{1,0:T(8,128)(2,1)S(1)} %get-tuple-element.51), channel_id=1, source_target_pairs={{0,8},{4,12},{8,0},{12,4},{1,9},{5,13},{9,1},{13,5},{2,10},{6,14},... | collective-permute-start | bytes 2359304 | tf_op jit(solution)/shard_map/ppermute | solution.py:323
  85.2 38.6 %collective-permute-start.10 = (bf16[384,2048]{1,0:T(8,128)(2,1)}, bf16[384,2048]{1,0:T(8,128)(2,1)}, u32[]{:S(2)}, u32[]{:S(2)}) collective-permute-start(bf16[384,2048]{1,0:T(8,128)(2,1)} %get-tuple-element.55), channel_id=1, source_target_pairs={{0,8},{4,12},{8,0},{12,4},{1,9},{5,13},{9,1},{13,5},{2,10},{6,14},... | collective-permute-start | bytes 4718600 | tf_op jit(solution)/shard_map/ppermute | solution.py:331
  88.6 35.2 %collective-permute-start.8 = (bf16[768,1024]{1,0:T(8,128)(2,1)}, bf16[768,1024]{1,0:T(8,128)(2,1)}, u32[]{:S(2)}, u32[]{:S(2)}) collective-permute-start(bf16[768,1024]{1,0:T(8,128)(2,1)} %collective-permute-done.3), channel_id=1, source_target_pairs={{1,2},{2,1},{5,6},{6,5},{10,9},{9,10},{14,13},{13,14},{17,18},{18,... | collective-permute-start | bytes 4718600 | tf_op jit(solution)/shard_map/ppermute | solution.py:223
  90.4 38.6 %collective-permute-start.9 = (bf16[768,1024]{1,0:T(8,128)(2,1)}, bf16[768,1024]{1,0:T(8,128)(2,1)}, u32[]{:S(2)}, u32[]{:S(2)}) collective-permute-start(bf16[768,1024]{1,0:T(8,128)(2,1)} %collective-permute-done.4), channel_id=1, source_target_pairs={{1,0},{2,3},{5,4},{6,7},{10,11},{9,8},{14,15},{13,12},{17,16},{18,... | collective-permute-start | bytes 4718600 | tf_op jit(solution)/shard_map/ppermute | solution.py:223
  91.7 2.2 %copy-start = (bf16[7168,64]{0,1:T(8,128)(2,1)S(1)}, bf16[7168,64]{0,1:T(8,128)(2,1)}, u32[]{:S(2)}) copy-start(bf16[7168,64]{0,1:T(8,128)(2,1)} %param.19) | copy-start | bytes 2752516
  131.0 20.5 %collective-permute-start.11 = (bf16[384,1024]{1,0:T(8,128)(2,1)}, bf16[384,1024]{1,0:T(8,128)(2,1)}, u32[]{:S(2)}, u32[]{:S(2)}) collective-permute-start(bf16[384,1024]{1,0:T(8,128)(2,1)} %slice.36), channel_id=1, source_target_pairs={{1,0},{2,3},{5,4},{6,7},{10,11},{9,8},{14,15},{13,12},{17,16},{18,... | collective-permute-start | bytes 2359304 | tf_op jit(solution)/shard_map/ppermute | solution.py:223
  132.3 39.8 %collective-permute-start.13 = (bf16[384,2048]{1,0:T(8,128)(2,1)}, bf16[384,2048]{1,0:T(8,128)(2,1)}, u32[]{:S(2)}, u32[]{:S(2)}) collective-permute-start(bf16[384,2048]{1,0:T(8,128)(2,1)} %get-tuple-element.66), channel_id=1, source_target_pairs={{0,8},{4,12},{8,0},{12,4},{1,9},{5,13},{9,1},{13,5},{2,10},{6,14},... | collective-permute-start | bytes 4718600 | tf_op jit(solution)/shard_map/ppermute | solution.py:337
  133.1 0.9 copy-start.4
  142.7 12.0 %copy-start.6 = (f32[192,384]{1,0:T(8,128)S(1)}, f32[192,384]{1,0:T(8,128)}, u32[]{:S(2)}) copy-start(f32[192,384]{1,0:T(8,128)} %copy-done.5) | copy-start | bytes 884740
  153.3 30.5 %collective-permute-start.12 = (bf16[384,1024]{1,0:T(8,128)(2,1)S(1)}, bf16[384,1024]{1,0:T(8,128)(2,1)S(1)}, u32[]{:S(2)}, u32[]{:S(2)}) collective-permute-start(bf16[384,1024]{1,0:T(8,128)(2,1)S(1)} %get-tuple-element.91), channel_id=1, source_target_pairs={{1,0},{2,3},{5,4},{6,7},{10,11},{9,8},{14,15},{13,12},{17,16},{18,... | collective-permute-start | bytes 2359304 | tf_op jit(solution)/shard_map/ppermute | solution.py:223
  154.8 29.0 %collective-permute-start.14 = (f32[192,384]{1,0:T(8,128)S(1)}, f32[192,384]{1,0:T(8,128)S(1)}, u32[]{:S(2)}, u32[]{:S(2)}) collective-permute-start(f32[192,384]{1,0:T(8,128)S(1)} %copy-done.6), channel_id=1, source_target_pairs={{0,1},{1,0},{2,3},{3,2},{4,5},{5,4},{6,7},{7,6},{8,9},{9,8},{10,11... | collective-permute-start | bytes 884744 | tf_op jit(solution)/shard_map/ppermute | solution.py:304
  183.8 23.4 %collective-permute-start.16 = (f32[64,384]{1,0:T(8,128)S(1)}, f32[64,384]{1,0:T(8,128)S(1)}, u32[]{:S(2)}, u32[]{:S(2)}) collective-permute-start(f32[64,384]{1,0:T(8,128)S(1)} %shard_map.114), channel_id=1, source_target_pairs={{0,8},{4,12},{8,0},{12,4},{1,9},{5,13},{9,1},{13,5},{2,10},{6,14},... | collective-permute-start | bytes 294920 | tf_op jit(solution)/shard_map/ppermute | solution.py:351
  183.9 4.2 %copy-start.1 = (bf16[7168,64]{0,1:T(8,128)(2,1)S(1)}, bf16[7168,64]{0,1:T(8,128)(2,1)}, u32[]{:S(2)}) copy-start(bf16[7168,64]{0,1:T(8,128)(2,1)} %param.19) | copy-start | bytes 2752516
  183.9 27.8 %collective-permute-start.15 = (f32[192,384]{1,0:T(8,128)S(1)}, f32[192,384]{1,0:T(8,128)S(1)}, u32[]{:S(2)}, u32[]{:S(2)}) collective-permute-start(f32[192,384]{1,0:T(8,128)S(1)} %add.26.refs_0_), channel_id=1, source_target_pairs={{0,2},{1,3},{2,0},{3,1},{4,6},{5,7},{6,4},{7,5},{8,10},{9,11},{10,... | collective-permute-start | bytes 884744 | tf_op jit(solution)/shard_map/ppermute | solution.py:304
  188.1 23.6 %copy-start.9 = (s32[1,6]{1,0:T(1,128)S(1)}, s32[1,6]{1,0:T(1,128)}, u32[]{:S(2)}) copy-start(s32[1,6]{1,0:T(1,128)} %lengths.3) | copy-start | bytes 76
  207.2 5.9 %collective-permute-start.17 = (bf16[64,384]{1,0:T(8,128)(2,1)S(1)}, bf16[64,384]{1,0:T(8,128)(2,1)S(1)}, u32[]{:S(2)}, u32[]{:S(2)}) collective-permute-start(bf16[64,384]{1,0:T(8,128)(2,1)S(1)} %add_convert_fusion.refs_0_), channel_id=1, source_target_pairs={{0,1},{1,2},{2,3},{3,0},{4,5},{5,6},{6,7},{7,4},{8,9},{9,10},{10,1... | collective-permute-start | bytes 147464 | tf_op jit(solution)/shard_map/ppermute | solution.py:260
  209.2 5.0 %collective-permute-start.18 = (bf16[64,384]{1,0:T(8,128)(2,1)S(1)}, bf16[64,384]{1,0:T(8,128)(2,1)S(1)}, u32[]{:S(2)}, u32[]{:S(2)}) collective-permute-start(bf16[64,384]{1,0:T(8,128)(2,1)S(1)} %add_convert_fusion.refs_0_), channel_id=1, source_target_pairs={{0,2},{1,3},{2,0},{3,1},{4,6},{5,7},{6,4},{7,5},{8,10},{9,11},{10,... | collective-permute-start | bytes 147464 | tf_op jit(solution)/shard_map/ppermute | solution.py:260
  209.3 5.0 %collective-permute-start.19 = (bf16[64,384]{1,0:T(8,128)(2,1)S(1)}, bf16[64,384]{1,0:T(8,128)(2,1)S(1)}, u32[]{:S(2)}, u32[]{:S(2)}) collective-permute-start(bf16[64,384]{1,0:T(8,128)(2,1)S(1)} %add_convert_fusion.refs_0_), channel_id=1, source_target_pairs={{0,3},{1,0},{2,1},{3,2},{4,7},{5,4},{6,5},{7,6},{8,11},{9,8},{10,9... | collective-permute-start | bytes 147464 | tf_op jit(solution)/shard_map/ppermute | solution.py:260
  (2 other events, 1.4 us)

commit v5 on v4

--- a/solution.py
+++ b/solution.py
@@ -149,7 +149,7 @@
         by_example(lengths, left),
         right,
         NT,
-        precision=lax.Precision.HIGHEST,
+        precision=lax.Precision.HIGH,
         preferred_element_type=jnp.float32,
     )
 

time: 217 us -> 217 us (level)
  no operation moved by 1% of the time
where the time goes in v5:
time: 217 us; the launch traced here: 216 us
  Pallas kernels  95.2 us (44%)
  starting transfers between devices  49.4 us (23%)
  blocking collectives  32.9 us (15%)
  waiting for transfers between devices  19.1 us (9%)
  local copies, waits for them, and re-layouts  11 us (5%)
  other arithmetic  8.24 us (4%)
    pallas_call x6, Pallas kernels, project(): pl.pallas_call(functools.partial(project_kernel, bounds, parts), grid_spe...  80.9 us
    all_gather x1, blocking collectives, body(): blocks = lax.all_gather(values, 'dp', axis=0)  32.9 us
    ppermute x9, starting transfers between devices, move(): return lax.ppermute(value, AXES, pairs)  27.9 us
    ppermute x9, waiting for transfers between devices, move(): return lax.ppermute(value, AXES, pairs)  16.7 us
    pallas_call x1, Pallas kernels, local_products(): pl.pallas_call(functools.partial(local_kernel, cuts), grid=(width // tile...  11.5 us
    ppermute x2, starting transfers between devices, exchange(): return lax.ppermute(value, 'tensor', [(i, i ^ apart) for i in range(4)])  5.65 us
    select_n x3, other arithmetic, by_block(): return (jnp.where(keep, first, second), jnp.where(keep, second, first))  5.19 us
    ppermute x3, starting transfers between devices, all_tensor(): lax.ppermute(value, 'tensor', [(i, (i + k) % count) for i in range(count)])  4.47 us
  transfers between devices with their start and end apart: 20, of which 6 were waited for; matrix products, arithmetic and copies ran while one was open for 6% of the time, Pallas kernels for 43%

profile of v5, /device:TPU:0, one launch (start us, length us, event | category | flops | bytes accessed | tf_op | source)
XLA Modules:
  0.0 216.1 jit_solution(11129222094880829457)
XLA Ops:
  0.5 2.7 %fusion = (bf16[384,1024]{1,0:T(8,128)(2,1)}, bf16[384,1024]{1,0:T(8,128)(2,1)}) fusion(bf16[384,2048]{1,0:T(8,128)(2,1)} %grad.1), kind=kLoop, calls=%fused_computation.15 | loop fusion | bytes 3145728 | tf_op jit(solution)/shard_map/slice | solution.py:298
  3.1 5.5 %collective-permute-start = (bf16[384,1024]{1,0:T(8,128)(2,1)}, bf16[384,1024]{1,0:T(8,128)(2,1)S(1)}, u32[]{:S(2)}, u32[]{:S(2)}) collective-permute-start(bf16[384,1024]{1,0:T(8,128)(2,1)} %get-tuple-element.95), channel_id=1, source_target_pairs={{0,2},{1,3},{4,6},{5,7},{11,9},{10,8},{15,13},{14,12},{16,18},{17,... | collective-permute-start | bytes 2359304 | tf_op jit(solution)/shard_map/ppermute | solution.py:223
  8.7 1.5 collective-permute-start.2
  10.2 1.4 collective-permute-start.1
  11.7 2.7 %slice.33 = bf16[384,2048]{1,0:T(8,128)(2,1)} slice(bf16[384,7168]{1,0:T(8,128)(2,1)} %refs_0_.3), slice={[0:384], [0:2048]} | slice | bytes 3145728 | tf_op jit(solution)/shard_map/slice | solution.py:317
  14.4 3.5 %collective-permute-start.6 = (bf16[384,2048]{1,0:T(8,128)(2,1)}, bf16[384,2048]{1,0:T(8,128)(2,1)}, u32[]{:S(2)}, u32[]{:S(2)}) collective-permute-start(bf16[384,2048]{1,0:T(8,128)(2,1)} %slice.33), channel_id=1, source_target_pairs={{0,8},{4,12},{8,0},{12,4},{1,9},{5,13},{9,1},{13,5},{2,10},{6,14},... | collective-permute-start | bytes 4718600 | tf_op jit(solution)/shard_map/ppermute | solution.py:317
  17.9 11.5 %shard_map.109 = (f32[192,384]{1,0:T(8,128)S(1)}, bf16[384,1024]{1,0:T(8,128)(2,1)S(1)}, bf16[384,2048]{1,0:T(8,128)(2,1)}, bf16[384,2048]{1,0:T(8,128)(2,1)}) custom-call(bf16[384,7168]{1,0:T(8,128)(2,1)} %refs_0_.3, bf16[384,7168]{1,0:T(8,128)(2,1)} %up.1, bf16[384,2048]{1,0:T(8,128)(2,1)} %grad.1, bf16[384,2048]{1,0:T(8,128)(2,1)} %normed.1, ...), custom_call_target="tpu_custom_call" | custom-call | flops 1 | bytes 1 | tf_op jit(solution)/shard_map/pallas_call | solution.py:117
  30.1 2.8 %collective-permute-done.1 = bf16[384,1024]{1,0:T(8,128)(2,1)} collective-permute-done((bf16[384,1024]{1,0:T(8,128)(2,1)}, bf16[384,1024]{1,0:T(8,128)(2,1)}, u32[]{:S(2)}, u32[]{:S(2)}) %collective-permute-start.1) | collective-permute-done | bytes 786464 | tf_op jit(solution)/shard_map/ppermute | solution.py:223
  35.4 11.8 %collective-permute-start.3 = (bf16[768,1024]{1,0:T(8,128)(2,1)S(1)}, bf16[768,1024]{1,0:T(8,128)(2,1)}, u32[]{:S(2)}, u32[]{:S(2)}) collective-permute-start(bf16[768,1024]{1,0:T(8,128)(2,1)S(1)} %pad_maximum_fusion), channel_id=1, source_target_pairs={{0,1},{1,0},{2,3},{3,2},{4,5},{5,4},{6,7},{7,6},{11,10},{10,11},{9... | collective-permute-start | bytes 4718600 | tf_op jit(solution)/shard_map/ppermute | solution.py:223
  47.2 1.8 collective-permute-start.4
  49.0 3.1 %collective-permute-start.7 = (bf16[384,1024]{1,0:T(8,128)(2,1)S(1)}, bf16[384,1024]{1,0:T(8,128)(2,1)S(1)}, u32[]{:S(2)}, u32[]{:S(2)}) collective-permute-start(bf16[384,1024]{1,0:T(8,128)(2,1)S(1)} %get-tuple-element.51), channel_id=1, source_target_pairs={{0,8},{4,12},{8,0},{12,4},{1,9},{5,13},{9,1},{13,5},{2,10},{6,14},... | collective-permute-start | bytes 2359304 | tf_op jit(solution)/shard_map/ppermute | solution.py:323
  52.3 32.9 %all_gather.3.refs_2_ = bf16[4,4,32,64]{3,2,1,0:T(8,128)(2,1)S(1)} all-gather(bf16[1,4,32,64]{3,2,1,0:T(8,128)(2,1)S(1)} %all_gather_reshape.3), channel_id=1, replica_groups=mesh['parts'=2,'dp'=4,'tensor'=4] {'dp'}, dimensions={0}, use_global_device_ids=true | all-gather | bytes 81920 | tf_op jit(solution)/shard_map/all_gather | solution.py:313
  85.2 3.4 %collective-permute-start.10 = (bf16[384,2048]{1,0:T(8,128)(2,1)}, bf16[384,2048]{1,0:T(8,128)(2,1)}, u32[]{:S(2)}, u32[]{:S(2)}) collective-permute-start(bf16[384,2048]{1,0:T(8,128)(2,1)} %get-tuple-element.55), channel_id=1, source_target_pairs={{0,8},{4,12},{8,0},{12,4},{1,9},{5,13},{9,1},{13,5},{2,10},{6,14},... | collective-permute-start | bytes 4718600 | tf_op jit(solution)/shard_map/ppermute | solution.py:331
  88.6 1.8 collective-permute-start.8
  91.7 2.1 broadcast_select_fusion.6
  93.9 19.1 %shard_map.110.refs_6_ = f32[64,384]{1,0:T(8,128)S(1)} custom-call(s32[1]{0:T(128)} %bitcast.3._, bf16[384,7168]{1,0:T(8,128)(2,1)} %refs_0_.3, bf16[384,1024]{1,0:T(8,128)(2,1)S(1)} %get-tuple-element.92.refs_1_, bf16[384,1024]{1,0:T(8,128)(2,1)S(1)} %get-tuple-element.93.refs_2_, bf16[7168,2048]{1,0:T(8,128)(2,1)} %refs_3_.5, ...), custom_call_target="tpu_custom_call" | custom-call | flops 1 | bytes 1 | tf_op jit(solution)/shard_map/pallas_call | solution.py:73
  113.0 9.5 %shard_map.111.refs_6_ = f32[64,384]{1,0:T(8,128)S(1)} custom-call(s32[1]{0:T(128)} %bitcast.3._, bf16[384,2048]{1,0:T(8,128)(2,1)} %collective-permute-done.6.refs_0_, bf16[384,1024]{1,0:T(8,128)(2,1)S(1)} %collective-permute-done.7.refs_1_, bf16[384,1024]{1,0:T(8,128)(2,1)S(1)} %get-tuple-element.88.refs_2_.refs_1_, ...), custom_call_target="tpu_custom_call" | custom-call | flops 1 | bytes 1 | tf_op jit(solution)/shard_map/pallas_call | solution.py:73
  123.8 5.1 %collective-permute-done.9 = bf16[768,1024]{1,0:T(8,128)(2,1)} collective-permute-done((bf16[768,1024]{1,0:T(8,128)(2,1)}, bf16[768,1024]{1,0:T(8,128)(2,1)}, u32[]{:S(2)}, u32[]{:S(2)}) %collective-permute-start.9) | collective-permute-done | bytes 1572896 | tf_op jit(solution)/shard_map/ppermute | solution.py:223
  128.9 2.1 slice.36
  134.0 7.1 %shard_map.112.refs_8_ = f32[64,384]{1,0:T(8,128)S(1)} custom-call(s32[1]{0:T(128)} %bitcast.3._, bf16[384,2048]{1,0:T(8,128)(2,1)} %collective-permute-done.10.refs_0_.refs_2_, bf16[384,1024]{1,0:T(8,128)(2,1)S(1)} %get-tuple-element.88.refs_2_.refs_1_, bf16[384,1024]{1,0:T(8,128)(2,1)S(1)} %get-tuple-element.87.refs_3_.refs_2_, ...), custom_call_target="tpu_custom_call" | custom-call | flops 1 | bytes 1 | tf_op jit(solution)/shard_map/pallas_call | solution.py:73
  141.1 1.6 broadcast_select_fusion
  142.7 8.8 %collective-permute-done.11 = bf16[384,1024]{1,0:T(8,128)(2,1)} collective-permute-done((bf16[384,1024]{1,0:T(8,128)(2,1)}, bf16[384,1024]{1,0:T(8,128)(2,1)}, u32[]{:S(2)}, u32[]{:S(2)}) %collective-permute-start.11) | collective-permute-done | bytes 786464 | tf_op jit(solution)/shard_map/ppermute | solution.py:223
  151.5 1.8 broadcast_select_fusion.4
  153.3 1.5 collective-permute-start.12
  154.8 2.8 %collective-permute-start.14 = (f32[192,384]{1,0:T(8,128)S(1)}, f32[192,384]{1,0:T(8,128)S(1)}, u32[]{:S(2)}, u32[]{:S(2)}) collective-permute-start(f32[192,384]{1,0:T(8,128)S(1)} %copy-done.6), channel_id=1, source_target_pairs={{0,1},{1,0},{2,3},{3,2},{4,5},{5,4},{6,7},{7,6},{8,9},{9,8},{10,11... | collective-permute-start | bytes 884744 | tf_op jit(solution)/shard_map/ppermute | solution.py:304
  157.5 14.5 %shard_map.113.refs_10_ = f32[64,384]{1,0:T(8,128)S(1)} custom-call(s32[1]{0:T(128)} %bitcast.3._, bf16[384,2048]{1,0:T(8,128)(2,1)} %collective-permute-done.6.refs_0_, bf16[384,1024]{1,0:T(8,128)(2,1)S(1)} %collective-permute-done.7.refs_1_, bf16[384,2048]{1,0:T(8,128)(2,1)} %collective-permute-done.10.refs_0_.refs_2_, ...), custom_call_target="tpu_custom_call" | custom-call | flops 1 | bytes 1 | tf_op jit(solution)/shard_map/pallas_call | solution.py:73
  172.1 11.7 %shard_map.114 = f32[64,384]{1,0:T(8,128)S(1)} custom-call(s32[1]{0:T(128)} %bitcast.3._, bf16[384,2048]{1,0:T(8,128)(2,1)} %collective-permute-done.13.refs_0_, bf16[384,1024]{1,0:T(8,128)(2,1)S(1)} %get-tuple-element.88.refs_2_.refs_1_, bf16[384,1024]{1,0:T(8,128)(2,1)S(1)} %get-tuple-element.86.refs_3_.refs_2_, ...), custom_call_target="tpu_custom_call" | custom-call | flops 1 | bytes 1 | tf_op jit(solution)/shard_map/pallas_call | solution.py:73
  183.9 2.9 %collective-permute-start.15 = (f32[192,384]{1,0:T(8,128)S(1)}, f32[192,384]{1,0:T(8,128)S(1)}, u32[]{:S(2)}, u32[]{:S(2)}) collective-permute-start(f32[192,384]{1,0:T(8,128)S(1)} %add.26.refs_0_), channel_id=1, source_target_pairs={{0,2},{1,3},{2,0},{3,1},{4,6},{5,7},{6,4},{7,5},{8,10},{9,11},{10,... | collective-permute-start | bytes 884744 | tf_op jit(solution)/shard_map/ppermute | solution.py:304
  188.1 19.1 %shard_map.116 = f32[64,384]{1,0:T(8,128)S(1)} custom-call(s32[1]{0:T(128)} %bitcast.3._, bf16[384,7168]{1,0:T(8,128)(2,1)} %refs_0_.3, bf16[384,1024]{1,0:T(8,128)(2,1)S(1)} %get-tuple-element.84.refs_1_, bf16[384,1024]{1,0:T(8,128)(2,1)S(1)} %get-tuple-element.83.refs_2_, bf16[7168,2048]{1,0:T(8,128)(2,1)} %refs_3_.5, ...), custom_call_target="tpu_custom_call" | custom-call | flops 1 | bytes 1 | tf_op jit(solution)/shard_map/pallas_call | solution.py:73
  207.2 2.0 collective-permute-start.17
  209.3 2.4 %collective-permute-start.19 = (bf16[64,384]{1,0:T(8,128)(2,1)S(1)}, bf16[64,384]{1,0:T(8,128)(2,1)S(1)}, u32[]{:S(2)}, u32[]{:S(2)}) collective-permute-start(bf16[64,384]{1,0:T(8,128)(2,1)S(1)} %add_convert_fusion.refs_0_), channel_id=1, source_target_pairs={{0,3},{1,0},{2,1},{3,2},{4,7},{5,4},{6,5},{7,6},{8,11},{9,8},{10,9... | collective-permute-start | bytes 147464 | tf_op jit(solution)/shard_map/ppermute | solution.py:260
  214.3 1.8 shard_map.117
  (59 shorter events, 13.5 us)
Async XLA Ops:
  0.0 85.2 %collective-permute-start.5 = (bf16[7168,2048]{1,0:T(8,128)(2,1)}, bf16[7168,2048]{1,0:T(8,128)(2,1)}, u32[]{:S(2)}, u32[]{:S(2)}) collective-permute-start(bf16[7168,2048]{1,0:T(8,128)(2,1)} %refs_3_.5), channel_id=1, source_target_pairs={{0,4},{4,0},{8,12},{12,8},{1,5},{5,1},{9,13},{13,9},{2,6},{6,2},{1... | collective-permute-start | bytes 88080392 | tf_op jit(solution)/shard_map/ppermute | solution.py:292
  3.1 27.0 %collective-permute-start = (bf16[384,1024]{1,0:T(8,128)(2,1)}, bf16[384,1024]{1,0:T(8,128)(2,1)S(1)}, u32[]{:S(2)}, u32[]{:S(2)}) collective-permute-start(bf16[384,1024]{1,0:T(8,128)(2,1)} %get-tuple-element.95), channel_id=1, source_target_pairs={{0,2},{1,3},{4,6},{5,7},{11,9},{10,8},{15,13},{14,12},{16,18},{17,... | collective-permute-start | bytes 2359304 | tf_op jit(solution)/shard_map/ppermute | solution.py:223
  8.7 21.5 %collective-permute-start.2 = (bf16[384,1024]{1,0:T(8,128)(2,1)}, bf16[384,1024]{1,0:T(8,128)(2,1)}, u32[]{:S(2)}, u32[]{:S(2)}) collective-permute-start(bf16[384,1024]{1,0:T(8,128)(2,1)} %get-tuple-element.95), channel_id=1, source_target_pairs={{8,2},{9,3},{12,6},{13,7},{3,9},{2,8},{7,13},{6,12},{24,18},{25,19... | collective-permute-start | bytes 2359304 | tf_op jit(solution)/shard_map/ppermute | solution.py:223
  10.2 7.7 %copy-start.2 = (bf16[7168,64]{0,1:T(8,128)(2,1)S(1)}, bf16[7168,64]{0,1:T(8,128)(2,1)}, u32[]{:S(2)}) copy-start(bf16[7168,64]{0,1:T(8,128)(2,1)} %param.18) | copy-start | bytes 2752516
  10.2 7.7 %copy-start.7 = (bf16[2048,64]{0,1:T(8,128)(2,1)S(1)}, bf16[2048,64]{0,1:T(8,128)(2,1)}, u32[]{:S(2)}) copy-start(bf16[2048,64]{0,1:T(8,128)(2,1)} %param.17) | copy-start | bytes 786436
  10.2 7.7 %copy-start.8 = (bf16[2048,64]{0,1:T(8,128)(2,1)S(1)}, bf16[2048,64]{0,1:T(8,128)(2,1)}, u32[]{:S(2)}) copy-start(bf16[2048,64]{0,1:T(8,128)(2,1)} %param.16) | copy-start | bytes 786436
  10.2 22.7 %collective-permute-start.1 = (bf16[384,1024]{1,0:T(8,128)(2,1)}, bf16[384,1024]{1,0:T(8,128)(2,1)}, u32[]{:S(2)}, u32[]{:S(2)}) collective-permute-start(bf16[384,1024]{1,0:T(8,128)(2,1)} %get-tuple-element.94), channel_id=1, source_target_pairs={{8,0},{9,1},{12,4},{13,5},{3,11},{2,10},{7,15},{6,14},{24,16},{25,... | collective-permute-start | bytes 2359304 | tf_op jit(solution)/shard_map/ppermute | solution.py:223
  14.4 70.8 %collective-permute-start.6 = (bf16[384,2048]{1,0:T(8,128)(2,1)}, bf16[384,2048]{1,0:T(8,128)(2,1)}, u32[]{:S(2)}, u32[]{:S(2)}) collective-permute-start(bf16[384,2048]{1,0:T(8,128)(2,1)} %slice.33), channel_id=1, source_target_pairs={{0,8},{4,12},{8,0},{12,4},{1,9},{5,13},{9,1},{13,5},{2,10},{6,14},... | collective-permute-start | bytes 4718600 | tf_op jit(solution)/shard_map/ppermute | solution.py:317
  17.9 15.0 %copy-start.10 = (bf16[384,2048]{1,0:T(8,128)(2,1)S(1)}, bf16[384,2048]{1,0:T(8,128)(2,1)}, u32[]{:S(2)}) copy-start(bf16[384,2048]{1,0:T(8,128)(2,1)} %grad.1) | copy-start | bytes 4718596
  34.2 0.9 copy-start.11
  34.3 1.2 copy-start.12
  34.3 17.9 %copy-start.13 = (bf16[4,2048]{1,0:T(4,128)(2,1)S(1)}, bf16[4,2048]{1,0:T(4,128)(2,1)}, u32[]{:S(2)}) copy-start(bf16[4,2048]{1,0:T(4,128)(2,1)} %param.20) | copy-start | bytes 49156
  35.4 49.7 %collective-permute-start.3 = (bf16[768,1024]{1,0:T(8,128)(2,1)S(1)}, bf16[768,1024]{1,0:T(8,128)(2,1)}, u32[]{:S(2)}, u32[]{:S(2)}) collective-permute-start(bf16[768,1024]{1,0:T(8,128)(2,1)S(1)} %pad_maximum_fusion), channel_id=1, source_target_pairs={{0,1},{1,0},{2,3},{3,2},{4,5},{5,4},{6,7},{7,6},{11,10},{10,11},{9... | collective-permute-start | bytes 4718600 | tf_op jit(solution)/shard_map/ppermute | solution.py:223
  47.2 37.9 %collective-permute-start.4 = (bf16[768,1024]{1,0:T(8,128)(2,1)S(1)}, bf16[768,1024]{1,0:T(8,128)(2,1)}, u32[]{:S(2)}, u32[]{:S(2)}) collective-permute-start(bf16[768,1024]{1,0:T(8,128)(2,1)S(1)} %pad_maximum_fusion), channel_id=1, source_target_pairs={{1,2},{2,1},{5,6},{6,5},{10,9},{9,10},{14,13},{13,14},{17,18},{18,... | collective-permute-start | bytes 4718600 | tf_op jit(solution)/shard_map/ppermute | solution.py:223
  49.0 36.1 %collective-permute-start.7 = (bf16[384,1024]{1,0:T(8,128)(2,1)S(1)}, bf16[384,1024]{1,0:T(8,128)(2,1)S(1)}, u32[]{:S(2)}, u32[]{:S(2)}) collective-permute-start(bf16[384,1024]{1,0:T(8,128)(2,1)S(1)} %get-tuple-element.51), channel_id=1, source_target_pairs={{0,8},{4,12},{8,0},{12,4},{1,9},{5,13},{9,1},{13,5},{2,10},{6,14},... | collective-permute-start | bytes 2359304 | tf_op jit(solution)/shard_map/ppermute | solution.py:323
  85.2 38.6 %collective-permute-start.10 = (bf16[384,2048]{1,0:T(8,128)(2,1)}, bf16[384,2048]{1,0:T(8,128)(2,1)}, u32[]{:S(2)}, u32[]{:S(2)}) collective-permute-start(bf16[384,2048]{1,0:T(8,128)(2,1)} %get-tuple-element.55), channel_id=1, source_target_pairs={{0,8},{4,12},{8,0},{12,4},{1,9},{5,13},{9,1},{13,5},{2,10},{6,14},... | collective-permute-start | bytes 4718600 | tf_op jit(solution)/shard_map/ppermute | solution.py:331
  88.6 35.2 %collective-permute-start.8 = (bf16[768,1024]{1,0:T(8,128)(2,1)}, bf16[768,1024]{1,0:T(8,128)(2,1)}, u32[]{:S(2)}, u32[]{:S(2)}) collective-permute-start(bf16[768,1024]{1,0:T(8,128)(2,1)} %collective-permute-done.3), channel_id=1, source_target_pairs={{1,2},{2,1},{5,6},{6,5},{10,9},{9,10},{14,13},{13,14},{17,18},{18,... | collective-permute-start | bytes 4718600 | tf_op jit(solution)/shard_map/ppermute | solution.py:223
  90.4 38.6 %collective-permute-start.9 = (bf16[768,1024]{1,0:T(8,128)(2,1)}, bf16[768,1024]{1,0:T(8,128)(2,1)}, u32[]{:S(2)}, u32[]{:S(2)}) collective-permute-start(bf16[768,1024]{1,0:T(8,128)(2,1)} %collective-permute-done.4), channel_id=1, source_target_pairs={{1,0},{2,3},{5,4},{6,7},{10,11},{9,8},{14,15},{13,12},{17,16},{18,... | collective-permute-start | bytes 4718600 | tf_op jit(solution)/shard_map/ppermute | solution.py:223
  91.7 2.2 %copy-start = (bf16[7168,64]{0,1:T(8,128)(2,1)S(1)}, bf16[7168,64]{0,1:T(8,128)(2,1)}, u32[]{:S(2)}) copy-start(bf16[7168,64]{0,1:T(8,128)(2,1)} %param.19) | copy-start | bytes 2752516
  131.0 20.5 %collective-permute-start.11 = (bf16[384,1024]{1,0:T(8,128)(2,1)}, bf16[384,1024]{1,0:T(8,128)(2,1)}, u32[]{:S(2)}, u32[]{:S(2)}) collective-permute-start(bf16[384,1024]{1,0:T(8,128)(2,1)} %slice.36), channel_id=1, source_target_pairs={{1,0},{2,3},{5,4},{6,7},{10,11},{9,8},{14,15},{13,12},{17,16},{18,... | collective-permute-start | bytes 2359304 | tf_op jit(solution)/shard_map/ppermute | solution.py:223
  132.3 39.8 %collective-permute-start.13 = (bf16[384,2048]{1,0:T(8,128)(2,1)}, bf16[384,2048]{1,0:T(8,128)(2,1)}, u32[]{:S(2)}, u32[]{:S(2)}) collective-permute-start(bf16[384,2048]{1,0:T(8,128)(2,1)} %get-tuple-element.66), channel_id=1, source_target_pairs={{0,8},{4,12},{8,0},{12,4},{1,9},{5,13},{9,1},{13,5},{2,10},{6,14},... | collective-permute-start | bytes 4718600 | tf_op jit(solution)/shard_map/ppermute | solution.py:337
  133.1 0.9 copy-start.4
  142.7 12.0 %copy-start.6 = (f32[192,384]{1,0:T(8,128)S(1)}, f32[192,384]{1,0:T(8,128)}, u32[]{:S(2)}) copy-start(f32[192,384]{1,0:T(8,128)} %copy-done.5) | copy-start | bytes 884740
  153.3 30.5 %collective-permute-start.12 = (bf16[384,1024]{1,0:T(8,128)(2,1)S(1)}, bf16[384,1024]{1,0:T(8,128)(2,1)S(1)}, u32[]{:S(2)}, u32[]{:S(2)}) collective-permute-start(bf16[384,1024]{1,0:T(8,128)(2,1)S(1)} %get-tuple-element.91), channel_id=1, source_target_pairs={{1,0},{2,3},{5,4},{6,7},{10,11},{9,8},{14,15},{13,12},{17,16},{18,... | collective-permute-start | bytes 2359304 | tf_op jit(solution)/shard_map/ppermute | solution.py:223
  154.8 29.0 %collective-permute-start.14 = (f32[192,384]{1,0:T(8,128)S(1)}, f32[192,384]{1,0:T(8,128)S(1)}, u32[]{:S(2)}, u32[]{:S(2)}) collective-permute-start(f32[192,384]{1,0:T(8,128)S(1)} %copy-done.6), channel_id=1, source_target_pairs={{0,1},{1,0},{2,3},{3,2},{4,5},{5,4},{6,7},{7,6},{8,9},{9,8},{10,11... | collective-permute-start | bytes 884744 | tf_op jit(solution)/shard_map/ppermute | solution.py:304
  183.8 23.4 %collective-permute-start.16 = (f32[64,384]{1,0:T(8,128)S(1)}, f32[64,384]{1,0:T(8,128)S(1)}, u32[]{:S(2)}, u32[]{:S(2)}) collective-permute-start(f32[64,384]{1,0:T(8,128)S(1)} %shard_map.114), channel_id=1, source_target_pairs={{0,8},{4,12},{8,0},{12,4},{1,9},{5,13},{9,1},{13,5},{2,10},{6,14},... | collective-permute-start | bytes 294920 | tf_op jit(solution)/shard_map/ppermute | solution.py:351
  183.9 4.2 %copy-start.1 = (bf16[7168,64]{0,1:T(8,128)(2,1)S(1)}, bf16[7168,64]{0,1:T(8,128)(2,1)}, u32[]{:S(2)}) copy-start(bf16[7168,64]{0,1:T(8,128)(2,1)} %param.19) | copy-start | bytes 2752516
  183.9 27.8 %collective-permute-start.15 = (f32[192,384]{1,0:T(8,128)S(1)}, f32[192,384]{1,0:T(8,128)S(1)}, u32[]{:S(2)}, u32[]{:S(2)}) collective-permute-start(f32[192,384]{1,0:T(8,128)S(1)} %add.26.refs_0_), channel_id=1, source_target_pairs={{0,2},{1,3},{2,0},{3,1},{4,6},{5,7},{6,4},{7,5},{8,10},{9,11},{10,... | collective-permute-start | bytes 884744 | tf_op jit(solution)/shard_map/ppermute | solution.py:304
  188.1 23.6 %copy-start.9 = (s32[1,6]{1,0:T(1,128)S(1)}, s32[1,6]{1,0:T(1,128)}, u32[]{:S(2)}) copy-start(s32[1,6]{1,0:T(1,128)} %lengths.3) | copy-start | bytes 76
  207.2 5.9 %collective-permute-start.17 = (bf16[64,384]{1,0:T(8,128)(2,1)S(1)}, bf16[64,384]{1,0:T(8,128)(2,1)S(1)}, u32[]{:S(2)}, u32[]{:S(2)}) collective-permute-start(bf16[64,384]{1,0:T(8,128)(2,1)S(1)} %add_convert_fusion.refs_0_), channel_id=1, source_target_pairs={{0,1},{1,2},{2,3},{3,0},{4,5},{5,6},{6,7},{7,4},{8,9},{9,10},{10,1... | collective-permute-start | bytes 147464 | tf_op jit(solution)/shard_map/ppermute | solution.py:260
  209.2 5.0 %collective-permute-start.18 = (bf16[64,384]{1,0:T(8,128)(2,1)S(1)}, bf16[64,384]{1,0:T(8,128)(2,1)S(1)}, u32[]{:S(2)}, u32[]{:S(2)}) collective-permute-start(bf16[64,384]{1,0:T(8,128)(2,1)S(1)} %add_convert_fusion.refs_0_), channel_id=1, source_target_pairs={{0,2},{1,3},{2,0},{3,1},{4,6},{5,7},{6,4},{7,5},{8,10},{9,11},{10,... | collective-permute-start | bytes 147464 | tf_op jit(solution)/shard_map/ppermute | solution.py:260
  209.3 5.0 %collective-permute-start.19 = (bf16[64,384]{1,0:T(8,128)(2,1)S(1)}, bf16[64,384]{1,0:T(8,128)(2,1)S(1)}, u32[]{:S(2)}, u32[]{:S(2)}) collective-permute-start(bf16[64,384]{1,0:T(8,128)(2,1)S(1)} %add_convert_fusion.refs_0_), channel_id=1, source_target_pairs={{0,3},{1,0},{2,1},{3,2},{4,7},{5,4},{6,5},{7,6},{8,11},{9,8},{10,9... | collective-permute-start | bytes 147464 | tf_op jit(solution)/shard_map/ppermute | solution.py:260
  (2 other events, 1.4 us)
